TPU v7x, 32 devices: a whole 2x2x4 slice. The times are simulated.
32 devices in a mesh: dp: 8 (over z, x), fsdp: 4 (over y, core).
Axes of the slice: x: 2, y: 2, z: 4, core: 2. Of those that a mesh axis runs over, the one named last changes fastest.
Arguments:
- latents: int32 [512, 96, 32], P(('dp', 'fsdp')), may hold values from 0 to 31
- targets: int32 [512, 48, 32], P(('dp', 'fsdp')), may hold values from 0 to 31
- horizon: int32 [512], P(('dp', 'fsdp')), may hold values from 8 to 48, as said below
- memory_valid: int32 [512], P(('dp', 'fsdp')), may hold values 0 or 1
- embed: float32 [1024, 256], P('dp', 'fsdp'), may hold values from -1 to 1
- qkv_weight: float32 [3, 256, 768], P(None, 'fsdp', 'dp'), may hold values from -0.375 to 0.375
- out_weight: float32 [3, 256, 256], P(None, 'fsdp', 'dp'), may hold values from -2 to 2
- up_weight: float32 [3, 256, 1024], P(None, 'fsdp', 'dp'), may hold values from -0.375 to 0.375
- down_weight: float32 [3, 1024, 256], P(None, 'dp', 'fsdp'), may hold values from -0.1875 to 0.1875
- head_weight: float32 [256, 1024], P('fsdp', 'dp'), may hold values from -0.375 to 0.375
- gains: float32 [7, 256], replicated, may hold values from 0.4 to 2.2
- embed_rows: float32 [1024], P('dp'), may hold values from 9.6270915e-11 to 3.8508366e-10
- embed_cols: float32 [256], P('fsdp'), may hold values from 9.6270915e-11 to 3.8508366e-10
- qkv_rows: float32 [3, 256], P(None, 'fsdp'), may hold values from 9.6270915e-11 to 3.8508366e-10
- qkv_cols: float32 [3, 768], P(None, 'dp'), may hold values from 9.6270915e-11 to 3.8508366e-10
- out_rows: float32 [3, 256], P(None, 'fsdp'), may hold values from 9.6270915e-11 to 3.8508366e-10
- out_cols: float32 [3, 256], P(None, 'dp'), may hold values from 9.6270915e-11 to 3.8508366e-10
- up_rows: float32 [3, 256], P(None, 'fsdp'), may hold values from 9.6270915e-11 to 3.8508366e-10
- up_cols: float32 [3, 1024], P(None, 'dp'), may hold values from 9.6270915e-11 to 3.8508366e-10
- down_rows: float32 [3, 1024], P(None, 'dp'), may hold values from 9.6270915e-11 to 3.8508366e-10
- down_cols: float32 [3, 256], P(None, 'fsdp'), may hold values from 9.6270915e-11 to 3.8508366e-10
- head_rows: float32 [256], P('fsdp'), may hold values from 9.6270915e-11 to 3.8508366e-10
- head_cols: float32 [1024], P('dp'), may hold values from 9.6270915e-11 to 3.8508366e-10
- gain_second: float32 [7, 256], replicated, may hold values from 9.627091e-10 to 3.8508365e-09
Outputs:
- loss_sum: float32 [], replicated
- position_count: float32 [], replicated
- grad_norm: float32 [], replicated
- embed_new: float32 [1024, 256], P('dp', 'fsdp')
- embed_grad: float32 [1024, 256], P('dp', 'fsdp')
- embed_rows_new: float32 [1024], P('dp')
- embed_cols_new: float32 [256], P('fsdp')
- qkv_new: float32 [3, 256, 768], P(None, 'fsdp', 'dp')
- qkv_grad: float32 [3, 256, 768], P(None, 'fsdp', 'dp')
- qkv_rows_new: float32 [3, 256], P(None, 'fsdp')
- qkv_cols_new: float32 [3, 768], P(None, 'dp')
- out_new: float32 [3, 256, 256], P(None, 'fsdp', 'dp')
- out_grad: float32 [3, 256, 256], P(None, 'fsdp', 'dp')
- out_rows_new: float32 [3, 256], P(None, 'fsdp')
- out_cols_new: float32 [3, 256], P(None, 'dp')
- up_new: float32 [3, 256, 1024], P(None, 'fsdp', 'dp')
- up_grad: float32 [3, 256, 1024], P(None, 'fsdp', 'dp')
- up_rows_new: float32 [3, 256], P(None, 'fsdp')
- up_cols_new: float32 [3, 1024], P(None, 'dp')
- down_new: float32 [3, 1024, 256], P(None, 'dp', 'fsdp')
- down_grad: float32 [3, 1024, 256], P(None, 'dp', 'fsdp')
- down_rows_new: float32 [3, 1024], P(None, 'dp')
- down_cols_new: float32 [3, 256], P(None, 'fsdp')
- head_new: float32 [256, 1024], P('fsdp', 'dp')
- head_grad: float32 [256, 1024], P('fsdp', 'dp')
- head_rows_new: float32 [256], P('fsdp')
- head_cols_new: float32 [1024], P('dp')
- gains_new: float32 [7, 256], replicated
- gains_grad: float32 [7, 256], replicated
- gain_second_new: float32 [7, 256], replicated
Inputs may be any that keep to these rules, and one draw needn't show every extreme that they name: `horizon`: some sample has all 48 positions counted.
All inputs are finite; a program needn't handle non-finite values. No bound on the sum of `memory_valid` on one device may be relied on, other than what follows from the above.
Results may differ from a plain program's by a relative error of at most 0.0095.
The roundings to bfloat16 on the way count: a program that leaves them out, or rounds other values in their place, can miss the bound.
Values may be sent and summed in bfloat16 or wider, within the bound.
No kernel may reach another device: no remote copies, remote signals or barrier semaphores. Data moves between devices by JAX's collectives and lax.ppermute only.
A program may use at most 192 MiB of HBM per device.

v0:
```python
import functools

import jax
import jax.numpy as jnp
from jax import lax
from jax.experimental import pallas as pl
from jax.experimental.pallas import tpu as pltpu
from jax.sharding import PartitionSpec as P

D = 256
HEADS = 8
HEAD = D // HEADS
FF = 1024
CATS = 32
CLASSES = 32
LAYERS = 3
SEG = 48
MEM = 48
CTX = 96
VOCAB = 1024
GROUP = 4
ROWS = GROUP * CTX
HALF = D // 2
VMEM_BYTES = 24 * 1024 * 1024

decay_two = 0.9
step_rate = 0.3
clip_limit = 0.05
tiny_term = 1e-30
norm_eps = 1e-06
masked_score = -1e30
log2_e = 1.4426950408889634
score_scale = HEAD ** (-0.5)
gelu_one = 0.7978845608028654
gelu_two = 0.044715


def dot_nn(left, right):
    return lax.dot_general(
        left, right, (((1,), (0,)), ((), ())), preferred_element_type=jnp.float32
    )


def dot_nt(left, right):
    return lax.dot_general(
        left, right, (((1,), (1,)), ((), ())), preferred_element_type=jnp.float32
    )


def dot_tn(left, right):
    return lax.dot_general(
        left, right, (((0,), (0,)), ((), ())), preferred_element_type=jnp.float32
    )


def inverse_rms(values):
    return lax.rsqrt(jnp.mean(values * values, axis=-1, keepdims=True) + norm_eps)


def rms_back(values, inverse, gain_row, upstream):
    normed = values * inverse
    scaled = upstream * gain_row
    inner = jnp.mean(scaled * normed, axis=-1, keepdims=True)
    return (
        inverse * (scaled - normed * inner),
        jnp.sum(upstream * normed, axis=0, keepdims=True),
    )


def head_masks():
    lane = lax.broadcasted_iota(jnp.int32, (1, D // 2), 1) // HEAD
    return [lane == head for head in range(HEADS // 2)]


def expand_heads(rows, masks):
    return jnp.concatenate([rows * mask.astype(rows.dtype) for mask in masks], axis=0)


def collapse_heads(spread, rows, masks):
    product = dot_tn(spread, rows)
    queries = product.shape[0] // len(masks)
    taken = product[(len(masks) - 1) * queries :]
    for at, mask in enumerate(masks[:-1]):
        taken = jnp.where(mask, product[at * queries : (at + 1) * queries], taken)
    return taken


def half_of(part, side):
    start = part * D + side * HALF
    return slice(start, start + HALF)


def fill_bias(bias_ref):
    spread = bias_ref.shape[2]
    queries = spread // (HEADS // 2)
    key_at = lax.broadcasted_iota(jnp.int32, (CTX, spread), 0)
    query_at = lax.broadcasted_iota(jnp.int32, (CTX, spread), 1) % queries + (CTX - queries)
    later = key_at > query_at
    crosses = (query_at >= MEM) & (key_at < MEM)
    bias_ref[0] = jnp.where(later | crosses, masked_score, 0.0)
    bias_ref[1] = jnp.where(later, masked_score, 0.0)


def block_place(device, steps):
    place, weight = 0, 1
    for step in steps[:-1]:
        digit = 0
        for bit in step:
            digit = 2 * digit + ((device >> bit) & 1)
        place += digit * weight
        weight <<= len(step)
    return place


def place_weights(targets, own_ref, other_ref, core, widths, mesh_plan, start=0):
    outer_count, inner_count, steps = mesh_plan
    rows = own_ref.shape[1]
    for high in range(inner_count // 2):
        for source, side in ((own_ref, core), (other_ref, 1 - core)):
            here = pl.ds(pl.multiple_of((2 * high + side) * rows, rows), rows)
            at = start
            for (target, column), width in zip(targets, widths):
                block = [
                    source[
                        block_place(outer * inner_count + 2 * high, steps), :, at : at + width
                    ]
                    for outer in range(outer_count)
                ]
                target[here, column : column + width * outer_count] = jnp.concatenate(
                    block, axis=1
                )
                at += width


def write_blocks(send_ref, keep_ref, sum_ref, core, widths, mesh_plan):
    outer_count, inner_count, steps = mesh_plan
    rows = keep_ref.shape[1]
    for high in range(inner_count // 2):
        for target, side in ((keep_ref, core), (send_ref, 1 - core)):
            here = pl.ds(pl.multiple_of((2 * high + side) * rows, rows), rows)
            taken = sum_ref[here, :]
            for outer in range(outer_count):
                block, column = [], 0
                for width in widths:
                    block.append(taken[:, column + outer * width : column + (outer + 1) * width])
                    column += width * outer_count
                target[block_place(outer * inner_count + 2 * high, steps)] = jnp.concatenate(
                    block, axis=1
                ).astype(target.dtype)


def one_hot_rows(latent_ref, hot_ref, first):
    spot = lax.broadcasted_iota(jnp.int32, (CATS, VOCAB), 1) // CLASSES
    group = lax.broadcasted_iota(jnp.int32, (CATS, VOCAB), 0)
    spreader = jnp.where(spot == group, 1.0, 0.0).astype(jnp.bfloat16)
    classes = (lax.broadcasted_iota(jnp.int32, (1, VOCAB), 1) % CLASSES).astype(jnp.float32)
    for sample in range(GROUP):
        drawn = dot_tn(latent_ref[sample].astype(jnp.float32).astype(jnp.bfloat16), spreader)
        hot_ref[pl.ds(first + sample * CTX, CTX), :] = jnp.where(
            drawn == classes, 1.0, 0.0
        ).astype(jnp.bfloat16)


def tail_rows(values, queries):
    if queries == CTX:
        return values
    return jnp.concatenate(
        [
            values[(sample + 1) * CTX - queries : (sample + 1) * CTX]
            for sample in range(values.shape[0] // CTX)
        ],
        axis=0,
    )


def attend_forward(step, hidden, gain_row, weight_ref, valid_ref, bias_ref, masks, refs):
    middle_ref, qkv_ref, mix_ref, chance_ref = refs
    queries = chance_ref.shape[3] // (HEADS // 2)
    normed = (hidden * inverse_rms(hidden) * gain_row).astype(jnp.bfloat16)
    qkv_ref[...] = dot_nn(normed, weight_ref[:, 0 : 3 * D]).astype(jnp.bfloat16)
    units = [(sample, side) for sample in range(GROUP) for side in range(2)]
    scores = []
    for sample, side in units:
        rows = slice(sample * CTX, (sample + 1) * CTX)
        tail = slice((sample + 1) * CTX - queries, (sample + 1) * CTX)
        spread = expand_heads(qkv_ref[tail, half_of(0, side)], masks)
        scores.append(dot_nt(qkv_ref[rows, half_of(1, side)], spread))
    for (sample, side), score in zip(units, scores):
        score = score + bias_ref[valid_ref[step * GROUP + sample]]
        peak = jnp.max(score, axis=0, keepdims=True)
        exponent = jnp.exp2((score - peak) * (score_scale * log2_e))
        total = jnp.sum(exponent, axis=0, keepdims=True)
        chance_ref[sample, side] = (exponent * (1.0 / total)).astype(jnp.bfloat16)
    for sample, side in units:
        rows = slice(sample * CTX, (sample + 1) * CTX)
        mix_ref[sample * queries : (sample + 1) * queries, half_of(0, side)] = collapse_heads(
            chance_ref[sample, side], qkv_ref[rows, half_of(2, side)], masks
        ).astype(jnp.bfloat16)
    middle_ref[...] = tail_rows(hidden, queries) + dot_nn(
        mix_ref[...], weight_ref[:, 3 * D : 4 * D]
    )


def gelu_parts(value):
    square = value * value
    share = 0.5 + 0.5 * jnp.tanh(value * (gelu_one + (gelu_one * gelu_two) * square))
    active = value * share
    bent = active * (1.0 - share)
    return active, share + bent * (2.0 * gelu_one + (6.0 * gelu_one * gelu_two) * square)


def feed_forward(middle, gain_row, weight_ref, inner_ref, slope_ref):
    normed = (middle * inverse_rms(middle) * gain_row).astype(jnp.bfloat16)
    for part in range(FF // D):
        columns = slice(part * D, (part + 1) * D)
        inner = dot_nn(normed, weight_ref[:, columns])
        for sample in range(GROUP):
            rows = slice(sample * CTX, (sample + 1) * CTX)
            active, slope = gelu_parts(inner[rows])
            inner_ref[rows, columns] = active.astype(jnp.bfloat16)
            slope_ref[rows, columns] = slope.astype(jnp.bfloat16)
    return middle + dot_nt(inner_ref[...], weight_ref[:, FF : 2 * FF])


def feed_back(here, upstream, middle, gain_row, weight_ref, slope_ref, refs):
    normed_ref, dinner_ref, dout_ref = refs
    dout = upstream.astype(jnp.bfloat16)
    dout_ref[here(0, ROWS), :] = dout
    inverse = inverse_rms(middle)
    normed_ref[here(0, ROWS), :] = (middle * inverse * gain_row).astype(jnp.bfloat16)
    for part in range(FF // D):
        columns = slice(part * D, (part + 1) * D)
        dact = dot_nn(dout, weight_ref[:, FF + part * D : FF + (part + 1) * D])
        dinner_ref[here(0, ROWS), columns] = (
            dact * slope_ref[:, columns].astype(jnp.float32)
        ).astype(jnp.bfloat16)
    dnormed = dot_nt(dinner_ref[here(0, ROWS), :], weight_ref[:, 0:FF])
    through, gain_part = rms_back(middle, inverse, gain_row, dnormed)
    return upstream + through, gain_part


def attend_back(step, here, saved, dmiddle, gain_row, weight_ref, masks, refs):
    hidden, qkv_ref, mix_ref, chance_ref = saved
    normed_ref, dmiddle_ref, dqkv_ref, mixes_ref = refs
    queries = chance_ref.shape[3] // (HEADS // 2)
    short = here(0, GROUP * queries, queries)
    dattend = dmiddle.astype(jnp.bfloat16)
    dmiddle_ref[short, :] = dattend
    mixes_ref[short, :] = mix_ref[...]
    dmix = dot_nt(dattend, weight_ref[:, 3 * D : 4 * D]).astype(jnp.bfloat16)
    units = [(sample, side) for sample in range(GROUP) for side in range(2)]
    slopes, dchances, dscores = [], [], []
    for sample, side in units:
        rows = slice(sample * CTX, (sample + 1) * CTX)
        slopes.append(
            expand_heads(
                dmix[sample * queries : (sample + 1) * queries, half_of(0, side)], masks
            )
        )
        dchances.append(dot_nt(qkv_ref[rows, half_of(2, side)], slopes[-1]))
    for (sample, side), dchance in zip(units, dchances):
        chance = chance_ref[sample, side].astype(jnp.float32)
        weighed = chance * dchance
        dscores.append(
            (weighed - chance * jnp.sum(weighed, axis=0, keepdims=True)).astype(jnp.bfloat16)
        )
    for at, (sample, side) in enumerate(units):
        rows = slice(sample * CTX, (sample + 1) * CTX)
        tail = slice((sample + 1) * CTX - queries, (sample + 1) * CTX)
        there = here(sample * CTX, CTX)
        spread = expand_heads(qkv_ref[tail, half_of(0, side)], masks)
        keys = qkv_ref[rows, half_of(1, side)]
        dvalues = dot_nn(chance_ref[sample, side], slopes[at])
        dkeys = dot_nn(dscores[at], spread) * score_scale
        dqueries = (collapse_heads(dscores[at], keys, masks) * score_scale).astype(jnp.bfloat16)
        if queries < CTX:
            nothing = jnp.zeros((CTX - queries, HALF), jnp.bfloat16)
            dqueries = jnp.concatenate([nothing, dqueries], axis=0)
        dqkv_ref[there, half_of(0, side)] = dqueries
        dqkv_ref[there, half_of(1, side)] = dkeys.astype(jnp.bfloat16)
        dqkv_ref[there, half_of(2, side)] = dvalues.astype(jnp.bfloat16)
    inverse = inverse_rms(hidden)
    normed_ref[here(0, ROWS), :] = (hidden * inverse * gain_row).astype(jnp.bfloat16)
    dnormed = dot_nt(dqkv_ref[here(0, ROWS), :], weight_ref[:, 0 : 3 * D])
    through, gain_part = rms_back(hidden, inverse, gain_row, dnormed)
    if queries < CTX:
        nothing = jnp.zeros((CTX - queries, D), jnp.float32)
        pieces = []
        for sample in range(GROUP):
            pieces = pieces + [nothing, dmiddle[sample * queries : (sample + 1) * queries]]
        dmiddle = jnp.concatenate(pieces, axis=0)
    return dmiddle + through, gain_part


def row_spec(width, rows=ROWS):
    return pl.BlockSpec((rows, width), lambda step: (step, 0))


def chance_spec(queries):
    return pl.BlockSpec((GROUP, 2, CTX, HEADS // 2 * queries), lambda step: (step, 0, 0, 0))


def latent_spec():
    return pl.BlockSpec((GROUP, CATS, CTX), lambda step: (step, 0, 0))


def whole_spec(shape):
    return pl.BlockSpec(shape, lambda step: (0,) * len(shape))


def smem_spec():
    return pl.BlockSpec(memory_space=pltpu.SMEM)


def forward_kernel(layer, widths, mesh_plan, source_ref, own_ref, other_ref, gains_ref, valid_ref, core_ref, *refs):
    entry_ref, att_ref, before_ref = refs[0], refs[5], refs[6]
    bias_ref = refs[7] if layer == 0 else refs[9]
    step = pl.program_id(0)

    @pl.when(step == 0)
    def _():
        fill_bias(bias_ref)
        att = [(att_ref, 0), (att_ref, 3 * D)]
        before = [(before_ref, 0)] if layer == 0 else [(before_ref, 0), (before_ref, FF)]
        targets = att + before if layer == 0 else before + att
        place_weights(targets, own_ref, other_ref, core_ref[0], widths[: len(targets)], mesh_plan)

    if layer == 0:
        one_hot_rows(source_ref, refs[8], 0)
        hidden = dot_nt(refs[8][...], before_ref[...])
    else:
        gain_ffn = gains_ref[LAYERS + layer - 1 : LAYERS + layer, :]
        hidden = feed_forward(source_ref[...], gain_ffn, before_ref, refs[7], refs[8])
    entry_ref[...] = hidden
    attend_forward(
        step,
        hidden,
        gains_ref[layer : layer + 1, :],
        att_ref,
        valid_ref,
        bias_ref,
        head_masks(),
        refs[1:5],
    )


def run_forward(layer, widths, mesh_plan, source, own, other, gains, valid, core):
    tokens = valid.shape[0] * CTX
    queries = SEG if layer == LAYERS - 1 else CTX
    f32, b16 = jnp.float32, jnp.bfloat16
    shape = jax.ShapeDtypeStruct
    short = tokens // CTX * queries
    outs = [
        (shape((tokens, D), f32), row_spec(D)),
        (shape((short, D), f32), row_spec(D, GROUP * queries)),
        (shape((tokens, 3 * D), b16), row_spec(3 * D)),
        (shape((short, D), b16), row_spec(D, GROUP * queries)),
        (shape((tokens // CTX, 2, CTX, HEADS // 2 * queries), b16), chance_spec(queries)),
        (shape((D, 4 * D), b16), whole_spec((D, 4 * D))),
    ]
    scratch = [pltpu.VMEM((2, CTX, HEADS // 2 * queries), f32)]
    if layer == 0:
        scratch = [pltpu.VMEM((D, VOCAB), b16)] + scratch + [pltpu.VMEM((ROWS, VOCAB), b16)]
        source_spec = latent_spec()
    else:
        source_spec = row_spec(D)
        outs.append((shape((D, 2 * FF), b16), whole_spec((D, 2 * FF))))
        outs = outs + [(shape((tokens, FF), b16), row_spec(FF))] * 2
    return pl.pallas_call(
        functools.partial(forward_kernel, layer, widths, mesh_plan),
        grid=(tokens // ROWS,),
        in_specs=[
            source_spec,
            whole_spec(own.shape),
            whole_spec(other.shape),
            whole_spec(gains.shape),
            smem_spec(),
            smem_spec(),
        ],
        out_specs=[spec for _, spec in outs],
        out_shape=[item for item, _ in outs],
        scratch_shapes=scratch,
        compiler_params=pltpu.CompilerParams(vmem_limit_bytes=VMEM_BYTES),
        cost_estimate=pl.CostEstimate(
            flops=2 * tokens * D * 12 * D,
            bytes_accessed=tokens * D * 16 + D * 12 * D * 4,
            transcendentals=tokens * (FF + HEADS * CTX),
        ),
        name="forward_part",
    )(source, own, other, gains, valid, core)


def top_kernel(widths, gather_plan, mesh_plan, start, middle_ref, own_ref, other_ref, drawn_ref, gains_ref, horizon_ref, core_ref, *refs):
    dmiddle_ref, send_ref, keep_ref, gain_ref, loss_ref, count_ref = refs[:6]
    weight_ref, head_ref, turned_ref, final_ref, dlogits_ref = refs[6:11]
    normed_ref, inner_ref, slope_ref, dinner_ref, dout_ref, last_ref, sum_ref = refs[11:18]
    targets_ref, counted_ref = refs[18:]
    tokens = middle_ref.shape[0]
    gain_final = gains_ref[2 * LAYERS : 2 * LAYERS + 1, :]
    gain_ffn = gains_ref[2 * LAYERS - 1 : 2 * LAYERS, :]
    place_weights(
        [(weight_ref, 0), (weight_ref, FF), (head_ref, 0)],
        own_ref,
        other_ref,
        core_ref[0],
        widths,
        gather_plan,
        start,
    )
    turned_ref[...] = head_ref[...].T
    samples = tokens // SEG
    targets_ref[...] = jnp.concatenate([drawn_ref[at] for at in range(samples)], axis=1)
    position = lax.broadcasted_iota(jnp.int32, (1, SEG), 1)
    counted_ref[...] = jnp.concatenate(
        [jnp.where(position < horizon_ref[at], 1.0, 0.0) for at in range(samples)], axis=1
    )
    count_ref[...] = jnp.sum(counted_ref[...], axis=1, keepdims=True)
    for block in range(tokens // ROWS):
        rows = slice(block * ROWS, (block + 1) * ROWS)
        middle = middle_ref[rows, :]
        normed = (middle * inverse_rms(middle) * gain_ffn).astype(jnp.bfloat16)
        normed_ref[rows, :] = normed
        for part in range(FF // D):
            columns = slice(part * D, (part + 1) * D)
            inner = dot_nn(normed, weight_ref[:, columns])
            for piece in range(GROUP):
                there = slice(block * ROWS + piece * CTX, block * ROWS + (piece + 1) * CTX)
                active, slope = gelu_parts(inner[piece * CTX : (piece + 1) * CTX])
                inner_ref[there, columns] = active.astype(jnp.bfloat16)
                slope_ref[there, columns] = slope
        last = middle + dot_nt(inner_ref[rows, :], weight_ref[:, FF : 2 * FF])
        last_ref[rows, :] = last
        final_ref[rows, :] = (last * inverse_rms(last) * gain_final).astype(jnp.bfloat16)
    span = D
    loss = jnp.zeros((1, span), jnp.float32)
    spots = lax.broadcasted_iota(jnp.int32, (CLASSES, span), 0)
    for part in range(tokens // span):
        columns = slice(part * span, (part + 1) * span)
        counted = counted_ref[0:1, columns]
        final = final_ref[columns, :]
        for quarter in range(VOCAB // D):
            logits = dot_nt(turned_ref[quarter * D : (quarter + 1) * D, :], final)
            for inside in range(D // CLASSES):
                group = quarter * (D // CLASSES) + inside
                values = logits[inside * CLASSES : (inside + 1) * CLASSES]
                shifted = values - jnp.max(values, axis=0, keepdims=True)
                exponent = jnp.exp2(shifted * log2_e)
                total = jnp.sum(exponent, axis=0, keepdims=True)
                hot = spots == targets_ref[group : group + 1, columns]
                chosen = jnp.sum(jnp.where(hot, shifted, 0.0), axis=0, keepdims=True)
                loss = loss + counted * (jnp.log(total) - chosen)
                chance = exponent * (1.0 / total)
                slope = (chance - jnp.where(hot, 1.0, 0.0)) * counted
                dlogits_ref[group * CLASSES : (group + 1) * CLASSES, columns] = slope.astype(
                    jnp.bfloat16
                )
    loss_ref[...] = jnp.sum(loss, axis=1, keepdims=True)
    sum_ref[:, 2 * FF :] = dot_nt(final_ref[...].T, dlogits_ref[...])
    dfinal = dot_nn(head_ref[...], dlogits_ref[...]).T
    last = last_ref[...]
    dlast, gain_part = rms_back(last, inverse_rms(last), gain_final, dfinal)
    gain_ref[1:2, :] = gain_part
    last_ref[...] = dlast
    gain_sum = jnp.zeros((1, D), jnp.float32)
    for block in range(tokens // ROWS):
        rows = slice(block * ROWS, (block + 1) * ROWS)
        upstream = last_ref[rows, :]
        dout = upstream.astype(jnp.bfloat16)
        dout_ref[rows, :] = dout
        for part in range(FF // D):
            columns = slice(part * D, (part + 1) * D)
            dact = dot_nn(dout, weight_ref[:, FF + part * D : FF + (part + 1) * D])
            dinner_ref[rows, columns] = (dact * slope_ref[rows, columns]).astype(jnp.bfloat16)
        dnormed = dot_nt(dinner_ref[rows, :], weight_ref[:, 0:FF])
        middle = middle_ref[rows, :]
        through, gain_part = rms_back(middle, inverse_rms(middle), gain_ffn, dnormed)
        gain_sum = gain_sum + gain_part
        dmiddle_ref[rows, :] = upstream + through
    gain_ref[0:1, :] = gain_sum
    sum_ref[:, 0:FF] = dot_nn(normed_ref[...].T, dinner_ref[...])
    sum_ref[:, FF : 2 * FF] = dot_nn(dout_ref[...].T, inner_ref[...])
    write_blocks(send_ref, keep_ref, sum_ref, core_ref[0], widths, mesh_plan)


def block_outs(own, widths):
    shape = jax.ShapeDtypeStruct
    blocks = own.shape[:2] + (sum(widths),)
    return [shape(blocks, jnp.bfloat16), shape(blocks, jnp.float32)]


def run_top(widths, gather_plan, mesh_plan, start, middle, own, other, targets, gains, horizon, core):
    tokens = middle.shape[0]
    f32, b16 = jnp.float32, jnp.bfloat16
    shape = jax.ShapeDtypeStruct
    vmem = pl.BlockSpec(memory_space=pltpu.VMEM)
    return pl.pallas_call(
        functools.partial(top_kernel, widths, gather_plan, mesh_plan, start),
        in_specs=[vmem] * 5 + [smem_spec()] * 2,
        out_specs=[vmem] * 6,
        out_shape=[shape((tokens, D), f32)]
        + block_outs(own, widths)
        + [shape((2, D), f32), shape((1, 1), f32), shape((1, 1), f32)],
        scratch_shapes=[
            pltpu.VMEM((D, 2 * FF), b16),
            pltpu.VMEM((D, VOCAB), b16),
            pltpu.VMEM((VOCAB, D), b16),
            pltpu.VMEM((tokens, D), b16),
            pltpu.VMEM((VOCAB, tokens), b16),
            pltpu.VMEM((tokens, D), b16),
            pltpu.VMEM((tokens, FF), b16),
            pltpu.VMEM((tokens, FF), f32),
            pltpu.VMEM((tokens, FF), b16),
            pltpu.VMEM((tokens, D), b16),
            pltpu.VMEM((tokens, D), f32),
            pltpu.VMEM((D, 2 * FF + VOCAB), f32),
            pltpu.VMEM((CATS, tokens), jnp.int32),
            pltpu.VMEM((1, tokens), f32),
        ],
        compiler_params=pltpu.CompilerParams(vmem_limit_bytes=VMEM_BYTES),
        cost_estimate=pl.CostEstimate(
            flops=6 * tokens * D * 3 * FF,
            bytes_accessed=tokens * D * 8 + D * 3 * FF * 10,
            transcendentals=tokens * (FF + VOCAB),
        ),
        name="loss_part",
    )(middle, own, other, targets, gains, horizon, core)


def backward_kernel(layer, widths, mesh_plan, *refs):
    entry_ref, qkv_ref, mix_ref, chance_ref, dmiddle_ref, att_ref, gains_ref, core_ref = refs[:8]
    if layer == 0:
        latent_ref, send_ref, keep_ref, gain_ref = refs[8:12]
        att_kept, before_kept, sum_ref = refs[12:16], refs[16:18], refs[18]
    else:
        before_ref, ffn_ref, slope_ref, inner_hbm, out_ref, send_ref, keep_ref, gain_ref = refs[8:16]
        att_kept, before_kept, sum_ref = refs[16:20], refs[20:23], refs[23]
        inner_ref, inner_sem = refs[24:26]
        copy = pltpu.make_async_copy(inner_hbm, inner_ref, inner_sem)
    step = pl.program_id(0)

    def here(start, length, unit=CTX):
        base = step * (GROUP * unit)
        return pl.ds(pl.multiple_of(base + start, 16), length)

    @pl.when(step == 0)
    def _():
        gain_ref[...] = jnp.zeros_like(gain_ref)
        if layer > 0:
            copy.start()

    dentry, gain_part = attend_back(
        step,
        here,
        (entry_ref[...], qkv_ref, mix_ref, chance_ref),
        dmiddle_ref[...],
        gains_ref[layer : layer + 1, :],
        att_ref,
        head_masks(),
        att_kept,
    )
    gain_ref[0:1, :] += gain_part
    if layer == 0:
        before_kept[0][here(0, ROWS), :] = dentry.astype(jnp.bfloat16)
        one_hot_rows(latent_ref, before_kept[1], pl.multiple_of(step * ROWS, ROWS))
    else:
        dbefore, gain_part = feed_back(
            here,
            dentry,
            before_ref[...],
            gains_ref[LAYERS + layer - 1 : LAYERS + layer, :],
            ffn_ref,
            slope_ref,
            before_kept,
        )
        out_ref[...] = dbefore
        gain_ref[1:2, :] += gain_part

    @pl.when(step == pl.num_programs(0) - 1)
    def _():
        normed_ref, dattend_ref, dqkv_ref, mixes_ref = att_kept
        att = [(normed_ref, dqkv_ref), (mixes_ref, dattend_ref)]
        if layer == 0:
            pairs = att + [(before_kept[0], before_kept[1])]
        else:
            copy.wait()
            normed_two_ref, dinner_ref, dout_ref = before_kept
            pairs = [(normed_two_ref, dinner_ref), (dout_ref, inner_ref)] + att
        column = 0
        for left, right in pairs:
            wide = right.shape[1]
            sum_ref[:, column : column + wide] = dot_nn(left[...].T, right[...])
            column += wide
        write_blocks(send_ref, keep_ref, sum_ref, core_ref[0], widths, mesh_plan)


def run_backward(layer, widths, mesh_plan, blocks_like, saved, dmiddle, gains, core, before):
    entry, _, qkv, mix, chance, weights = saved[:6]
    tokens = entry.shape[0]
    queries = chance.shape[3] // (HEADS // 2)
    short = tokens // CTX * queries
    f32, b16 = jnp.float32, jnp.bfloat16
    shape = jax.ShapeDtypeStruct
    in_specs = [
        row_spec(D),
        row_spec(3 * D),
        row_spec(D, GROUP * queries),
        chance_spec(queries),
        row_spec(D, GROUP * queries),
        whole_spec(weights.shape),
        whole_spec(gains.shape),
        smem_spec(),
    ]
    operands = [entry, qkv, mix, chance, dmiddle, weights, gains, core]
    blocks = block_outs(blocks_like, widths)
    outs = [(item, whole_spec(item.shape)) for item in blocks]
    outs.append((shape((2, D), f32), whole_spec((2, D))))
    scratch = [
        pltpu.VMEM((tokens, D), b16),
        pltpu.VMEM((short, D), b16),
        pltpu.VMEM((tokens, 3 * D), b16),
        pltpu.VMEM((short, D), b16),
    ]
    if layer == 0:
        in_specs.append(latent_spec())
        operands.append(before)
        scratch = scratch + [pltpu.VMEM((tokens, D), b16), pltpu.VMEM((tokens, VOCAB), b16)]
        wide = 4 * D + VOCAB
    else:
        in_specs = in_specs + [row_spec(D), whole_spec(before[1].shape), row_spec(FF)]
        in_specs.append(pl.BlockSpec(memory_space=pl.ANY))
        operands = operands + list(before)
        outs.insert(0, (shape((tokens, D), f32), row_spec(D)))
        scratch = scratch + [
            pltpu.VMEM((tokens, D), b16),
            pltpu.VMEM((tokens, FF), b16),
            pltpu.VMEM((tokens, D), b16),
        ]
        wide = 4 * D + 2 * FF
    scratch.append(pltpu.VMEM((D, wide), f32))
    if layer > 0:
        scratch = scratch + [pltpu.VMEM((tokens, FF), b16), pltpu.SemaphoreType.DMA]
    return pl.pallas_call(
        functools.partial(backward_kernel, layer, widths, mesh_plan),
        grid=(tokens // ROWS,),
        in_specs=in_specs,
        out_specs=[spec for _, spec in outs],
        out_shape=[item for item, _ in outs],
        scratch_shapes=scratch,
        compiler_params=pltpu.CompilerParams(vmem_limit_bytes=VMEM_BYTES),
        cost_estimate=pl.CostEstimate(
            flops=6 * tokens * D * wide,
            bytes_accessed=tokens * D * 24 + D * wide * 6,
            transcendentals=tokens * FF,
        ),
        name="backward_part",
    )(*operands)


def pack_kernel(*refs):
    qkv_ref, out_ref, up_ref, down_ref, embed_ref, head_ref = refs[:6]
    low = lambda value: value.astype(jnp.bfloat16)
    att = [[low(qkv_ref[at]), low(out_ref[at].T)] for at in range(LAYERS)]
    ffn = [[low(up_ref[at]), low(down_ref[at])] for at in range(LAYERS)]
    pieces = [
        att[0] + [low(embed_ref[...])],
        ffn[0] + att[1],
        ffn[1] + att[2] + ffn[2] + [low(head_ref[...])],
    ]
    for target, piece in zip(refs[6:], pieces):
        target[...] = jnp.concatenate(piece, axis=1)


def run_pack(masters, chunk_widths):
    vmem = pl.BlockSpec(memory_space=pltpu.VMEM)
    rows = masters[0].shape[1]
    return pl.pallas_call(
        pack_kernel,
        in_specs=[vmem] * 6,
        out_specs=[vmem] * 3,
        out_shape=[
            jax.ShapeDtypeStruct((rows, sum(widths)), jnp.bfloat16) for widths in chunk_widths
        ],
        name="pack",
    )(*masters)


def matrix_plan(widths):
    order = [
        (2, 2), (3, 2), (5, 0), (2, 1), (3, 1), (0, 2), (1, 2),
        (2, 0), (3, 0), (0, 1), (1, 1), (0, 0), (1, 0), (4, 0),
    ]
    plan, column = {}, 0
    for which, layer in order:
        plan[(which, layer)] = (column, widths[which])
        column += widths[which]
    return plan, column


def matrix_list():
    return [(which, layer) for which in range(4) for layer in range(LAYERS)] + [(4, 0), (5, 0)]


MATRICES = 4 * LAYERS + 2
LANES = 128
INNER_ROWS = 16
COMMON_ROWS = 16
ROW_IS_INNER = [True, True, True, False, False, True]


def master_of(masters, which, layer):
    if which == 1:
        return masters[1][layer].T
    return masters[which][layer] if which < 4 else masters[which][...]


def old_row(refs, which, layer):
    return refs[which][layer : layer + 1, :] if which < 4 else refs[which][...]


LATE = [(0, 0), (1, 0), (4, 0)]
EDGE = INNER_ROWS + COMMON_ROWS


def whole_sum(value):
    return jnp.sum(jnp.sum(value, axis=1, keepdims=True), axis=0, keepdims=True)


def square_sums(raw, chosen, plan, first):
    square = raw * raw
    rows = square.shape[0]
    inner, entries = [], []
    for item in matrix_list():
        if item in chosen:
            column, width = plan[item]
            part = square[:, column - first : column - first + width]
            inner.append(jnp.sum(part, axis=1, keepdims=True))
        else:
            inner.append(jnp.zeros((rows, 1), jnp.float32))
        entries.append(jnp.sum(inner[-1], axis=0, keepdims=True))
    inner.append(jnp.zeros((rows, LANES - MATRICES), jnp.float32))
    return jnp.concatenate(inner, axis=1).T, entries, jnp.sum(square, axis=0, keepdims=True)


def store_row(target_ref, row, values):
    total = values.shape[1]
    for at, start in enumerate(range(0, total, LANES)):
        stop = min(start + LANES, total)
        target_ref[row + at : row + at + 1, 0 : stop - start] = values[:, start:stop]


def load_row(source_ref, row, total):
    return jnp.concatenate(
        [
            source_ref[row + at : row + at + 1, 0 : min(LANES, total - start)]
            for at, start in enumerate(range(0, total, LANES))
        ],
        axis=1,
    )


def late_row(widths):
    _, total = matrix_plan(widths)
    late = sum(widths[which] for which, _ in LATE)
    return EDGE + -(-(total - late) // LANES)


def packet_rows(widths):
    late = sum(widths[which] for which, _ in LATE)
    return -(-(late_row(widths) + -(-late // LANES)) // 8) * 8


def early_kernel(widths, *refs):
    raw_ref, masters, row_refs = refs[0], refs[1:7], refs[7:13]
    gains_at, loss_ref, count_ref, packet_ref = refs[13:16], refs[16], refs[17], refs[18]
    plan, _ = matrix_plan(widths)
    chosen = [item for item in matrix_list() if item not in LATE]
    inner, entries, outer = square_sums(raw_ref[...], chosen, plan, 0)
    weights, row_sums = [], []
    for which, layer in matrix_list():
        master = masters[which][layer] if which < 4 else masters[which][...]
        weights.append(whole_sum(master * master))
        row_sums.append(whole_sum(old_row(row_refs, which, layer)))
    packet_ref[...] = jnp.zeros_like(packet_ref)
    packet_ref[0:INNER_ROWS, 0 : inner.shape[1]] = inner[0:INNER_ROWS, :]
    top, two, one = [ref[...] for ref in gains_at]
    gain = jnp.concatenate(
        [jnp.zeros((1, D), jnp.float32), one[0:1], two[0:1], one[1:2], two[1:2], top], axis=0
    )
    scalars = [loss_ref[...], count_ref[...]] + weights + entries + row_sums
    scalars.append(jnp.zeros((1, LANES - len(scalars)), jnp.float32))
    at = INNER_ROWS
    packet_ref[at : at + 7, :] = gain[:, 0:LANES]
    packet_ref[at + 7 : at + 8, :] = jnp.concatenate(scalars, axis=1)
    packet_ref[at + 8 : at + 15, :] = gain[:, LANES:]
    store_row(packet_ref, EDGE, outer)


def late_kernel(widths, early_ref, raw_ref, gain_ref, packet_ref):
    plan, total = matrix_plan(widths)
    inner, entries, outer = square_sums(raw_ref[...], LATE, plan, total - raw_ref.shape[1])
    packet_ref[...] = early_ref[...]
    packet_ref[0:INNER_ROWS, 0 : inner.shape[1]] += inner[0:INNER_ROWS, :]
    at = INNER_ROWS
    packet_ref[at : at + 1, :] = gain_ref[0:1, 0:LANES]
    packet_ref[at + 8 : at + 9, :] = gain_ref[0:1, LANES:]
    before = jnp.zeros((1, 2 + MATRICES), jnp.float32)
    behind = jnp.zeros((1, LANES - 2 - 2 * MATRICES), jnp.float32)
    packet_ref[at + 7 : at + 8, :] += jnp.concatenate([before] + entries + [behind], axis=1)
    store_row(packet_ref, late_row(widths), outer)


def run_early(widths, raw, masters, rows, gain_parts, loss, count):
    vmem = pl.BlockSpec(memory_space=pltpu.VMEM)
    operands = [raw] + masters + rows + gain_parts + [loss, count]
    return pl.pallas_call(
        functools.partial(early_kernel, widths),
        in_specs=[vmem] * len(operands),
        out_specs=vmem,
        out_shape=jax.ShapeDtypeStruct((packet_rows(widths), LANES), jnp.float32),
        name="early_statistics",
    )(*operands)


def run_late(widths, packet, raw, gain_part):
    vmem = pl.BlockSpec(memory_space=pltpu.VMEM)
    return pl.pallas_call(
        functools.partial(late_kernel, widths),
        in_specs=[vmem] * 3,
        out_specs=vmem,
        out_shape=jax.ShapeDtypeStruct(packet.shape, jnp.float32),
        name="late_statistics",
    )(packet, raw, gain_part)


def update_kernel(widths, sizes, *refs):
    packet_ref, raw_early, raw_late = refs[:3]
    masters, inner_refs, outer_refs = refs[3:9], refs[9:15], refs[15:21]
    gains_ref, second_ref = refs[21:23]
    outs = refs[23:]
    outer_count, inner_count = sizes
    plan, total = matrix_plan(widths)
    rows = raw_early.shape[0]
    at = INNER_ROWS
    scalars = packet_ref[at + 7 : at + 8, :]
    pick = lambda at: scalars[:, at : at + 1]
    gain_sum = jnp.concatenate(
        [packet_ref[at : at + 7, :], packet_ref[at + 8 : at + 15, :]], axis=1
    )
    gain_square = jnp.sum(jnp.sum(gain_sum * gain_sum, axis=1, keepdims=True), axis=0, keepdims=True)
    square_total = gain_square
    for at in range(MATRICES):
        square_total = square_total + pick(2 + MATRICES + at)
    count_total = pick(1)
    norm_value = jnp.sqrt(square_total) / count_total
    scaling = jnp.minimum(1.0, clip_limit / norm_value) / count_total
    square_scale = scaling * scaling
    early = raw_early.shape[1]
    outer_early = load_row(packet_ref, EDGE, early)
    outer_late = load_row(packet_ref, late_row(widths), total - early)
    inner_new = []
    for at, (which, layer) in enumerate(matrix_list()):
        outer_length = widths[which] * outer_count
        inner_new.append(
            decay_two * old_row(inner_refs, which, layer)
            + (1 - decay_two)
            * (square_scale * packet_ref[at : at + 1, 0:rows] / outer_length + tiny_term)
        )
    stacked = jnp.concatenate(inner_new, axis=0)
    stacked = jnp.concatenate([stacked, jnp.ones((LANES - MATRICES, rows), jnp.float32)], axis=0)
    if rows < LANES:
        stacked = jnp.concatenate([stacked, jnp.ones((LANES, LANES - rows), jnp.float32)], axis=1)
    turned = lax.rsqrt(stacked).T
    outs[0][...] = pick(0)
    outs[1][...] = count_total
    outs[2][...] = norm_value
    first_out = {4: 3, 0: 7, 1: 11, 2: 15, 3: 19, 5: 23}
    for at, (which, layer) in enumerate(matrix_list()):
        column, width = plan[(which, layer)]
        outer_length, inner_length = width * outer_count, rows * inner_count
        row_length = inner_length if ROW_IS_INNER[which] else outer_length
        copies = outer_count if ROW_IS_INNER[which] else inner_count
        entries = outer_length * inner_length
        if column < early:
            raw = raw_early[:, column : column + width]
            outer_total = outer_early[:, column : column + width]
        else:
            raw = raw_late[:, column - early : column - early + width]
            outer_total = outer_late[:, column - early : column - early + width]
        outer_new = decay_two * old_row(outer_refs, which, layer) + (1 - decay_two) * (
            square_scale * outer_total / inner_length + tiny_term
        )
        mean_rows = decay_two * (pick(2 + 2 * MATRICES + at) / (copies * row_length)) + (
            1 - decay_two
        ) * (square_scale * pick(2 + MATRICES + at) / entries + tiny_term)
        factor = step_rate * jnp.sqrt(pick(2 + at) / entries) * jnp.sqrt(mean_rows)
        grad = raw * scaling
        updated = master_of(masters, which, layer) - grad * (
            turned[0:rows, at : at + 1] * (factor * lax.rsqrt(outer_new))
        )
        first = first_out[which]
        row_new, column_new = (
            (inner_new[at], outer_new) if ROW_IS_INNER[which] else (outer_new, inner_new[at])
        )
        if which < 4:
            if which == 1:
                updated, grad = updated.T, grad.T
            outs[first][layer] = updated
            outs[first + 1][layer] = grad
            outs[first + 2][layer : layer + 1, :] = row_new
            outs[first + 3][layer : layer + 1, :] = column_new
        else:
            outs[first][...] = updated
            outs[first + 1][...] = grad
            outs[first + 2][...] = row_new
            outs[first + 3][...] = column_new
    gain_grad = gain_sum * scaling
    second_new = decay_two * second_ref[...] + (1 - decay_two) * (gain_grad * gain_grad + tiny_term)
    gains = gains_ref[...]
    spread = jnp.sqrt(jnp.mean(gains * gains, axis=-1, keepdims=True))
    outs[27][...] = gains - step_rate * spread * gain_grad * lax.rsqrt(second_new)
    outs[28][...] = gain_grad
    outs[29][...] = second_new


def run_update(widths, sizes, packet, raw_early, raw_late, masters, inner, outer, gains, second):
    vmem = pl.BlockSpec(memory_space=pltpu.VMEM)
    operands = [packet, raw_early, raw_late] + masters + inner + outer + [gains, second]
    shapes = [(1, 1)] * 3
    for which in [4, 0, 1, 2, 3, 5]:
        shapes = shapes + [masters[which].shape] * 2
        pair = [inner[which].shape, outer[which].shape]
        shapes = shapes + (pair if ROW_IS_INNER[which] else pair[::-1])
    shapes = shapes + [gains.shape] * 3
    return pl.pallas_call(
        functools.partial(update_kernel, widths, sizes),
        in_specs=[vmem] * len(operands),
        out_specs=[vmem] * len(shapes),
        out_shape=[jax.ShapeDtypeStruct(item, jnp.float32) for item in shapes],
        name="update",
    )(*operands)


def swap(value, mask):
    count = lax.axis_size("dp") * lax.axis_size("fsdp")
    return lax.ppermute(value, ("dp", "fsdp"), [(place, place ^ mask) for place in range(count)])


def device_index():
    return lax.axis_index("dp") * lax.axis_size("fsdp") + lax.axis_index("fsdp")


def step_masks(step):
    masks = []
    for digit in range(1, 1 << len(step)):
        masks.append(sum(1 << bit for at, bit in enumerate(step[::-1]) if (digit >> at) & 1))
    return masks


def tie(*values):
    return lax.optimization_barrier(values)


def behind(value, *ahead):
    return lax.optimization_barrier((value,) + ahead)[0]


class Gather:
    def __init__(self, piece, steps):
        self.held, self.steps, self.at = piece[None], steps, 0

    def send(self):
        self.others = tuple(swap(self.held, mask) for mask in step_masks(self.steps[self.at]))

    def join(self):
        step = self.steps[self.at]
        pieces = [self.held] + list(self.others)
        for at, bit in enumerate(step[::-1]):
            upper = (device_index() >> bit) & 1 == 1
            pieces = [
                jnp.where(upper, pieces[place ^ (1 << at)], pieces[place])
                for place in range(len(pieces))
            ]
        self.held = jnp.concatenate(pieces)
        self.at += 1


class Scatter:
    def __init__(self, sent, kept, steps):
        self.sent, self.kept, self.steps, self.at = (sent,), kept, steps, 0

    def send(self):
        masks = step_masks(self.steps[self.at])
        self.others = tuple(swap(sent, mask) for sent, mask in zip(self.sent, masks))

    def join(self):
        self.at += 1
        summed = self.kept
        for other in self.others:
            summed = summed + other.astype(jnp.float32)
        if self.at == len(self.steps):
            self.kept = summed
            return
        step = self.steps[self.at]
        count = 1 << len(step)
        own = 0
        for bit in step:
            own = 2 * own + ((device_index() >> bit) & 1)
        parts = summed.reshape((count, summed.shape[0] // count) + summed.shape[1:])
        if count == 2:
            self.sent = (jnp.where(own == 1, parts[0], parts[1]).astype(jnp.bfloat16),)
            self.kept = jnp.where(own == 1, parts[1], parts[0])
            return
        pick = lambda digit: lax.dynamic_index_in_dim(parts, own ^ digit, 0, keepdims=False)
        self.sent = tuple(pick(digit).astype(jnp.bfloat16) for digit in range(1, count))
        self.kept = pick(0)


def sum_packets(packet, group, inner_bits):
    masks = step_masks(group)
    others = [swap(packet, mask) for mask in masks]
    inner, outer = packet[:INNER_ROWS], packet[EDGE:]
    common = [packet[INNER_ROWS:EDGE]]
    inner, outer = [inner], [outer]
    for mask, other in zip(masks, others):
        common.append(other[INNER_ROWS:EDGE])
        if mask >> inner_bits << inner_bits == mask:
            inner.append(other[:INNER_ROWS])
        if mask >> inner_bits == 0:
            outer.append(other[EDGE:])
    tree = lambda items: (
        items[0] if len(items) == 1 else tree(
            [items[at] + items[at + 1] for at in range(0, len(items), 2)]
        )
    )
    return jnp.concatenate([tree(inner), tree(common), tree(outer)])


def merged(parts):
    whole = Scatter(None, jnp.concatenate([part.kept for part in parts], axis=2), parts[0].steps)
    whole.sent = tuple(
        jnp.concatenate(pieces, axis=2) for pieces in zip(*[part.sent for part in parts])
    )
    whole.at = parts[0].at
    return whole


def shards(
    latents,
    targets,
    horizon,
    memory_valid,
    embed,
    qkv_weight,
    out_weight,
    up_weight,
    down_weight,
    head_weight,
    gains,
    embed_rows,
    embed_cols,
    qkv_rows,
    qkv_cols,
    out_rows,
    out_cols,
    up_rows,
    up_cols,
    down_rows,
    down_cols,
    head_rows,
    head_cols,
    gain_second,
):
    samples = latents.shape[0]
    sizes = (lax.axis_size("dp"), lax.axis_size("fsdp"))
    highest = (sizes[0] * sizes[1]).bit_length() - 1
    gather_steps = [(bit,) for bit in reversed(range(3, highest))] + [(2, 1), (0,)]
    third_steps = [(4, 3)] + [(bit,) for bit in range(5, highest)] + [(2, 1), (0,)]
    scatter_steps = gather_steps[::-1]
    mesh_plan = (sizes[0], sizes[1], gather_steps)
    third_plan = (sizes[0], sizes[1], third_steps)
    core = (lax.axis_index("fsdp") & 1).astype(jnp.int32).reshape(1)

    out_turned = jnp.swapaxes(out_weight, 1, 2)
    down_turned = jnp.swapaxes(down_weight, 1, 2)
    masters = [qkv_weight, out_turned, up_weight, down_turned, embed.T, head_weight]
    widths = [qkv_weight.shape[2], out_weight.shape[2], up_weight.shape[2], down_weight.shape[1]]
    widths = widths + [embed.shape[0], head_weight.shape[1]]
    att_widths, ffn_widths = widths[0:2], widths[2:4]
    chunk_widths = [
        att_widths + widths[4:5],
        ffn_widths + att_widths,
        ffn_widths + att_widths + ffn_widths + widths[5:6],
    ]
    first, second, third = [
        Gather(piece, steps)
        for piece, steps in zip(
            run_pack(masters, chunk_widths), [gather_steps, gather_steps, third_steps]
        )
    ]
    latent_rows = latents.transpose(0, 2, 1)
    target_rows = targets.transpose(0, 2, 1)
    shared = (gains, memory_valid, core)
    back_shared = (gains, core)

    count = len(gather_steps)
    while first.at < count - 1:
        first.send()
        second.send()
        first.join()
        second.join()
    while third.at < len(third_steps) - 2:
        third.send()
        third.join()
    third.send()
    first.send()
    (other,) = first.others
    held, other, second.held = tie(first.held, other, second.held)
    second.send()
    kept = [run_forward(0, chunk_widths[0], mesh_plan, latent_rows, held, other, *shared)]
    middle, (other,), third.others = tie(kept[0][1], second.others, third.others)
    third.join()
    middle, third.held = tie(middle, third.held)
    third.send()
    kept.append(
        run_forward(1, chunk_widths[1], mesh_plan, middle, second.held, other, *shared)
    )
    middle, (other,) = tie(kept[1][1], third.others)
    kept.append(run_forward(2, chunk_widths[2], third_plan, middle, third.held, other, *shared))

    dmiddle, sent, held, gain_top, loss, counted = run_top(
        ffn_widths + widths[5:6],
        third_plan,
        mesh_plan,
        sum(ffn_widths + att_widths),
        kept[2][1],
        third.held,
        other,
        target_rows,
        gains,
        horizon,
        core,
    )
    top = Scatter(sent, held, scatter_steps)
    top.send()
    like = first.held
    before = [(kept[at][1], kept[at + 1][6], kept[at + 1][8], kept[at + 1][7]) for at in range(2)]
    dmiddle, sent, held, gain_two = run_backward(
        2, chunk_widths[1], mesh_plan, like, kept[2], dmiddle, *back_shared, before[1]
    )
    dmiddle, sent, held, top.others = tie(dmiddle, sent, held, top.others)
    two = Scatter(sent, held, scatter_steps)
    two.send()
    top.join()
    two.join()
    pair = merged([top, two])
    dmiddle, pair.sent = tie(dmiddle, pair.sent)
    pair.send()
    dmiddle, sent, held, gain_one = run_backward(
        1, chunk_widths[1], mesh_plan, like, kept[1], dmiddle, *back_shared, before[0]
    )
    dmiddle, sent, held, pair.others = tie(dmiddle, sent, held, pair.others)
    one = Scatter(sent, held, scatter_steps)
    one.send()
    pair.join()
    one.join()
    dmiddle, pair.sent, one.sent = tie(dmiddle, pair.sent, one.sent)
    one.send()
    pair.send()
    sent, held, gain_zero = run_backward(
        0, chunk_widths[0], mesh_plan, like, kept[0], dmiddle, *back_shared, latent_rows
    )
    sent, held, pair.others, one.others = tie(sent, held, pair.others, one.others)
    zero = Scatter(sent, held, scatter_steps)
    zero.send()
    one.join()
    one.send()
    pair.join()
    zero.join()
    one.others = behind(one.others, zero.sent)
    zero.send()
    one.join()
    early = merged([pair, one])
    while early.at < count:
        early.send()
        zero.others = behind(zero.others, early.sent)
        early.join()
    raw_early = early.kept[0]

    flat = lambda item: item if item.ndim == 2 else item.reshape(1, -1)
    inner = [flat(item) for item in (qkv_rows, out_rows, up_rows, down_cols, embed_cols, head_rows)]
    outer = [flat(item) for item in (qkv_cols, out_cols, up_cols, down_rows, embed_rows, head_cols)]
    row_stats = [inner[at] if ROW_IS_INNER[at] else outer[at] for at in range(6)]
    packet = run_early(
        widths, raw_early, masters, row_stats, [gain_top, gain_two, gain_one], loss, counted
    )
    while zero.at < count:
        zero.join()
        if zero.at < count:
            zero.send()
    raw_late = zero.kept[0]
    packet = run_late(widths, packet, raw_late, gain_zero)
    inner_bits = sizes[1].bit_length() - 1
    rest = list(range(3, highest))
    groups = [(0,), (2, 1)] + [tuple(rest[at : at + 2][::-1]) for at in range(0, len(rest), 2)]
    for group in groups:
        packet = sum_packets(packet, group, inner_bits)
    results = run_update(
        widths, sizes, packet, raw_early, raw_late, masters, inner, outer, gains, gain_second
    )
    results = list(results)
    for at in range(3):
        results[at] = results[at].reshape(())
    for at in (3, 4, 11, 12, 19, 20):
        results[at] = jnp.swapaxes(results[at], -1, -2)
    for at in (5, 6, 25, 26):
        results[at] = results[at].reshape(-1)
    return tuple(results)


def solution(mesh):
    return jax.shard_map(
        shards,
        mesh=mesh,
        in_specs=(
            P(("dp", "fsdp"), None, None),
            P(("dp", "fsdp"), None, None),
            P(("dp", "fsdp")),
            P(("dp", "fsdp")),
            P("dp", "fsdp"),
            P(None, "fsdp", "dp"),
            P(None, "fsdp", "dp"),
            P(None, "fsdp", "dp"),
            P(None, "dp", "fsdp"),
            P("fsdp", "dp"),
            P(),
            P("dp"),
            P("fsdp"),
            P(None, "fsdp"),
            P(None, "dp"),
            P(None, "fsdp"),
            P(None, "dp"),
            P(None, "fsdp"),
            P(None, "dp"),
            P(None, "dp"),
            P(None, "fsdp"),
            P("fsdp"),
            P("dp"),
            P(),
        ),
        out_specs=(
            P(),
            P(),
            P(),
            P("dp", "fsdp"),
            P("dp", "fsdp"),
            P("dp"),
            P("fsdp"),
            P(None, "fsdp", "dp"),
            P(None, "fsdp", "dp"),
            P(None, "fsdp"),
            P(None, "dp"),
            P(None, "fsdp", "dp"),
            P(None, "fsdp", "dp"),
            P(None, "fsdp"),
            P(None, "dp"),
            P(None, "fsdp", "dp"),
            P(None, "fsdp", "dp"),
            P(None, "fsdp"),
            P(None, "dp"),
            P(None, "dp", "fsdp"),
            P(None, "dp", "fsdp"),
            P(None, "dp"),
            P(None, "fsdp"),
            P("fsdp", "dp"),
            P("fsdp", "dp"),
            P("fsdp"),
            P("dp"),
            P(),
            P(),
            P(),
        ),
        check_vma=False,
    )
```

profile of v0, /device:TPU:0, one launch (start us, length us, event | category | flops | bytes accessed | tf_op | source)
XLA Modules:
  0.0 214.1 jit_solution(14489901538224607266)
XLA Ops:
  0.7 1.8 pack.1
  2.5 4.0 %collective-permute-start = (bf16[1,64,256]{2,1,0:T(8,128)(2,1)}, bf16[1,64,256]{2,1,0:T(8,128)(2,1)S(1)}, u32[]{:S(2)}, u32[]{:S(2)}) collective-permute-start(bf16[1,64,256]{2,1,0:T(8,128)(2,1)} %bitcast.106), channel_id=1, source_target_pairs={{0,16},{1,17},{2,18},{3,19},{4,20},{5,21},{6,22},{7,23},{8,24},{9,... | collective-permute-start | bytes 98312 | tf_op jit(solution)/shard_map/ppermute | solution.py:945
  6.6 2.4 %collective-permute-done = bf16[1,64,256]{2,1,0:T(8,128)(2,1)S(1)} collective-permute-done((bf16[1,64,256]{2,1,0:T(8,128)(2,1)}, bf16[1,64,256]{2,1,0:T(8,128)(2,1)S(1)}, u32[]{:S(2)}, u32[]{:S(2)}) %collective-permute-start) | collective-permute-done | bytes 32800 | tf_op jit(solution)/shard_map/ppermute | solution.py:945
  9.8 1.9 collective-permute-start.1
  12.8 1.4 collective-permute-start.7
  14.5 2.8 %collective-permute-start.2 = (bf16[4,64,256]{2,1,0:T(8,128)(2,1)S(1)}, bf16[4,64,256]{2,1,0:T(8,128)(2,1)S(1)}, u32[]{:S(2)}, u32[]{:S(2)}) collective-permute-start(bf16[4,64,256]{2,1,0:T(8,128)(2,1)S(1)} %pad_maximum_fusion.9), channel_id=1, source_target_pairs={{0,6},{1,7},{2,4},{3,5},{4,2},{5,3},{6,0},{7,1},{8,14},{9,15},{10,... | collective-permute-start | bytes 393224 | tf_op jit(solution)/shard_map/ppermute | solution.py:945
  18.1 1.9 collective-permute-start.10
  20.1 1.4 collective-permute-start.8
  21.5 1.7 collective-permute-start.9
  23.2 1.9 collective-permute-done.3
  25.0 1.9 collective-permute-done.4
  27.1 5.0 %collective-permute-start.12 = (bf16[1,64,768]{2,1,0:T(8,128)(2,1)S(1)}, bf16[1,64,768]{2,1,0:T(8,128)(2,1)S(1)}, u32[]{:S(2)}, u32[]{:S(2)}) collective-permute-start(bf16[1,64,768]{2,1,0:T(8,128)(2,1)S(1)} %bitcast.102), channel_id=1, source_target_pairs={{0,24},{1,25},{2,26},{3,27},{4,28},{5,29},{6,30},{7,31},{8,16},{9,... | collective-permute-start | bytes 294920 | tf_op jit(solution)/shard_map/ppermute | solution.py:945
  32.1 1.7 collective-permute-start.13
  33.9 1.7 collective-permute-start.14
  36.0 4.7 %collective-permute-done.13 = bf16[1,64,768]{2,1,0:T(8,128)(2,1)S(1)} collective-permute-done((bf16[1,64,768]{2,1,0:T(8,128)(2,1)S(1)}, bf16[1,64,768]{2,1,0:T(8,128)(2,1)S(1)}, u32[]{:S(2)}, u32[]{:S(2)}) %collective-permute-start.13) | collective-permute-done | bytes 98336 | tf_op jit(solution)/shard_map/ppermute | solution.py:945
  42.8 1.5 collective-permute-start.16
  45.0 9.1 %forward_part.3 = (f32[1536,256]{1,0:T(8,128)S(1)}, f32[1536,256]{1,0:T(8,128)S(1)}, bf16[1536,768]{1,0:T(8,128)(2,1)S(1)}, bf16[1536,256]{1,0:T(8,128)(2,1)S(1)...) custom-call(s32[16,32,96]{2,1,0:T(8,128)S(1)} %bitcast.83, ...), custom_call_target="tpu_custom_call" | custom-call | flops 2415919104 | bytes 9437184 | tf_op jit(solution)/shard_map/forward_part/pallas_call | solution.py:369
  54.1 1.5 copy-done.25
  58.5 3.9 %collective-permute-done.17 = bf16[4,64,768]{2,1,0:T(8,128)(2,1)} collective-permute-done((bf16[4,64,768]{2,1,0:T(8,128)(2,1)}, bf16[4,64,768]{2,1,0:T(8,128)(2,1)}, u32[]{:S(2)}, u32[]{:S(2)}) %collective-permute-start.17) | collective-permute-done | bytes 393248 | tf_op jit(solution)/shard_map/ppermute | solution.py:945
  62.3 1.7 broadcast_select_fusion.7
  66.4 11.6 %forward_part.4 = (f32[1536,256]{1,0:T(8,128)S(1)}, f32[1536,256]{1,0:T(8,128)S(1)}, bf16[1536,768]{1,0:T(8,128)(2,1)S(1)}, bf16[1536,256]{1,0:T(8,128)(2,1)S(1)...) custom-call(f32[1536,256]{1,0:T(8,128)S(1)} %get-tuple-element.156.s, ...), custom_call_target="tpu_custom_call" | custom-call | flops 2415919104 | bytes 9437184 | tf_op jit(solution)/shard_map/forward_part/pallas_call | solution.py:369
  83.5 11.1 %forward_part.5 = (f32[1536,256]{1,0:T(8,128)S(1)}, f32[768,256]{1,0:T(8,128)S(1)}, bf16[1536,768]{1,0:T(8,128)(2,1)S(1)}, bf16[768,256]{1,0:T(8,128)(2,1)S(1)},...) custom-call(f32[1536,256]{1,0:T(8,128)S(1)} %get-tuple-element.160.s, ...), custom_call_target="tpu_custom_call" | custom-call | flops 2415919104 | bytes 9437184 | tf_op jit(solution)/shard_map/forward_part/pallas_call | solution.py:369
  94.6 8.5 %loss_part.1 = (f32[768,256]{1,0:T(8,128)S(1)}, bf16[16,64,384]{2,1,0:T(8,128)(2,1)S(1)}, f32[16,64,384]{2,1,0:T(8,128)S(1)}, f32[2,256]{1,0:T(2,128)S(1)}, f32[1,1]{1,0:T(1,128)}, /*index=5*/f32[1,1]{1,0:T(1,128)}) custom-call(f32[768,256]{1,0:T(8,128)S(1)} %get-tuple-element.162.middle_ref, bf16[16,64,768]{2,1,0:T(8,128)(2,1)S(1)} %pad_maximum_fusion.own_ref, ...), custom_call_target="tpu_custom_call" | custom-call | flops 3623878656 | bytes 9437184 | tf_op jit(solution)/shard_map/loss_part/pallas_call | solution.py:496
  103.1 12.5 %backward_part.3 = (f32[1536,256]{1,0:T(8,128)S(1)}, bf16[16,64,384]{2,1,0:T(8,128)(2,1)}, f32[16,64,384]{2,1,0:T(8,128)S(1)}, f32[2,256]{1,0:T(2,128)S(1)}) custom-call(f32[1536,256]{1,0:T(8,128)S(1)} %get-tuple-element.164.refs_0_, bf16[1536,768]{1,0:T(8,128)(2,1)S(1)} %get-tuple-element.165.refs_1_, bf16[768,256]{1,0:T(8,128)(2,1)S(1)} %get-tuple-element.166.refs_2_, ...), custom_call_target="tpu_custom_call" | custom-call | flops 7247757312 | bytes 14155776 | tf_op jit(solution)/shard_map/backward_part/pallas_call | solution.py:642
  118.7 1.5 convert_add_fusion.2
  121.0 1.5 convert_add_fusion.1
  124.7 1.5 collective-permute-start.22
  131.1 1.4 copy-done.36
  133.6 13.2 %backward_part.4 = (f32[1536,256]{1,0:T(8,128)S(1)}, bf16[16,64,384]{2,1,0:T(8,128)(2,1)S(1)}, f32[16,64,384]{2,1,0:T(8,128)S(1)}, f32[2,256]{1,0:T(2,128)S(1)}) custom-call(f32[1536,256]{1,0:T(8,128)S(1)} %copy-done.22, bf16[1536,768]{1,0:T(8,128)(2,1)S(1)} %copy-done.16, bf16[1536,256]{1,0:T(8,128)(2,1)S(1)} %copy-done.32, ...), custom_call_target="tpu_custom_call" | custom-call | flops 7247757312 | bytes 14155776 | tf_op jit(solution)/shard_map/backward_part/pallas_call | solution.py:642
  153.6 1.5 collective-permute-start.27
  155.0 1.7 collective-permute-start.28
  156.8 10.0 %backward_part.5 = (bf16[16,64,256]{2,1,0:T(8,128)(2,1)S(1)}, f32[16,64,256]{2,1,0:T(8,128)S(1)}, f32[2,256]{1,0:T(2,128)S(1)}) custom-call(f32[1536,256]{1,0:T(8,128)S(1)} %copy-done.30, bf16[1536,768]{1,0:T(8,128)(2,1)S(1)} %copy-done.24, bf16[1536,256]{1,0:T(8,128)(2,1)S(1)} %copy-done.40, bf16[16,2,96,384]{3,2,1,0:T(8,128)(2,1)S(1)} %copy-done.26, ...), custom_call_target="tpu_custom_call" | custom-call | flops 4831838208 | bytes 12582912 | tf_op jit(solution)/shard_map/backward_part/pallas_call | solution.py:642
  167.2 1.4 collective-permute-start.29
  169.8 1.5 collective-permute-start.33
  172.7 2.4 %collective-permute-start.31 = (bf16[1,64,1152]{2,1,0:T(8,128)(2,1)S(1)}, bf16[1,64,1152]{2,1,0:T(8,128)(2,1)S(1)}, u32[]{:S(2)}, u32[]{:S(2)}) collective-permute-start(bf16[1,64,1152]{2,1,0:T(8,128)(2,1)S(1)} %pad_maximum_fusion.8), channel_id=1, source_target_pairs={{0,16},{1,17},{2,18},{3,19},{4,20},{5,21},{6,22},{7,23},{8,24},{9,... | collective-permute-start | bytes 442376 | tf_op jit(solution)/shard_map/ppermute | solution.py:945
  175.9 2.8 %collective-permute-done.34 = bf16[4,64,256]{2,1,0:T(8,128)(2,1)S(1)} collective-permute-done((bf16[4,64,256]{2,1,0:T(8,128)(2,1)S(1)}, bf16[4,64,256]{2,1,0:T(8,128)(2,1)S(1)}, u32[]{:S(2)}, u32[]{:S(2)}) %collective-permute-start.34) | collective-permute-done | bytes 131104 | tf_op jit(solution)/shard_map/ppermute | solution.py:945
  178.8 1.4 collective-permute-start.35
  180.2 3.2 %collective-permute-done.35 = bf16[2,64,256]{2,1,0:T(8,128)(2,1)S(1)} collective-permute-done((bf16[2,64,256]{2,1,0:T(8,128)(2,1)S(1)}, bf16[2,64,256]{2,1,0:T(8,128)(2,1)S(1)}, u32[]{:S(2)}, u32[]{:S(2)}) %collective-permute-start.35) | collective-permute-done | bytes 65568 | tf_op jit(solution)/shard_map/ppermute | solution.py:945
  183.5 2.1 collective-permute-start.36
  186.4 3.6 %early_statistics.1.early_ref = f32[48,128]{1,0:T(8,128)} custom-call(f32[64,1152]{1,0:T(8,128)} %fusion.4.refs_0_.refs_1_, f32[3,64,96]{2,1,0:T(8,128)} %refs_3_.3, f32[3,32,64]{2,1,0:T(8,128)} %bitcast.97, f32[3,64,128]{2,1,0:T(8,128)} %refs_5_.3, f32[3,64,128]{2,1,0:T(8,128)} %bitcast.94, f32[64,128]{1,0:T(8,128)} %bitcast.100, f32[64,128]{1,0:T(8,128)} %refs_8_.3, ...), custom_call_target="tpu_custom_call" | custom-call | tf_op jit(solution)/shard_map/early_statistics/pallas_call | solution.py:815
  190.6 1.7 late_statistics.1
  192.3 1.4 collective-permute-done.37
  194.4 1.5 collective-permute-start.38
  198.3 1.5 collective-permute-done.39
  199.8 1.7 collective-permute-done.40
  204.2 2.4 %collective-permute-start.43 = (f32[48,128]{1,0:T(8,128)S(1)}, f32[48,128]{1,0:T(8,128)S(1)}, u32[]{:S(2)}, u32[]{:S(2)}) collective-permute-start(f32[48,128]{1,0:T(8,128)S(1)} %pad_maximum_fusion.13), channel_id=1, source_target_pairs={{0,24},{1,25},{2,26},{3,27},{4,28},{5,29},{6,30},{7,31},{8,16},{9,... | collective-permute-start | bytes 73736 | tf_op jit(solution)/shard_map/ppermute | solution.py:945
  207.7 2.1 collective-permute-done.43
  210.5 3.5 %update.1 = (f32[1,1]{1,0:T(1,128)}, f32[1,1]{1,0:T(1,128)}, f32[1,1]{1,0:T(1,128)}, f32[64,128]{1,0:T(8,128)}, f32[64,128]{1,0:T(8,128)}, /*index=5*/f32[1,128]...) custom-call(f32[48,128]{1,0:T(8,128)} %pad_maximum_fusion.12.refs_0_, ...), custom_call_target="tpu_custom_call" | custom-call | tf_op jit(solution)/shard_map/update/pallas_call | solution.py:934
  (206 shorter events, 48.4 us)
Async XLA Ops:
  2.5 6.5 %collective-permute-start = (bf16[1,64,256]{2,1,0:T(8,128)(2,1)}, bf16[1,64,256]{2,1,0:T(8,128)(2,1)S(1)}, u32[]{:S(2)}, u32[]{:S(2)}) collective-permute-start(bf16[1,64,256]{2,1,0:T(8,128)(2,1)} %bitcast.106), channel_id=1, source_target_pairs={{0,16},{1,17},{2,18},{3,19},{4,20},{5,21},{6,22},{7,23},{8,24},{9,... | collective-permute-start | bytes 98312 | tf_op jit(solution)/shard_map/ppermute | solution.py:945
  6.6 5.4 %collective-permute-start.6 = (bf16[1,64,384]{2,1,0:T(8,128)(2,1)}, bf16[1,64,384]{2,1,0:T(8,128)(2,1)S(1)}, u32[]{:S(2)}, u32[]{:S(2)}) collective-permute-start(bf16[1,64,384]{2,1,0:T(8,128)(2,1)} %bitcast.105), channel_id=1, source_target_pairs={{0,16},{1,17},{2,18},{3,19},{4,20},{5,21},{6,22},{7,23},{8,24},{9,... | collective-permute-start | bytes 147464 | tf_op jit(solution)/shard_map/ppermute | solution.py:945
  9.8 4.7 %collective-permute-start.1 = (bf16[2,64,256]{2,1,0:T(8,128)(2,1)S(1)}, bf16[2,64,256]{2,1,0:T(8,128)(2,1)S(1)}, u32[]{:S(2)}, u32[]{:S(2)}) collective-permute-start(bf16[2,64,256]{2,1,0:T(8,128)(2,1)S(1)} %pad_maximum_fusion.11), channel_id=1, source_target_pairs={{0,8},{1,9},{2,10},{3,11},{4,12},{5,13},{6,14},{7,15},{8,0},{9,1},... | collective-permute-start | bytes 196616 | tf_op jit(solution)/shard_map/ppermute | solution.py:945
  12.8 5.3 %collective-permute-start.7 = (bf16[2,64,384]{2,1,0:T(8,128)(2,1)S(1)}, bf16[2,64,384]{2,1,0:T(8,128)(2,1)S(1)}, u32[]{:S(2)}, u32[]{:S(2)}) collective-permute-start(bf16[2,64,384]{2,1,0:T(8,128)(2,1)S(1)} %pad_maximum_fusion.10), channel_id=1, source_target_pairs={{0,8},{1,9},{2,10},{3,11},{4,12},{5,13},{6,14},{7,15},{8,0},{9,1},... | collective-permute-start | bytes 294920 | tf_op jit(solution)/shard_map/ppermute | solution.py:945
  14.5 12.6 %copy-start.51 = (bf16[64,768]{1,0:T(8,128)(2,1)S(1)}, bf16[64,768]{1,0:T(8,128)(2,1)}, u32[]{:S(2)}) copy-start(bf16[64,768]{1,0:T(8,128)(2,1)} %get-tuple-element.151) | copy-start | bytes 294916
  14.5 7.0 %collective-permute-start.2 = (bf16[4,64,256]{2,1,0:T(8,128)(2,1)S(1)}, bf16[4,64,256]{2,1,0:T(8,128)(2,1)S(1)}, u32[]{:S(2)}, u32[]{:S(2)}) collective-permute-start(bf16[4,64,256]{2,1,0:T(8,128)(2,1)S(1)} %pad_maximum_fusion.9), channel_id=1, source_target_pairs={{0,6},{1,7},{2,4},{3,5},{4,2},{5,3},{6,0},{7,1},{8,14},{9,15},{10,... | collective-permute-start | bytes 393224 | tf_op jit(solution)/shard_map/ppermute | solution.py:945
  17.4 7.6 %collective-permute-start.3 = (bf16[4,64,256]{2,1,0:T(8,128)(2,1)S(1)}, bf16[4,64,256]{2,1,0:T(8,128)(2,1)S(1)}, u32[]{:S(2)}, u32[]{:S(2)}) collective-permute-start(bf16[4,64,256]{2,1,0:T(8,128)(2,1)S(1)} %pad_maximum_fusion.9), channel_id=1, source_target_pairs={{0,4},{1,5},{2,6},{3,7},{4,0},{5,1},{6,2},{7,3},{8,12},{9,13},{10,... | collective-permute-start | bytes 393224 | tf_op jit(solution)/shard_map/ppermute | solution.py:945
  17.9 9.0 %collective-permute-start.4 = (bf16[4,64,256]{2,1,0:T(8,128)(2,1)S(1)}, bf16[4,64,256]{2,1,0:T(8,128)(2,1)S(1)}, u32[]{:S(2)}, u32[]{:S(2)}) collective-permute-start(bf16[4,64,256]{2,1,0:T(8,128)(2,1)S(1)} %pad_maximum_fusion.9), channel_id=1, source_target_pairs={{0,2},{1,3},{2,0},{3,1},{4,6},{5,7},{6,4},{7,5},{8,10},{9,11},{10,... | collective-permute-start | bytes 393224 | tf_op jit(solution)/shard_map/ppermute | solution.py:945
  18.1 14.0 %collective-permute-start.10 = (bf16[4,64,384]{2,1,0:T(8,128)(2,1)S(1)}, bf16[4,64,384]{2,1,0:T(8,128)(2,1)S(1)}, u32[]{:S(2)}, u32[]{:S(2)}) collective-permute-start(bf16[4,64,384]{2,1,0:T(8,128)(2,1)S(1)} %pad_maximum_fusion.7), channel_id=1, source_target_pairs={{0,2},{1,3},{2,0},{3,1},{4,6},{5,7},{6,4},{7,5},{8,10},{9,11},{10,... | collective-permute-start | bytes 589832 | tf_op jit(solution)/shard_map/ppermute | solution.py:945
  20.1 13.8 %collective-permute-start.8 = (bf16[4,64,384]{2,1,0:T(8,128)(2,1)S(1)}, bf16[4,64,384]{2,1,0:T(8,128)(2,1)S(1)}, u32[]{:S(2)}, u32[]{:S(2)}) collective-permute-start(bf16[4,64,384]{2,1,0:T(8,128)(2,1)S(1)} %pad_maximum_fusion.7), channel_id=1, source_target_pairs={{0,6},{1,7},{2,4},{3,5},{4,2},{5,3},{6,0},{7,1},{8,14},{9,15},{10,... | collective-permute-start | bytes 589832 | tf_op jit(solution)/shard_map/ppermute | solution.py:945
  21.5 14.1 %collective-permute-start.9 = (bf16[4,64,384]{2,1,0:T(8,128)(2,1)S(1)}, bf16[4,64,384]{2,1,0:T(8,128)(2,1)S(1)}, u32[]{:S(2)}, u32[]{:S(2)}) collective-permute-start(bf16[4,64,384]{2,1,0:T(8,128)(2,1)S(1)} %pad_maximum_fusion.7), channel_id=1, source_target_pairs={{0,4},{1,5},{2,6},{3,7},{4,0},{5,1},{6,2},{7,3},{8,12},{9,13},{10,... | collective-permute-start | bytes 589832 | tf_op jit(solution)/shard_map/ppermute | solution.py:945
  27.0 8.9 %collective-permute-start.5 = (bf16[16,64,256]{2,1,0:T(8,128)(2,1)S(1)}, bf16[16,64,256]{2,1,0:T(8,128)(2,1)S(1)}, u32[]{:S(2)}, u32[]{:S(2)}) collective-permute-start(bf16[16,64,256]{2,1,0:T(8,128)(2,1)S(1)} %pad_maximum_fusion.2.own_ref), channel_id=1, source_target_pairs={{0,1},{1,0},{2,3},{3,2},{4,5},{5,4},{6,7},{7,6},{8,9},{9,8},{10,11... | collective-permute-start | bytes 1572872 | tf_op jit(solution)/shard_map/ppermute | solution.py:945
  27.1 8.9 %collective-permute-start.12 = (bf16[1,64,768]{2,1,0:T(8,128)(2,1)S(1)}, bf16[1,64,768]{2,1,0:T(8,128)(2,1)S(1)}, u32[]{:S(2)}, u32[]{:S(2)}) collective-permute-start(bf16[1,64,768]{2,1,0:T(8,128)(2,1)S(1)} %bitcast.102), channel_id=1, source_target_pairs={{0,24},{1,25},{2,26},{3,27},{4,28},{5,29},{6,30},{7,31},{8,16},{9,... | collective-permute-start | bytes 294920 | tf_op jit(solution)/shard_map/ppermute | solution.py:945
  32.1 8.5 %collective-permute-start.13 = (bf16[1,64,768]{2,1,0:T(8,128)(2,1)S(1)}, bf16[1,64,768]{2,1,0:T(8,128)(2,1)S(1)}, u32[]{:S(2)}, u32[]{:S(2)}) collective-permute-start(bf16[1,64,768]{2,1,0:T(8,128)(2,1)S(1)} %bitcast.103), channel_id=1, source_target_pairs={{0,16},{1,17},{2,18},{3,19},{4,20},{5,21},{6,22},{7,23},{8,24},{9,... | collective-permute-start | bytes 294920 | tf_op jit(solution)/shard_map/ppermute | solution.py:945
  33.9 6.8 %collective-permute-start.14 = (bf16[1,64,768]{2,1,0:T(8,128)(2,1)S(1)}, bf16[1,64,768]{2,1,0:T(8,128)(2,1)S(1)}, u32[]{:S(2)}, u32[]{:S(2)}) collective-permute-start(bf16[1,64,768]{2,1,0:T(8,128)(2,1)S(1)} %bitcast.104), channel_id=1, source_target_pairs={{0,8},{1,9},{2,10},{3,11},{4,12},{5,13},{6,14},{7,15},{8,0},{9,1},... | collective-permute-start | bytes 294920 | tf_op jit(solution)/shard_map/ppermute | solution.py:945
  35.9 26.4 %collective-permute-start.11 = (bf16[16,64,384]{2,1,0:T(8,128)(2,1)S(1)}, bf16[16,64,384]{2,1,0:T(8,128)(2,1)S(1)}, u32[]{:S(2)}, u32[]{:S(2)}) collective-permute-start(bf16[16,64,384]{2,1,0:T(8,128)(2,1)S(1)} %pad_maximum_fusion.1.own_ref), channel_id=1, source_target_pairs={{0,1},{1,0},{2,3},{3,2},{4,5},{5,4},{6,7},{7,6},{8,9},{9,8},{10,11... | collective-permute-start | bytes 2359304 | tf_op jit(solution)/shard_map/ppermute | solution.py:945
  41.5 16.9 %collective-permute-start.15 = (bf16[4,64,768]{2,1,0:T(8,128)(2,1)}, bf16[4,64,768]{2,1,0:T(8,128)(2,1)}, u32[]{:S(2)}, u32[]{:S(2)}) collective-permute-start(bf16[4,64,768]{2,1,0:T(8,128)(2,1)} %pad_maximum_fusion.3), channel_id=1, source_target_pairs={{0,2},{1,3},{2,0},{3,1},{4,6},{5,7},{6,4},{7,5},{8,10},{9,11},{10,... | collective-permute-start | bytes 1179656 | tf_op jit(solution)/shard_map/ppermute | solution.py:945
  42.8 15.7 %collective-permute-start.16 = (bf16[4,64,768]{2,1,0:T(8,128)(2,1)}, bf16[4,64,768]{2,1,0:T(8,128)(2,1)}, u32[]{:S(2)}, u32[]{:S(2)}) collective-permute-start(bf16[4,64,768]{2,1,0:T(8,128)(2,1)} %pad_maximum_fusion.3), channel_id=1, source_target_pairs={{0,4},{1,5},{2,6},{3,7},{4,0},{5,1},{6,2},{7,3},{8,12},{9,13},{10,... | collective-permute-start | bytes 1179656 | tf_op jit(solution)/shard_map/ppermute | solution.py:945
  44.3 18.1 %collective-permute-start.17 = (bf16[4,64,768]{2,1,0:T(8,128)(2,1)}, bf16[4,64,768]{2,1,0:T(8,128)(2,1)}, u32[]{:S(2)}, u32[]{:S(2)}) collective-permute-start(bf16[4,64,768]{2,1,0:T(8,128)(2,1)} %pad_maximum_fusion.3), channel_id=1, source_target_pairs={{0,6},{1,7},{2,4},{3,5},{4,2},{5,3},{6,0},{7,1},{8,14},{9,15},{10,... | collective-permute-start | bytes 1179656 | tf_op jit(solution)/shard_map/ppermute | solution.py:945
  65.5 18.0 %collective-permute-start.18 = (bf16[16,64,768]{2,1,0:T(8,128)(2,1)S(1)}, bf16[16,64,768]{2,1,0:T(8,128)(2,1)S(1)}, u32[]{:S(2)}, u32[]{:S(2)}) collective-permute-start(bf16[16,64,768]{2,1,0:T(8,128)(2,1)S(1)} %pad_maximum_fusion.own_ref), channel_id=1, source_target_pairs={{0,1},{1,0},{2,3},{3,2},{4,5},{5,4},{6,7},{7,6},{8,9},{9,8},{10,11... | collective-permute-start | bytes 4718600 | tf_op jit(solution)/shard_map/ppermute | solution.py:945
  83.4 11.2 %copy-start.21 = (f32[1536,256]{1,0:T(8,128)}, f32[1536,256]{1,0:T(8,128)S(1)}, u32[]{:S(2)}) copy-start(f32[1536,256]{1,0:T(8,128)S(1)} %get-tuple-element.180.refs_0_) | copy-start | bytes 4718596
  83.4 11.2 %copy-start.7 = (s32[16,48,32]{1,2,0:T(8,128)S(1)}, s32[16,48,32]{1,2,0:T(8,128)}, u32[]{:S(2)}) copy-start(s32[16,48,32]{1,2,0:T(8,128)} %param.25) | copy-start | bytes 294916
  103.1 12.5 %copy-start.1 = (f32[2,256]{1,0:T(2,128)}, f32[2,256]{1,0:T(2,128)S(1)}, u32[]{:S(2)}) copy-start(f32[2,256]{1,0:T(2,128)S(1)} %get-tuple-element.221.refs_13_) | copy-start | bytes 6148
  103.1 14.2 %collective-permute-start.19 = (bf16[16,64,384]{2,1,0:T(8,128)(2,1)S(1)}, bf16[16,64,384]{2,1,0:T(8,128)(2,1)S(1)}, u32[]{:S(2)}, u32[]{:S(2)}) collective-permute-start(bf16[16,64,384]{2,1,0:T(8,128)(2,1)S(1)} %get-tuple-element.176), channel_id=1, source_target_pairs={{0,1},{1,0},{2,3},{3,2},{4,5},{5,4},{6,7},{7,6},{8,9},{9,8},{10,11... | collective-permute-start | bytes 2359304 | tf_op jit(solution)/shard_map/ppermute | solution.py:945
  118.2 2.8 %collective-permute-start.20 = (bf16[16,64,384]{2,1,0:T(8,128)(2,1)}, bf16[16,64,384]{2,1,0:T(8,128)(2,1)}, u32[]{:S(2)}, u32[]{:S(2)}) collective-permute-start(bf16[16,64,384]{2,1,0:T(8,128)(2,1)} %get-tuple-element.179), channel_id=1, source_target_pairs={{0,1},{1,0},{2,3},{3,2},{4,5},{5,4},{6,7},{7,6},{8,9},{9,8},{10,11... | collective-permute-start | bytes 2359304 | tf_op jit(solution)/shard_map/ppermute | solution.py:945
  123.8 24.7 %collective-permute-start.21 = (bf16[4,64,768]{2,1,0:T(8,128)(2,1)S(1)}, bf16[4,64,768]{2,1,0:T(8,128)(2,1)S(1)}, u32[]{:S(2)}, u32[]{:S(2)}) collective-permute-start(bf16[4,64,768]{2,1,0:T(8,128)(2,1)S(1)} %pad_maximum_fusion.4), channel_id=1, source_target_pairs={{0,2},{1,3},{2,0},{3,1},{4,6},{5,7},{6,4},{7,5},{8,10},{9,11},{10,... | collective-permute-start | bytes 1179656 | tf_op jit(solution)/shard_map/ppermute | solution.py:945
  124.7 23.8 %collective-permute-start.22 = (bf16[4,64,768]{2,1,0:T(8,128)(2,1)S(1)}, bf16[4,64,768]{2,1,0:T(8,128)(2,1)S(1)}, u32[]{:S(2)}, u32[]{:S(2)}) collective-permute-start(bf16[4,64,768]{2,1,0:T(8,128)(2,1)S(1)} %pad_maximum_fusion.5), channel_id=1, source_target_pairs={{0,4},{1,5},{2,6},{3,7},{4,0},{5,1},{6,2},{7,3},{8,12},{9,13},{10,... | collective-permute-start | bytes 1179656 | tf_op jit(solution)/shard_map/ppermute | solution.py:945
  126.2 22.3 %collective-permute-start.23 = (bf16[4,64,768]{2,1,0:T(8,128)(2,1)S(1)}, bf16[4,64,768]{2,1,0:T(8,128)(2,1)S(1)}, u32[]{:S(2)}, u32[]{:S(2)}) collective-permute-start(bf16[4,64,768]{2,1,0:T(8,128)(2,1)S(1)} %pad_maximum_fusion.6), channel_id=1, source_target_pairs={{0,6},{1,7},{2,4},{3,5},{4,2},{5,3},{6,0},{7,1},{8,14},{9,15},{10,... | collective-permute-start | bytes 1179656 | tf_op jit(solution)/shard_map/ppermute | solution.py:945
  149.6 2.7 %collective-permute-start.24 = (bf16[16,64,384]{2,1,0:T(8,128)(2,1)S(1)}, bf16[16,64,384]{2,1,0:T(8,128)(2,1)S(1)}, u32[]{:S(2)}, u32[]{:S(2)}) collective-permute-start(bf16[16,64,384]{2,1,0:T(8,128)(2,1)S(1)} %get-tuple-element.205), channel_id=1, source_target_pairs={{0,1},{1,0},{2,3},{3,2},{4,5},{5,4},{6,7},{7,6},{8,9},{9,8},{10,11... | collective-permute-start | bytes 2359304 | tf_op jit(solution)/shard_map/ppermute | solution.py:945
  152.6 14.3 %collective-permute-start.25 = (bf16[2,64,768]{2,1,0:T(8,128)(2,1)S(1)}, bf16[2,64,768]{2,1,0:T(8,128)(2,1)S(1)}, u32[]{:S(2)}, u32[]{:S(2)}) collective-permute-start(bf16[2,64,768]{2,1,0:T(8,128)(2,1)S(1)} %select_convert_fusion), channel_id=1, source_target_pairs={{0,8},{1,9},{2,10},{3,11},{4,12},{5,13},{6,14},{7,15},{8,0},{9,1},... | collective-permute-start | bytes 589832 | tf_op jit(solution)/shard_map/ppermute | solution.py:945
  153.3 13.6 %collective-permute-start.26 = (bf16[4,64,384]{2,1,0:T(8,128)(2,1)S(1)}, bf16[4,64,384]{2,1,0:T(8,128)(2,1)S(1)}, u32[]{:S(2)}, u32[]{:S(2)}) collective-permute-start(bf16[4,64,384]{2,1,0:T(8,128)(2,1)S(1)} %get-tuple-element.211), channel_id=1, source_target_pairs={{0,2},{1,3},{2,0},{3,1},{4,6},{5,7},{6,4},{7,5},{8,10},{9,11},{10,... | collective-permute-start | bytes 589832 | tf_op jit(solution)/shard_map/ppermute | solution.py:945
  153.6 13.3 %collective-permute-start.27 = (bf16[4,64,384]{2,1,0:T(8,128)(2,1)S(1)}, bf16[4,64,384]{2,1,0:T(8,128)(2,1)S(1)}, u32[]{:S(2)}, u32[]{:S(2)}) collective-permute-start(bf16[4,64,384]{2,1,0:T(8,128)(2,1)S(1)} %get-tuple-element.212), channel_id=1, source_target_pairs={{0,4},{1,5},{2,6},{3,7},{4,0},{5,1},{6,2},{7,3},{8,12},{9,13},{10,... | collective-permute-start | bytes 589832 | tf_op jit(solution)/shard_map/ppermute | solution.py:945
  155.0 11.8 %collective-permute-start.28 = (bf16[4,64,384]{2,1,0:T(8,128)(2,1)S(1)}, bf16[4,64,384]{2,1,0:T(8,128)(2,1)S(1)}, u32[]{:S(2)}, u32[]{:S(2)}) collective-permute-start(bf16[4,64,384]{2,1,0:T(8,128)(2,1)S(1)} %get-tuple-element.213), channel_id=1, source_target_pairs={{0,6},{1,7},{2,4},{3,5},{4,2},{5,3},{6,0},{7,1},{8,14},{9,15},{10,... | collective-permute-start | bytes 589832 | tf_op jit(solution)/shard_map/ppermute | solution.py:945
  166.9 2.0 collective-permute-start.30
  167.2 5.5 %collective-permute-start.29 = (bf16[2,64,384]{2,1,0:T(8,128)(2,1)S(1)}, bf16[2,64,384]{2,1,0:T(8,128)(2,1)S(1)}, u32[]{:S(2)}, u32[]{:S(2)}) collective-permute-start(bf16[2,64,384]{2,1,0:T(8,128)(2,1)S(1)} %select_convert_fusion.2), channel_id=1, source_target_pairs={{0,8},{1,9},{2,10},{3,11},{4,12},{5,13},{6,14},{7,15},{8,0},{9,1},... | collective-permute-start | bytes 294920 | tf_op jit(solution)/shard_map/ppermute | solution.py:945
  169.1 6.1 %collective-permute-start.32 = (bf16[4,64,256]{2,1,0:T(8,128)(2,1)S(1)}, bf16[4,64,256]{2,1,0:T(8,128)(2,1)S(1)}, u32[]{:S(2)}, u32[]{:S(2)}) collective-permute-start(bf16[4,64,256]{2,1,0:T(8,128)(2,1)S(1)} %get-tuple-element.274), channel_id=1, source_target_pairs={{0,2},{1,3},{2,0},{3,1},{4,6},{5,7},{6,4},{7,5},{8,10},{9,11},{10,... | collective-permute-start | bytes 393224 | tf_op jit(solution)/shard_map/ppermute | solution.py:945
  169.8 6.1 %collective-permute-start.33 = (bf16[4,64,256]{2,1,0:T(8,128)(2,1)S(1)}, bf16[4,64,256]{2,1,0:T(8,128)(2,1)S(1)}, u32[]{:S(2)}, u32[]{:S(2)}) collective-permute-start(bf16[4,64,256]{2,1,0:T(8,128)(2,1)S(1)} %get-tuple-element.273), channel_id=1, source_target_pairs={{0,4},{1,5},{2,6},{3,7},{4,0},{5,1},{6,2},{7,3},{8,12},{9,13},{10,... | collective-permute-start | bytes 393224 | tf_op jit(solution)/shard_map/ppermute | solution.py:945
  171.3 7.4 %collective-permute-start.34 = (bf16[4,64,256]{2,1,0:T(8,128)(2,1)S(1)}, bf16[4,64,256]{2,1,0:T(8,128)(2,1)S(1)}, u32[]{:S(2)}, u32[]{:S(2)}) collective-permute-start(bf16[4,64,256]{2,1,0:T(8,128)(2,1)S(1)} %get-tuple-element.272), channel_id=1, source_target_pairs={{0,6},{1,7},{2,4},{3,5},{4,2},{5,3},{6,0},{7,1},{8,14},{9,15},{10,... | collective-permute-start | bytes 393224 | tf_op jit(solution)/shard_map/ppermute | solution.py:945
  172.7 12.9 %collective-permute-start.31 = (bf16[1,64,1152]{2,1,0:T(8,128)(2,1)S(1)}, bf16[1,64,1152]{2,1,0:T(8,128)(2,1)S(1)}, u32[]{:S(2)}, u32[]{:S(2)}) collective-permute-start(bf16[1,64,1152]{2,1,0:T(8,128)(2,1)S(1)} %pad_maximum_fusion.8), channel_id=1, source_target_pairs={{0,16},{1,17},{2,18},{3,19},{4,20},{5,21},{6,22},{7,23},{8,24},{9,... | collective-permute-start | bytes 442376 | tf_op jit(solution)/shard_map/ppermute | solution.py:945
  178.8 4.7 %collective-permute-start.35 = (bf16[2,64,256]{2,1,0:T(8,128)(2,1)S(1)}, bf16[2,64,256]{2,1,0:T(8,128)(2,1)S(1)}, u32[]{:S(2)}, u32[]{:S(2)}) collective-permute-start(bf16[2,64,256]{2,1,0:T(8,128)(2,1)S(1)} %select_convert_fusion.3), channel_id=1, source_target_pairs={{0,8},{1,9},{2,10},{3,11},{4,12},{5,13},{6,14},{7,15},{8,0},{9,1},... | collective-permute-start | bytes 196616 | tf_op jit(solution)/shard_map/ppermute | solution.py:945
  183.5 6.4 %collective-permute-start.36 = (bf16[1,64,256]{2,1,0:T(8,128)(2,1)S(1)}, bf16[1,64,256]{2,1,0:T(8,128)(2,1)S(1)}, u32[]{:S(2)}, u32[]{:S(2)}) collective-permute-start(bf16[1,64,256]{2,1,0:T(8,128)(2,1)S(1)} %select_convert_fusion.5), channel_id=1, source_target_pairs={{0,16},{1,17},{2,18},{3,19},{4,20},{5,21},{6,22},{7,23},{8,24},{9,... | collective-permute-start | bytes 98312 | tf_op jit(solution)/shard_map/ppermute | solution.py:945
  192.3 1.4 collective-permute-start.37
  194.4 3.9 %collective-permute-start.38 = (f32[48,128]{1,0:T(8,128)S(1)}, f32[48,128]{1,0:T(8,128)S(1)}, u32[]{:S(2)}, u32[]{:S(2)}) collective-permute-start(f32[48,128]{1,0:T(8,128)S(1)} %pad_maximum_fusion.14), channel_id=1, source_target_pairs={{0,4},{1,5},{2,6},{3,7},{4,0},{5,1},{6,2},{7,3},{8,12},{9,13},{10,... | collective-permute-start | bytes 73736 | tf_op jit(solution)/shard_map/ppermute | solution.py:945
  195.9 3.8 %collective-permute-start.39 = (f32[48,128]{1,0:T(8,128)S(1)}, f32[48,128]{1,0:T(8,128)S(1)}, u32[]{:S(2)}, u32[]{:S(2)}) collective-permute-start(f32[48,128]{1,0:T(8,128)S(1)} %pad_maximum_fusion.14), channel_id=1, source_target_pairs={{0,2},{1,3},{2,0},{3,1},{4,6},{5,7},{6,4},{7,5},{8,10},{9,11},{10,... | collective-permute-start | bytes 73736 | tf_op jit(solution)/shard_map/ppermute | solution.py:945
  196.7 4.7 %collective-permute-start.40 = (f32[48,128]{1,0:T(8,128)S(1)}, f32[48,128]{1,0:T(8,128)S(1)}, u32[]{:S(2)}, u32[]{:S(2)}) collective-permute-start(f32[48,128]{1,0:T(8,128)S(1)} %pad_maximum_fusion.14), channel_id=1, source_target_pairs={{0,6},{1,7},{2,4},{3,5},{4,2},{5,3},{6,0},{7,1},{8,14},{9,15},{10,... | collective-permute-start | bytes 73736 | tf_op jit(solution)/shard_map/ppermute | solution.py:945
  202.2 4.4 %collective-permute-start.41 = (f32[48,128]{1,0:T(8,128)S(1)}, f32[48,128]{1,0:T(8,128)S(1)}, u32[]{:S(2)}, u32[]{:S(2)}) collective-permute-start(f32[48,128]{1,0:T(8,128)S(1)} %pad_maximum_fusion.13), channel_id=1, source_target_pairs={{0,8},{1,9},{2,10},{3,11},{4,12},{5,13},{6,14},{7,15},{8,0},{9,1},... | collective-permute-start | bytes 73736 | tf_op jit(solution)/shard_map/ppermute | solution.py:945
  203.0 4.7 %collective-permute-start.42 = (f32[48,128]{1,0:T(8,128)S(1)}, f32[48,128]{1,0:T(8,128)S(1)}, u32[]{:S(2)}, u32[]{:S(2)}) collective-permute-start(f32[48,128]{1,0:T(8,128)S(1)} %pad_maximum_fusion.13), channel_id=1, source_target_pairs={{0,16},{1,17},{2,18},{3,19},{4,20},{5,21},{6,22},{7,23},{8,24},{9,... | collective-permute-start | bytes 73736 | tf_op jit(solution)/shard_map/ppermute | solution.py:945
  204.2 5.6 %collective-permute-start.43 = (f32[48,128]{1,0:T(8,128)S(1)}, f32[48,128]{1,0:T(8,128)S(1)}, u32[]{:S(2)}, u32[]{:S(2)}) collective-permute-start(f32[48,128]{1,0:T(8,128)S(1)} %pad_maximum_fusion.13), channel_id=1, source_target_pairs={{0,24},{1,25},{2,26},{3,27},{4,28},{5,29},{6,30},{7,31},{8,16},{9,... | collective-permute-start | bytes 73736 | tf_op jit(solution)/shard_map/ppermute | solution.py:945
  (48 other events, 177.7 us)
where the time goes:
time: 215 us; the launch traced here: 214 us
  Pallas kernels  86.5 us (40%)
  starting transfers between devices  55.4 us (26%)
  waiting for transfers between devices  31.2 us (15%)
  local copies, waits for them, and re-layouts  24.9 us (12%)
  other arithmetic  14.6 us (7%)
    ppermute x44, starting transfers between devices, swap(): lax.ppermute(value, ('dp', 'fsdp'), [(place, place ^ mask) for place in r...  55.4 us
    pallas_call x3, Pallas kernels, run_backward(): pl.pallas_call(functools.partial(backward_kernel, layer, widths, mesh_pla...  35.6 us
    pallas_call x3, Pallas kernels, run_forward(): pl.pallas_call(functools.partial(forward_kernel, layer, widths, mesh_plan...  31.8 us
    ppermute x44, waiting for transfers between devices, swap(): lax.ppermute(value, ('dp', 'fsdp'), [(place, place ^ mask) for place in r...  31.2 us
    unnamed x104, local copies, waits for them, and re-layouts  23.2 us
    pallas_call x1, Pallas kernels, run_top(): pl.pallas_call(functools.partial(top_kernel, widths, gather_plan, mesh_pl...  8.48 us
    add x10, other arithmetic, join(): summed = summed + other.astype(jnp.float32)  4.82 us
    select_n x9, other arithmetic, join(): jnp.where(upper, pieces[place ^ 1 << at], pieces[place])  4.74 us
  transfers between devices with their start and end apart: 44, of which 18 were waited for; matrix products, arithmetic and copies ran while one was open for 4% of the time, Pallas kernels for 28%

commit v1 on v0

--- a/solution.py
+++ b/solution.py
@@ -292,6 +292,10 @@
     return dmiddle + through, gain_part
 
 
+def vmem_bytes(blocks, share=1.0):
+    return int(VMEM_BYTES * share) if blocks.shape[1] >= 64 else 2 * VMEM_BYTES
+
+
 def row_spec(width, rows=ROWS):
     return pl.BlockSpec((rows, width), lambda step: (step, 0))
 
@@ -323,7 +327,7 @@
         att = [(att_ref, 0), (att_ref, 3 * D)]
         before = [(before_ref, 0)] if layer == 0 else [(before_ref, 0), (before_ref, FF)]
         targets = att + before if layer == 0 else before + att
-        place_weights(targets, own_ref, other_ref, core_ref[0], widths[: len(targets)], mesh_plan)
+        place_weights(targets, own_ref, other_ref, core_ref[0] & 1, widths[: len(targets)], mesh_plan)
 
     if layer == 0:
         one_hot_rows(source_ref, refs[8], 0)
@@ -355,7 +359,12 @@
         (shape((short, D), f32), row_spec(D, GROUP * queries)),
         (shape((tokens, 3 * D), b16), row_spec(3 * D)),
         (shape((short, D), b16), row_spec(D, GROUP * queries)),
-        (shape((tokens // CTX, 2, CTX, HEADS // 2 * queries), b16), chance_spec(queries)),
+        (
+            (shape if layer == LAYERS - 1 else pltpu.HBM)(
+                (tokens // CTX, 2, CTX, HEADS // 2 * queries), b16
+            ),
+            chance_spec(queries),
+        ),
         (shape((D, 4 * D), b16), whole_spec((D, 4 * D))),
     ]
     scratch = [pltpu.VMEM((2, CTX, HEADS // 2 * queries), f32)]
@@ -365,7 +374,7 @@
     else:
         source_spec = row_spec(D)
         outs.append((shape((D, 2 * FF), b16), whole_spec((D, 2 * FF))))
-        outs = outs + [(shape((tokens, FF), b16), row_spec(FF))] * 2
+        outs = outs + [(pltpu.HBM((tokens, FF), b16), row_spec(FF))] * 2
     return pl.pallas_call(
         functools.partial(forward_kernel, layer, widths, mesh_plan),
         grid=(tokens // ROWS,),
@@ -380,7 +389,7 @@
         out_specs=[spec for _, spec in outs],
         out_shape=[item for item, _ in outs],
         scratch_shapes=scratch,
-        compiler_params=pltpu.CompilerParams(vmem_limit_bytes=VMEM_BYTES),
+        compiler_params=pltpu.CompilerParams(vmem_limit_bytes=vmem_bytes(own, 0.6)),
         cost_estimate=pl.CostEstimate(
             flops=2 * tokens * D * 12 * D,
             bytes_accessed=tokens * D * 16 + D * 12 * D * 4,
@@ -402,7 +411,7 @@
         [(weight_ref, 0), (weight_ref, FF), (head_ref, 0)],
         own_ref,
         other_ref,
-        core_ref[0],
+        core_ref[0] & 1,
         widths,
         gather_plan,
         start,
@@ -479,7 +488,7 @@
     gain_ref[0:1, :] = gain_sum
     sum_ref[:, 0:FF] = dot_nn(normed_ref[...].T, dinner_ref[...])
     sum_ref[:, FF : 2 * FF] = dot_nn(dout_ref[...].T, inner_ref[...])
-    write_blocks(send_ref, keep_ref, sum_ref, core_ref[0], widths, mesh_plan)
+    write_blocks(send_ref, keep_ref, sum_ref, core_ref[0] & 1, widths, mesh_plan)
 
 
 def block_outs(own, widths):
@@ -516,7 +525,7 @@
             pltpu.VMEM((CATS, tokens), jnp.int32),
             pltpu.VMEM((1, tokens), f32),
         ],
-        compiler_params=pltpu.CompilerParams(vmem_limit_bytes=VMEM_BYTES),
+        compiler_params=pltpu.CompilerParams(vmem_limit_bytes=vmem_bytes(own)),
         cost_estimate=pl.CostEstimate(
             flops=6 * tokens * D * 3 * FF,
             bytes_accessed=tokens * D * 8 + D * 3 * FF * 10,
@@ -590,7 +599,7 @@
             wide = right.shape[1]
             sum_ref[:, column : column + wide] = dot_nn(left[...].T, right[...])
             column += wide
-        write_blocks(send_ref, keep_ref, sum_ref, core_ref[0], widths, mesh_plan)
+        write_blocks(send_ref, keep_ref, sum_ref, core_ref[0] & 1, widths, mesh_plan)
 
 
 def run_backward(layer, widths, mesh_plan, blocks_like, saved, dmiddle, gains, core, before):
@@ -600,6 +609,11 @@
     short = tokens // CTX * queries
     f32, b16 = jnp.float32, jnp.bfloat16
     shape = jax.ShapeDtypeStruct
+    in_hbm = lambda item: pltpu.with_memory_space_constraint(item, pltpu.HBM)
+    if layer < LAYERS - 1:
+        chance = in_hbm(chance)
+    if layer > 0:
+        before = before[:2] + (in_hbm(before[2]), in_hbm(before[3]))
     in_specs = [
         row_spec(D),
         row_spec(3 * D),
@@ -646,7 +660,7 @@
         out_specs=[spec for _, spec in outs],
         out_shape=[item for item, _ in outs],
         scratch_shapes=scratch,
-        compiler_params=pltpu.CompilerParams(vmem_limit_bytes=VMEM_BYTES),
+        compiler_params=pltpu.CompilerParams(vmem_limit_bytes=vmem_bytes(blocks_like)),
         cost_estimate=pl.CostEstimate(
             flops=6 * tokens * D * wide,
             bytes_accessed=tokens * D * 24 + D * wide * 6,
@@ -964,55 +978,106 @@
     return lax.optimization_barrier((value,) + ahead)[0]
 
 
+def own_digit(device_ref, step):
+    digit = 0
+    for bit in step:
+        digit = 2 * digit + ((device_ref[0] >> bit) & 1)
+    return digit
+
+
+def gather_kernel(step, device_ref, *refs):
+    count = 1 << len(step)
+    own = own_digit(device_ref, step)
+    blocks = refs[0].shape[0]
+    for digit in range(count):
+        base = (own ^ digit) * blocks
+        for block in range(blocks):
+            refs[count][base + block] = refs[digit][block]
+
+
+def run_gather_join(step, pieces, device):
+    vmem = pl.BlockSpec(memory_space=pltpu.VMEM)
+    blocks, rows, width = pieces[0].shape
+    return pl.pallas_call(
+        functools.partial(gather_kernel, step),
+        in_specs=[smem_spec()] + [vmem] * len(pieces),
+        out_specs=vmem,
+        out_shape=jax.ShapeDtypeStruct((blocks * len(pieces), rows, width), jnp.bfloat16),
+        name="gather_join",
+    )(device, *pieces)
+
+
+def scatter_kernel(step, counts, device_ref, *refs):
+    parts, at = [], 0
+    for count in counts:
+        parts.append(refs[at : at + 1 + count])
+        at += 1 + count
+    targets = refs[at:]
+    own = own_digit(device_ref, step)
+    blocks = targets[0].shape[0]
+    for digit, target in enumerate(targets):
+        base = (own ^ digit) * blocks
+        for block in range(blocks):
+            columns = []
+            for part in parts:
+                total = part[0][base + block]
+                for other in part[1:]:
+                    total = total + other[base + block].astype(jnp.float32)
+                columns.append(total)
+            target[block] = jnp.concatenate(columns, axis=1).astype(target.dtype)
+
+
+def run_scatter_join(step, chunks, device):
+    vmem = pl.BlockSpec(memory_space=pltpu.VMEM)
+    count = 1 << len(step)
+    blocks, rows, _ = chunks[0].kept.shape
+    shape = (blocks // count, rows, sum(chunk.kept.shape[2] for chunk in chunks))
+    operands = []
+    for chunk in chunks:
+        operands = operands + [chunk.kept] + list(chunk.others)
+    return pl.pallas_call(
+        functools.partial(scatter_kernel, step, [len(chunk.others) for chunk in chunks]),
+        in_specs=[smem_spec()] + [vmem] * len(operands),
+        out_specs=[vmem] * count,
+        out_shape=[
+            jax.ShapeDtypeStruct(shape, jnp.bfloat16 if digit else jnp.float32)
+            for digit in range(count)
+        ],
+        name="scatter_join",
+    )(device, *operands)
+
+
 class Gather:
-    def __init__(self, piece, steps):
-        self.held, self.steps, self.at = piece[None], steps, 0
+    def __init__(self, held, steps, device, at=0):
+        self.held, self.steps, self.device, self.at = held, steps, device, at
 
     def send(self):
         self.others = tuple(swap(self.held, mask) for mask in step_masks(self.steps[self.at]))
 
     def join(self):
-        step = self.steps[self.at]
         pieces = [self.held] + list(self.others)
-        for at, bit in enumerate(step[::-1]):
-            upper = (device_index() >> bit) & 1 == 1
-            pieces = [
-                jnp.where(upper, pieces[place ^ (1 << at)], pieces[place])
-                for place in range(len(pieces))
-            ]
-        self.held = jnp.concatenate(pieces)
+        self.held = run_gather_join(self.steps[self.at], pieces, self.device)
         self.at += 1
 
 
 class Scatter:
-    def __init__(self, sent, kept, steps):
-        self.sent, self.kept, self.steps, self.at = (sent,), kept, steps, 0
+    def __init__(self, sent, kept, steps, device, at=0):
+        self.sent, self.kept, self.steps, self.device, self.at = sent, kept, steps, device, at
 
     def send(self):
         masks = step_masks(self.steps[self.at])
         self.others = tuple(swap(sent, mask) for sent, mask in zip(self.sent, masks))
 
     def join(self):
-        self.at += 1
-        summed = self.kept
-        for other in self.others:
-            summed = summed + other.astype(jnp.float32)
-        if self.at == len(self.steps):
-            self.kept = summed
-            return
-        step = self.steps[self.at]
-        count = 1 << len(step)
-        own = 0
-        for bit in step:
-            own = 2 * own + ((device_index() >> bit) & 1)
-        parts = summed.reshape((count, summed.shape[0] // count) + summed.shape[1:])
-        if count == 2:
-            self.sent = (jnp.where(own == 1, parts[0], parts[1]).astype(jnp.bfloat16),)
-            self.kept = jnp.where(own == 1, parts[1], parts[0])
-            return
-        pick = lambda digit: lax.dynamic_index_in_dim(parts, own ^ digit, 0, keepdims=False)
-        self.sent = tuple(pick(digit).astype(jnp.bfloat16) for digit in range(1, count))
-        self.kept = pick(0)
+        joined = join_all([self])
+        self.sent, self.kept, self.at = joined.sent, joined.kept, joined.at
+
+
+def join_all(chunks):
+    steps, at, device = chunks[0].steps, chunks[0].at + 1, chunks[0].device
+    step = steps[at] if at < len(steps) else ()
+    kept, *sent = run_scatter_join(step, chunks, device)
+    return Scatter(tuple(sent), kept, steps, device, at)
 
 
 def sum_packets(packet, group, inner_bits):
@@ -1074,12 +1139,9 @@
     sizes = (lax.axis_size("dp"), lax.axis_size("fsdp"))
     highest = (sizes[0] * sizes[1]).bit_length() - 1
     gather_steps = [(bit,) for bit in reversed(range(3, highest))] + [(2, 1), (0,)]
-    third_steps = [(4, 3)] + [(bit,) for bit in range(5, highest)] + [(2, 1), (0,)]
     scatter_steps = gather_steps[::-1]
     mesh_plan = (sizes[0], sizes[1], gather_steps)
-    third_plan = (sizes[0], sizes[1], third_steps)
-    core = (lax.axis_index("fsdp") & 1).astype(jnp.int32).reshape(1)
-
+    device = device_index().astype(jnp.int32).reshape(1)
     out_turned = jnp.swapaxes(out_weight, 1, 2)
     down_turned = jnp.swapaxes(down_weight, 1, 2)
     masters = [qkv_weight, out_turned, up_weight, down_turned, embed.T, head_weight]
@@ -1091,28 +1153,40 @@
         ffn_widths + att_widths,
         ffn_widths + att_widths + ffn_widths + widths[5:6],
     ]
-    first, second, third = [
-        Gather(piece, steps)
-        for piece, steps in zip(
-            run_pack(masters, chunk_widths), [gather_steps, gather_steps, third_steps]
-        )
+    chunks = [
+        Gather(piece[None], gather_steps, device) for piece in run_pack(masters, chunk_widths)
     ]
+    first, second, third = chunks
     latent_rows = latents.transpose(0, 2, 1)
     target_rows = targets.transpose(0, 2, 1)
-    shared = (gains, memory_valid, core)
-    back_shared = (gains, core)
+    shared = (gains, memory_valid, device)
+    back_shared = (gains, device)
 
     count = len(gather_steps)
-    while first.at < count - 1:
+    for at in range(count - 2):
         first.send()
         second.send()
+        if at == 0:
+            third.send()
+            first.others, second.others = tie(first.others, second.others)
+        else:
+            first.others, second.others, third.others = tie(
+                first.others, second.others, third.others
+            )
+            third.join()
         first.join()
         second.join()
-    while third.at < len(third_steps) - 2:
-        third.send()
-        third.join()
+        if at > 0:
+            first.held, second.held, third.held = tie(first.held, second.held, third.held)
+            third.send()
+    first.send()
+    second.send()
+    first.others, second.others, third.others = tie(first.others, second.others, third.others)
+    first.join()
+    first.send()
+    second.join()
+    third.join()
     third.send()
-    first.send()
     (other,) = first.others
     held, other, second.held = tie(first.held, other, second.held)
     second.send()
@@ -1125,11 +1199,11 @@
         run_forward(1, chunk_widths[1], mesh_plan, middle, second.held, other, *shared)
     )
     middle, (other,) = tie(kept[1][1], third.others)
-    kept.append(run_forward(2, chunk_widths[2], third_plan, middle, third.held, other, *shared))
+    kept.append(run_forward(2, chunk_widths[2], mesh_plan, middle, third.held, other, *shared))
 
     dmiddle, sent, held, gain_top, loss, counted = run_top(
         ffn_widths + widths[5:6],
-        third_plan,
+        mesh_plan,
         mesh_plan,
         sum(ffn_widths + att_widths),
         kept[2][1],
@@ -1138,9 +1212,9 @@
         target_rows,
         gains,
         horizon,
-        core,
-    )
-    top = Scatter(sent, held, scatter_steps)
+        device,
+    )
+    top = Scatter((sent,), held, scatter_steps, device)
     top.send()
     like = first.held
     before = [(kept[at][1], kept[at + 1][6], kept[at + 1][8], kept[at + 1][7]) for at in range(2)]
@@ -1148,18 +1222,16 @@
         2, chunk_widths[1], mesh_plan, like, kept[2], dmiddle, *back_shared, before[1]
     )
     dmiddle, sent, held, top.others = tie(dmiddle, sent, held, top.others)
-    two = Scatter(sent, held, scatter_steps)
+    two = Scatter((sent,), held, scatter_steps, device)
     two.send()
-    top.join()
-    two.join()
-    pair = merged([top, two])
+    pair = join_all([top, two])
     dmiddle, pair.sent = tie(dmiddle, pair.sent)
     pair.send()
     dmiddle, sent, held, gain_one = run_backward(
         1, chunk_widths[1], mesh_plan, like, kept[1], dmiddle, *back_shared, before[0]
     )
     dmiddle, sent, held, pair.others = tie(dmiddle, sent, held, pair.others)
-    one = Scatter(sent, held, scatter_steps)
+    one = Scatter((sent,), held, scatter_steps, device)
     one.send()
     pair.join()
     one.join()
@@ -1170,16 +1242,17 @@
         0, chunk_widths[0], mesh_plan, like, kept[0], dmiddle, *back_shared, latent_rows
     )
     sent, held, pair.others, one.others = tie(sent, held, pair.others, one.others)
-    zero = Scatter(sent, held, scatter_steps)
+    zero = Scatter((sent,), held, scatter_steps, device)
     zero.send()
     one.join()
     one.send()
-    pair.join()
+    while pair.at < one.at:
+        pair.join()
+        pair.send()
     zero.join()
     one.others = behind(one.others, zero.sent)
     zero.send()
-    one.join()
-    early = merged([pair, one])
+    early = join_all([pair, one])
     while early.at < count:
         early.send()
         zero.others = behind(zero.others, early.sent)

time: 215 us -> 251 us (1.17)
  Pallas kernels: 86.5 us -> 130 us
  other arithmetic: 14.6 us -> 2.06 us
  local copies, waits for them, and re-layouts: 24.9 us -> 36.5 us
  waiting for transfers between devices: 31.2 us -> 28 us
  starting transfers between devices: 55.4 us -> 52.2 us
    pallas_call x0 -> x19, Pallas kernels: none -> 38.2 us  [the longest x10 21.7 us: run_scatter_join(): pl.pallas_call(functools.partial(scatter_kernel, step, [len(chunk.others)...]
    unnamed x104 -> x140, local copies, waits for them, and re-layouts: 23.2 us -> 36.5 us
    add x10 -> x0, other arithmetic: 4.82 us -> none  [join(): summed = summed + other.astype(jnp.float32)]
    select_n x11 -> x0, other arithmetic: 4.77 us -> none  [the longest x9 4.74 us: join(): jnp.where(upper, pieces[place ^ 1 << at], pieces[place])]
    ppermute x44 -> x43, starting transfers between devices: 55.4 us -> 52.2 us  [swap(): lax.ppermute(value, ('dp', 'fsdp'), [(place, place ^ mask) for place in r...]
    ppermute x44 -> x43, waiting for transfers between devices: 31.2 us -> 28 us  [swap(): lax.ppermute(value, ('dp', 'fsdp'), [(place, place ^ mask) for place in r...]
    pallas_call x3, Pallas kernels: 31.8 us -> 34.6 us  [run_forward(): pl.pallas_call(functools.partial(forward_kernel, layer, widths, mesh_plan...]
  transfers between devices with their start and end apart: 44 -> 43, of which waited for: 18 -> 15; matrix products, arithmetic and copies ran while one was open for 4% -> 0% of each run, Pallas kernels for 28% -> 34%
where the time goes in v1:
time: 251 us; the launch traced here: 250 us
  Pallas kernels  130 us (52%)
  starting transfers between devices  52.2 us (21%)
  local copies, waits for them, and re-layouts  36.5 us (15%)
  waiting for transfers between devices  28 us (11%)
    ppermute x43, starting transfers between devices, swap(): lax.ppermute(value, ('dp', 'fsdp'), [(place, place ^ mask) for place in r...  52.2 us
    pallas_call x3, Pallas kernels, run_backward(): pl.pallas_call(functools.partial(backward_kernel, layer, widths, mesh_pla...  37.9 us
    unnamed x140, local copies, waits for them, and re-layouts  36.5 us
    pallas_call x3, Pallas kernels, run_forward(): pl.pallas_call(functools.partial(forward_kernel, layer, widths, mesh_plan...  34.6 us
    ppermute x43, waiting for transfers between devices, swap(): lax.ppermute(value, ('dp', 'fsdp'), [(place, place ^ mask) for place in r...  28 us
    pallas_call x10, Pallas kernels, run_scatter_join(): pl.pallas_call(functools.partial(scatter_kernel, step, [len(chunk.others)...  21.7 us
    pallas_call x9, Pallas kernels, run_gather_join(): pl.pallas_call(functools.partial(gather_kernel, step), in_specs=[smem_spe...  16.5 us
    pallas_call x1, Pallas kernels, run_top(): pl.pallas_call(functools.partial(top_kernel, widths, gather_plan, mesh_pl...  8.87 us
  transfers between devices with their start and end apart: 43, of which 15 were waited for; matrix products, arithmetic and copies ran while one was open for 0% of the time, Pallas kernels for 34%

profile of v1, /device:TPU:0, one launch (start us, length us, event | category | flops | bytes accessed | tf_op | source)
XLA Modules:
  0.0 250.2 jit_solution(6853934870868877047)
XLA Ops:
  0.7 1.8 pack.1
  2.5 4.0 %collective-permute-start.1 = (bf16[1,64,384]{2,1,0:T(8,128)(2,1)}, bf16[1,64,384]{2,1,0:T(8,128)(2,1)S(1)}, u32[]{:S(2)}, u32[]{:S(2)}) collective-permute-start(bf16[1,64,384]{2,1,0:T(8,128)(2,1)} %bitcast.46), channel_id=1, source_target_pairs={{0,16},{1,17},{2,18},{3,19},{4,20},{5,21},{6,22},{7,23},{8,24},{9,... | collective-permute-start | bytes 147464 | tf_op jit(solution)/shard_map/ppermute | solution.py:959
  6.6 2.9 %collective-permute-start.4 = (bf16[1,64,768]{2,1,0:T(8,128)(2,1)}, bf16[1,64,768]{2,1,0:T(8,128)(2,1)S(1)}, u32[]{:S(2)}, u32[]{:S(2)}) collective-permute-start(bf16[1,64,768]{2,1,0:T(8,128)(2,1)} %bitcast.44), channel_id=1, source_target_pairs={{0,16},{1,17},{2,18},{3,19},{4,20},{5,21},{6,22},{7,23},{8,24},{9,... | collective-permute-start | bytes 294920 | tf_op jit(solution)/shard_map/ppermute | solution.py:959
  9.5 5.0 %collective-permute-done.refs_1_ = bf16[1,64,256]{2,1,0:T(8,128)(2,1)S(1)} collective-permute-done((bf16[1,64,256]{2,1,0:T(8,128)(2,1)}, bf16[1,64,256]{2,1,0:T(8,128)(2,1)S(1)}, u32[]{:S(2)}, u32[]{:S(2)}) %collective-permute-start) | collective-permute-done | bytes 32800 | tf_op jit(solution)/shard_map/ppermute | solution.py:959
  18.0 2.0 collective-permute-start.2
  20.0 2.4 collective-permute-done.2.refs_1_
  23.1 1.6 gather_join.11.refs_0_
  24.7 1.6 gather_join.12.refs_0_
  26.3 1.6 gather_join.13.refs_0_
  28.0 2.4 collective-permute-start.7
  31.0 2.0 collective-permute-start.11
  35.5 1.5 collective-permute-start.8
  38.8 5.1 %collective-permute-done.5.refs_1_ = bf16[4,64,256]{2,1,0:T(8,128)(2,1)S(1)} collective-permute-done((bf16[4,64,256]{2,1,0:T(8,128)(2,1)}, bf16[4,64,256]{2,1,0:T(8,128)(2,1)S(1)}, u32[]{:S(2)}, u32[]{:S(2)}) %collective-permute-start.5) | collective-permute-done | bytes 131104 | tf_op jit(solution)/shard_map/ppermute | solution.py:959
  44.5 2.0 gather_join.14.own_ref
  46.5 2.2 gather_join.15.own_ref
  49.2 1.8 gather_join.16.refs_0_
  51.0 2.4 collective-permute-start.16
  54.5 9.9 %forward_part.3 = (f32[1536,256]{1,0:T(8,128)S(1)}, f32[1536,256]{1,0:T(8,128)S(1)}, bf16[1536,768]{1,0:T(8,128)(2,1)S(1)}, bf16[1536,256]{1,0:T(8,128)(2,1)S(1)...) custom-call(s32[16,32,96]{2,1,0:T(8,128)S(1)} %bitcast.29, bf16[16,64,256]{2,1,0:T(8,128)(2,1)S(1)} %copy-done.6, ...), custom_call_target="tpu_custom_call" | custom-call | flops 2415919104 | bytes 9437184 | tf_op jit(solution)/shard_map/forward_part/pallas_call | solution.py:378
  69.9 1.8 collective-permute-done.15.refs_2_
  72.6 2.8 %gather_join.17.own_ref = bf16[16,64,768]{2,1,0:T(8,128)(2,1)} custom-call(s32[1]{0:T(128)} %bitcast.device_ref.core_ref.refs_7_, bf16[4,64,768]{2,1,0:T(8,128)(2,1)} %gather_join.16.refs_0_, bf16[4,64,768]{2,1,0:T(8,128)(2,1)} %copy-done.46, bf16[4,64,768]{2,1,0:T(8,128)(2,1)} %copy-done.45, bf16[4,64,768]{2,1,0:T(8,128)(2,1)} %copy-done.44), custom_call_target="tpu_custom_call" | custom-call | tf_op jit(solution)/shard_map/gather_join/pallas_call | solution.py:1001
  75.4 1.5 copy-done.19
  76.9 12.8 %forward_part.4 = (f32[1536,256]{1,0:T(8,128)S(1)}, f32[1536,256]{1,0:T(8,128)S(1)}, bf16[1536,768]{1,0:T(8,128)(2,1)S(1)}, bf16[1536,256]{1,0:T(8,128)(2,1)S(1)...) custom-call(f32[1536,256]{1,0:T(8,128)S(1)} %copy-done.19, ...), custom_call_target="tpu_custom_call" | custom-call | flops 2415919104 | bytes 9437184 | tf_op jit(solution)/shard_map/forward_part/pallas_call | solution.py:378
  89.8 12.0 %forward_part.5 = (f32[1536,256]{1,0:T(8,128)S(1)}, f32[768,256]{1,0:T(8,128)S(1)}, bf16[1536,768]{1,0:T(8,128)(2,1)S(1)}, bf16[768,256]{1,0:T(8,128)(2,1)S(1)},...) custom-call(f32[1536,256]{1,0:T(8,128)S(1)} %get-tuple-element.212.s, ...), custom_call_target="tpu_custom_call" | custom-call | flops 2415919104 | bytes 9437184 | tf_op jit(solution)/shard_map/forward_part/pallas_call | solution.py:378
  101.8 8.9 %loss_part.1 = (f32[768,256]{1,0:T(8,128)S(1)}, bf16[16,64,384]{2,1,0:T(8,128)(2,1)S(1)}, f32[16,64,384]{2,1,0:T(8,128)S(1)}, f32[2,256]{1,0:T(2,128)S(1)}, f32[1,1]{1,0:T(1,128)}, /*index=5*/f32[1,1]{1,0:T(1,128)}) custom-call(f32[768,256]{1,0:T(8,128)S(1)} %get-tuple-element.214.middle_ref, bf16[16,64,768]{2,1,0:T(8,128)(2,1)S(1)} %copy-done.3, ...), custom_call_target="tpu_custom_call" | custom-call | flops 3623878656 | bytes 9437184 | tf_op jit(solution)/shard_map/loss_part/pallas_call | solution.py:505
  112.4 12.8 %backward_part.3 = (f32[1536,256]{1,0:T(8,128)S(1)}, bf16[16,64,384]{2,1,0:T(8,128)(2,1)S(1)}, f32[16,64,384]{2,1,0:T(8,128)S(1)}, f32[2,256]{1,0:T(2,128)S(1)}) custom-call(f32[1536,256]{1,0:T(8,128)S(1)} %get-tuple-element.216.refs_0_, bf16[1536,768]{1,0:T(8,128)(2,1)S(1)} %get-tuple-element.217.refs_1_, bf16[768,256]{1,0:T(8,128)(2,1)S(1)} %get-tuple-element.218.refs_2_, ...), custom_call_target="tpu_custom_call" | custom-call | flops 7247757312 | bytes 14155776 | tf_op jit(solution)/shard_map/backward_part/pallas_call | solution.py:656
  128.7 1.9 collective-permute-done.19.refs_3_
  131.5 3.9 %scatter_join.10 = (f32[4,64,768]{2,1,0:T(8,128)}, bf16[4,64,768]{2,1,0:T(8,128)(2,1)}, bf16[4,64,768]{2,1,0:T(8,128)(2,1)}, bf16[4,64,768]{2,1,0:T(8,128)(2,1)}) custom-call(s32[1]{0:T(128)} %bitcast.device_ref.core_ref.refs_7_, f32[16,64,384]{2,1,0:T(8,128)} %copy-done, bf16[16,64,384]{2,1,0:T(8,128)(2,1)} %copy-done.37, f32[16,64,384]{2,1,0:T(8,128)} %copy-done.1, ...), custom_call_target="tpu_custom_call" | custom-call | tf_op jit(solution)/shard_map/scatter_join/pallas_call | solution.py:1038
  138.9 1.7 copy-done.17
  144.8 14.5 %backward_part.4 = (f32[1536,256]{1,0:T(8,128)S(1)}, bf16[16,64,384]{2,1,0:T(8,128)(2,1)S(1)}, f32[16,64,384]{2,1,0:T(8,128)S(1)}, f32[2,256]{1,0:T(2,128)S(1)}) custom-call(f32[1536,256]{1,0:T(8,128)S(1)} %copy-done.22, bf16[1536,768]{1,0:T(8,128)(2,1)S(1)} %copy-done.17, bf16[1536,256]{1,0:T(8,128)(2,1)S(1)} %copy-done.28, ...), custom_call_target="tpu_custom_call" | custom-call | flops 7247757312 | bytes 14155776 | tf_op jit(solution)/shard_map/backward_part/pallas_call | solution.py:656
  163.3 2.4 scatter_join.11
  166.6 2.7 %scatter_join.12 = (f32[4,64,384]{2,1,0:T(8,128)}, bf16[4,64,384]{2,1,0:T(8,128)(2,1)}, bf16[4,64,384]{2,1,0:T(8,128)(2,1)}, bf16[4,64,384]{2,1,0:T(8,128)(2,1)}) custom-call(s32[1]{0:T(128)} %bitcast.device_ref.core_ref.refs_7_, f32[16,64,384]{2,1,0:T(8,128)} %copy-done.2, bf16[16,64,384]{2,1,0:T(8,128)(2,1)} %copy-done.38), custom_call_target="tpu_custom_call" | custom-call | tf_op jit(solution)/shard_map/scatter_join/pallas_call | solution.py:1038
  173.9 1.7 copy-done.24
  178.3 10.6 %backward_part.5 = (bf16[16,64,256]{2,1,0:T(8,128)(2,1)S(1)}, f32[16,64,256]{2,1,0:T(8,128)S(1)}, f32[2,256]{1,0:T(2,128)S(1)}) custom-call(f32[1536,256]{1,0:T(8,128)S(1)} %copy-done.26, bf16[1536,768]{1,0:T(8,128)(2,1)S(1)} %copy-done.24, bf16[1536,256]{1,0:T(8,128)(2,1)S(1)} %copy-done.34, bf16[16,2,96,384]{3,2,1,0:T(8,128)(2,1)} %get-tuple-element.259.refs_3_, ...), custom_call_target="tpu_custom_call" | custom-call | flops 4831838208 | bytes 12582912 | tf_op jit(solution)/shard_map/backward_part/pallas_call | solution.py:656
  191.4 2.0 scatter_join.13
  195.0 2.2 scatter_join.14
  201.4 2.0 scatter_join.15
  203.4 4.4 %collective-permute-start.30 = (bf16[1,64,1152]{2,1,0:T(8,128)(2,1)}, bf16[1,64,1152]{2,1,0:T(8,128)(2,1)S(1)}, u32[]{:S(2)}, u32[]{:S(2)}) collective-permute-start(bf16[1,64,1152]{2,1,0:T(8,128)(2,1)} %get-tuple-element.289), channel_id=1, source_target_pairs={{0,16},{1,17},{2,18},{3,19},{4,20},{5,21},{6,22},{7,23},{8,24},{9,... | collective-permute-start | bytes 442376 | tf_op jit(solution)/shard_map/ppermute | solution.py:959
  208.5 1.8 scatter_join.17
  211.6 3.3 %collective-permute-done.34.refs_1_ = bf16[2,64,256]{2,1,0:T(8,128)(2,1)S(1)} collective-permute-done((bf16[2,64,256]{2,1,0:T(8,128)(2,1)}, bf16[2,64,256]{2,1,0:T(8,128)(2,1)S(1)}, u32[]{:S(2)}, u32[]{:S(2)}) %collective-permute-start.34) | collective-permute-done | bytes 65568 | tf_op jit(solution)/shard_map/ppermute | solution.py:959
  215.5 1.6 scatter_join.18
  217.1 3.1 %collective-permute-start.35 = (bf16[1,64,256]{2,1,0:T(8,128)(2,1)}, bf16[1,64,256]{2,1,0:T(8,128)(2,1)S(1)}, u32[]{:S(2)}, u32[]{:S(2)}) collective-permute-start(bf16[1,64,256]{2,1,0:T(8,128)(2,1)} %get-tuple-element.302), channel_id=1, source_target_pairs={{0,16},{1,17},{2,18},{3,19},{4,20},{5,21},{6,22},{7,23},{8,24},{9,... | collective-permute-start | bytes 98312 | tf_op jit(solution)/shard_map/ppermute | solution.py:959
  220.8 1.7 scatter_join.16
  222.6 3.6 %early_statistics.1.early_ref = f32[48,128]{1,0:T(8,128)} custom-call(f32[64,1152]{1,0:T(8,128)} %bitcast.31, f32[3,64,96]{2,1,0:T(8,128)} %refs_3_.3, f32[3,32,64]{2,1,0:T(8,128)} %bitcast.39, f32[3,64,128]{2,1,0:T(8,128)} %refs_5_.3, f32[3,64,128]{2,1,0:T(8,128)} %bitcast.34, f32[64,128]{1,0:T(8,128)} %bitcast.42, f32[64,128]{1,0:T(8,128)} %refs_8_.3, ...), custom_call_target="tpu_custom_call" | custom-call | tf_op jit(solution)/shard_map/early_statistics/pallas_call | solution.py:829
  228.3 1.7 late_statistics.1
  232.1 1.9 collective-permute-start.39
  240.1 2.0 collective-permute-start.41
  242.1 1.7 collective-permute-start.40
  246.5 3.5 %update.1 = (f32[1,1]{1,0:T(1,128)}, f32[1,1]{1,0:T(1,128)}, f32[1,1]{1,0:T(1,128)}, f32[64,128]{1,0:T(8,128)}, f32[64,128]{1,0:T(8,128)}, /*index=5*/f32[1,128]...) custom-call(f32[48,128]{1,0:T(8,128)} %pad_maximum_fusion.refs_0_, ...), custom_call_target="tpu_custom_call" | custom-call | tf_op jit(solution)/shard_map/update/pallas_call | solution.py:948
  (214 shorter events, 68.3 us)
Async XLA Ops:
  2.5 12.0 %collective-permute-start.1 = (bf16[1,64,384]{2,1,0:T(8,128)(2,1)}, bf16[1,64,384]{2,1,0:T(8,128)(2,1)S(1)}, u32[]{:S(2)}, u32[]{:S(2)}) collective-permute-start(bf16[1,64,384]{2,1,0:T(8,128)(2,1)} %bitcast.46), channel_id=1, source_target_pairs={{0,16},{1,17},{2,18},{3,19},{4,20},{5,21},{6,22},{7,23},{8,24},{9,... | collective-permute-start | bytes 147464 | tf_op jit(solution)/shard_map/ppermute | solution.py:959
  6.6 7.9 %collective-permute-start = (bf16[1,64,256]{2,1,0:T(8,128)(2,1)}, bf16[1,64,256]{2,1,0:T(8,128)(2,1)S(1)}, u32[]{:S(2)}, u32[]{:S(2)}) collective-permute-start(bf16[1,64,256]{2,1,0:T(8,128)(2,1)} %bitcast.48), channel_id=1, source_target_pairs={{0,16},{1,17},{2,18},{3,19},{4,20},{5,21},{6,22},{7,23},{8,24},{9,... | collective-permute-start | bytes 98312 | tf_op jit(solution)/shard_map/ppermute | solution.py:959
  6.6 13.4 %collective-permute-start.4 = (bf16[1,64,768]{2,1,0:T(8,128)(2,1)}, bf16[1,64,768]{2,1,0:T(8,128)(2,1)S(1)}, u32[]{:S(2)}, u32[]{:S(2)}) collective-permute-start(bf16[1,64,768]{2,1,0:T(8,128)(2,1)} %bitcast.44), channel_id=1, source_target_pairs={{0,16},{1,17},{2,18},{3,19},{4,20},{5,21},{6,22},{7,23},{8,24},{9,... | collective-permute-start | bytes 294920 | tf_op jit(solution)/shard_map/ppermute | solution.py:959
  16.6 5.9 %collective-permute-start.3 = (bf16[2,64,384]{2,1,0:T(8,128)(2,1)}, bf16[2,64,384]{2,1,0:T(8,128)(2,1)S(1)}, u32[]{:S(2)}, u32[]{:S(2)}) collective-permute-start(bf16[2,64,384]{2,1,0:T(8,128)(2,1)} %gather_join.10.refs_0_), channel_id=1, source_target_pairs={{0,8},{1,9},{2,10},{3,11},{4,12},{5,13},{6,14},{7,15},{8,0},{9,1},... | collective-permute-start | bytes 294920 | tf_op jit(solution)/shard_map/ppermute | solution.py:959
  18.0 4.5 %collective-permute-start.2 = (bf16[2,64,256]{2,1,0:T(8,128)(2,1)}, bf16[2,64,256]{2,1,0:T(8,128)(2,1)S(1)}, u32[]{:S(2)}, u32[]{:S(2)}) collective-permute-start(bf16[2,64,256]{2,1,0:T(8,128)(2,1)} %gather_join.9.refs_0_), channel_id=1, source_target_pairs={{0,8},{1,9},{2,10},{3,11},{4,12},{5,13},{6,14},{7,15},{8,0},{9,1},... | collective-permute-start | bytes 196616 | tf_op jit(solution)/shard_map/ppermute | solution.py:959
  28.0 26.5 %copy-start.7 = (f32[7,256]{1,0:T(8,128)S(1)}, f32[7,256]{1,0:T(8,128)}, u32[]{:S(2)}) copy-start(f32[7,256]{1,0:T(8,128)} %refs_21_.1) | copy-start | bytes 21508
  28.0 26.5 %copy-start.13 = (s32[16,96,32]{1,2,0:T(8,128)S(1)}, s32[16,96,32]{1,2,0:T(8,128)}, u32[]{:S(2)}) copy-start(s32[16,96,32]{1,2,0:T(8,128)} %param.24) | copy-start | bytes 589828
  28.0 26.5 %copy-start.14 = (s32[16]{0:T(128)S(1)}, s32[16]{0:T(128)}, u32[]{:S(2)}) copy-start(s32[16]{0:T(128)} %valid_ref.5) | copy-start | bytes 196
  28.0 7.5 %collective-permute-start.7 = (bf16[4,64,256]{2,1,0:T(8,128)(2,1)}, bf16[4,64,256]{2,1,0:T(8,128)(2,1)S(1)}, u32[]{:S(2)}, u32[]{:S(2)}) collective-permute-start(bf16[4,64,256]{2,1,0:T(8,128)(2,1)} %gather_join.11.refs_0_), channel_id=1, source_target_pairs={{0,6},{1,7},{2,4},{3,5},{4,2},{5,3},{6,0},{7,1},{8,14},{9,15},{10,... | collective-permute-start | bytes 393224 | tf_op jit(solution)/shard_map/ppermute | solution.py:959
  30.4 7.9 %collective-permute-start.6 = (bf16[4,64,256]{2,1,0:T(8,128)(2,1)}, bf16[4,64,256]{2,1,0:T(8,128)(2,1)S(1)}, u32[]{:S(2)}, u32[]{:S(2)}) collective-permute-start(bf16[4,64,256]{2,1,0:T(8,128)(2,1)} %gather_join.11.refs_0_), channel_id=1, source_target_pairs={{0,4},{1,5},{2,6},{3,7},{4,0},{5,1},{6,2},{7,3},{8,12},{9,13},{10,... | collective-permute-start | bytes 393224 | tf_op jit(solution)/shard_map/ppermute | solution.py:959
  31.0 12.9 %collective-permute-start.11 = (bf16[2,64,768]{2,1,0:T(8,128)(2,1)}, bf16[2,64,768]{2,1,0:T(8,128)(2,1)S(1)}, u32[]{:S(2)}, u32[]{:S(2)}) collective-permute-start(bf16[2,64,768]{2,1,0:T(8,128)(2,1)} %gather_join.13.refs_0_), channel_id=1, source_target_pairs={{0,8},{1,9},{2,10},{3,11},{4,12},{5,13},{6,14},{7,15},{8,0},{9,1},... | collective-permute-start | bytes 589832 | tf_op jit(solution)/shard_map/ppermute | solution.py:959
  33.0 10.9 %collective-permute-start.10 = (bf16[4,64,384]{2,1,0:T(8,128)(2,1)}, bf16[4,64,384]{2,1,0:T(8,128)(2,1)S(1)}, u32[]{:S(2)}, u32[]{:S(2)}) collective-permute-start(bf16[4,64,384]{2,1,0:T(8,128)(2,1)} %gather_join.12.refs_0_), channel_id=1, source_target_pairs={{0,6},{1,7},{2,4},{3,5},{4,2},{5,3},{6,0},{7,1},{8,14},{9,15},{10,... | collective-permute-start | bytes 589832 | tf_op jit(solution)/shard_map/ppermute | solution.py:959
  34.4 9.5 %collective-permute-start.9 = (bf16[4,64,384]{2,1,0:T(8,128)(2,1)}, bf16[4,64,384]{2,1,0:T(8,128)(2,1)S(1)}, u32[]{:S(2)}, u32[]{:S(2)}) collective-permute-start(bf16[4,64,384]{2,1,0:T(8,128)(2,1)} %gather_join.12.refs_0_), channel_id=1, source_target_pairs={{0,4},{1,5},{2,6},{3,7},{4,0},{5,1},{6,2},{7,3},{8,12},{9,13},{10,... | collective-permute-start | bytes 589832 | tf_op jit(solution)/shard_map/ppermute | solution.py:959
  35.5 8.4 %collective-permute-start.8 = (bf16[4,64,384]{2,1,0:T(8,128)(2,1)}, bf16[4,64,384]{2,1,0:T(8,128)(2,1)S(1)}, u32[]{:S(2)}, u32[]{:S(2)}) collective-permute-start(bf16[4,64,384]{2,1,0:T(8,128)(2,1)} %gather_join.12.refs_0_), channel_id=1, source_target_pairs={{0,2},{1,3},{2,0},{3,1},{4,6},{5,7},{6,4},{7,5},{8,10},{9,11},{10,... | collective-permute-start | bytes 589832 | tf_op jit(solution)/shard_map/ppermute | solution.py:959
  38.3 5.6 %collective-permute-start.5 = (bf16[4,64,256]{2,1,0:T(8,128)(2,1)}, bf16[4,64,256]{2,1,0:T(8,128)(2,1)S(1)}, u32[]{:S(2)}, u32[]{:S(2)}) collective-permute-start(bf16[4,64,256]{2,1,0:T(8,128)(2,1)} %gather_join.11.refs_0_), channel_id=1, source_target_pairs={{0,2},{1,3},{2,0},{3,1},{4,6},{5,7},{6,4},{7,5},{8,10},{9,11},{10,... | collective-permute-start | bytes 393224 | tf_op jit(solution)/shard_map/ppermute | solution.py:959
  46.5 2.3 collective-permute-start.12
  48.8 23.0 %collective-permute-start.13 = (bf16[16,64,384]{2,1,0:T(8,128)(2,1)}, bf16[16,64,384]{2,1,0:T(8,128)(2,1)S(1)}, u32[]{:S(2)}, u32[]{:S(2)}) collective-permute-start(bf16[16,64,384]{2,1,0:T(8,128)(2,1)} %gather_join.15.own_ref), channel_id=1, source_target_pairs={{0,1},{1,0},{2,3},{3,2},{4,5},{5,4},{6,7},{7,6},{8,9},{9,8},{10,11... | collective-permute-start | bytes 2359304 | tf_op jit(solution)/shard_map/ppermute | solution.py:959
  51.0 18.9 %collective-permute-start.16 = (bf16[4,64,768]{2,1,0:T(8,128)(2,1)}, bf16[4,64,768]{2,1,0:T(8,128)(2,1)S(1)}, u32[]{:S(2)}, u32[]{:S(2)}) collective-permute-start(bf16[4,64,768]{2,1,0:T(8,128)(2,1)} %gather_join.16.refs_0_), channel_id=1, source_target_pairs={{0,6},{1,7},{2,4},{3,5},{4,2},{5,3},{6,0},{7,1},{8,14},{9,15},{10,... | collective-permute-start | bytes 1179656 | tf_op jit(solution)/shard_map/ppermute | solution.py:959
  53.5 18.3 %collective-permute-start.15 = (bf16[4,64,768]{2,1,0:T(8,128)(2,1)}, bf16[4,64,768]{2,1,0:T(8,128)(2,1)S(1)}, u32[]{:S(2)}, u32[]{:S(2)}) collective-permute-start(bf16[4,64,768]{2,1,0:T(8,128)(2,1)} %gather_join.16.refs_0_), channel_id=1, source_target_pairs={{0,4},{1,5},{2,6},{3,7},{4,0},{5,1},{6,2},{7,3},{8,12},{9,13},{10,... | collective-permute-start | bytes 1179656 | tf_op jit(solution)/shard_map/ppermute | solution.py:959
  54.0 17.7 %collective-permute-start.14 = (bf16[4,64,768]{2,1,0:T(8,128)(2,1)}, bf16[4,64,768]{2,1,0:T(8,128)(2,1)S(1)}, u32[]{:S(2)}, u32[]{:S(2)}) collective-permute-start(bf16[4,64,768]{2,1,0:T(8,128)(2,1)} %gather_join.16.refs_0_), channel_id=1, source_target_pairs={{0,2},{1,3},{2,0},{3,1},{4,6},{5,7},{6,4},{7,5},{8,10},{9,11},{10,... | collective-permute-start | bytes 1179656 | tf_op jit(solution)/shard_map/ppermute | solution.py:959
  75.4 14.3 %copy-start.3 = (bf16[16,64,768]{2,1,0:T(8,128)(2,1)S(1)}, bf16[16,64,768]{2,1,0:T(8,128)(2,1)}, u32[]{:S(2)}) copy-start(bf16[16,64,768]{2,1,0:T(8,128)(2,1)} %gather_join.17.own_ref) | copy-start | bytes 4718596
  75.4 14.3 %collective-permute-start.17 = (bf16[16,64,768]{2,1,0:T(8,128)(2,1)}, bf16[16,64,768]{2,1,0:T(8,128)(2,1)S(1)}, u32[]{:S(2)}, u32[]{:S(2)}) collective-permute-start(bf16[16,64,768]{2,1,0:T(8,128)(2,1)} %gather_join.17.own_ref), channel_id=1, source_target_pairs={{0,1},{1,0},{2,3},{3,2},{4,5},{5,4},{6,7},{7,6},{8,9},{9,8},{10,11... | collective-permute-start | bytes 4718600 | tf_op jit(solution)/shard_map/ppermute | solution.py:959
  89.7 12.0 %copy-start.27 = (bf16[1536,256]{1,0:T(8,128)(2,1)}, bf16[1536,256]{1,0:T(8,128)(2,1)S(1)}, u32[]{:S(2)}) copy-start(bf16[1536,256]{1,0:T(8,128)(2,1)S(1)} %get-tuple-element.235.refs_2_) | copy-start | bytes 2359300
  111.9 16.3 %collective-permute-start.18 = (bf16[16,64,384]{2,1,0:T(8,128)(2,1)S(1)}, bf16[16,64,384]{2,1,0:T(8,128)(2,1)S(1)}, u32[]{:S(2)}, u32[]{:S(2)}) collective-permute-start(bf16[16,64,384]{2,1,0:T(8,128)(2,1)S(1)} %get-tuple-element.228), channel_id=1, source_target_pairs={{0,1},{1,0},{2,3},{3,2},{4,5},{5,4},{6,7},{7,6},{8,9},{9,8},{10,11... | collective-permute-start | bytes 2359304 | tf_op jit(solution)/shard_map/ppermute | solution.py:959
  128.2 2.4 collective-permute-start.19
  135.4 26.9 %collective-permute-start.20 = (bf16[4,64,768]{2,1,0:T(8,128)(2,1)}, bf16[4,64,768]{2,1,0:T(8,128)(2,1)S(1)}, u32[]{:S(2)}, u32[]{:S(2)}) collective-permute-start(bf16[4,64,768]{2,1,0:T(8,128)(2,1)} %get-tuple-element.249), channel_id=1, source_target_pairs={{0,2},{1,3},{2,0},{3,1},{4,6},{5,7},{6,4},{7,5},{8,10},{9,11},{10,... | collective-permute-start | bytes 1179656 | tf_op jit(solution)/shard_map/ppermute | solution.py:959
  136.7 25.6 %collective-permute-start.21 = (bf16[4,64,768]{2,1,0:T(8,128)(2,1)}, bf16[4,64,768]{2,1,0:T(8,128)(2,1)S(1)}, u32[]{:S(2)}, u32[]{:S(2)}) collective-permute-start(bf16[4,64,768]{2,1,0:T(8,128)(2,1)} %get-tuple-element.250), channel_id=1, source_target_pairs={{0,4},{1,5},{2,6},{3,7},{4,0},{5,1},{6,2},{7,3},{8,12},{9,13},{10,... | collective-permute-start | bytes 1179656 | tf_op jit(solution)/shard_map/ppermute | solution.py:959
  138.2 24.1 %collective-permute-start.22 = (bf16[4,64,768]{2,1,0:T(8,128)(2,1)}, bf16[4,64,768]{2,1,0:T(8,128)(2,1)S(1)}, u32[]{:S(2)}, u32[]{:S(2)}) collective-permute-start(bf16[4,64,768]{2,1,0:T(8,128)(2,1)} %get-tuple-element.251), channel_id=1, source_target_pairs={{0,6},{1,7},{2,4},{3,5},{4,2},{5,3},{6,0},{7,1},{8,14},{9,15},{10,... | collective-permute-start | bytes 1179656 | tf_op jit(solution)/shard_map/ppermute | solution.py:959
  162.3 3.4 %collective-permute-start.23 = (bf16[16,64,384]{2,1,0:T(8,128)(2,1)S(1)}, bf16[16,64,384]{2,1,0:T(8,128)(2,1)S(1)}, u32[]{:S(2)}, u32[]{:S(2)}) collective-permute-start(bf16[16,64,384]{2,1,0:T(8,128)(2,1)S(1)} %get-tuple-element.263), channel_id=1, source_target_pairs={{0,1},{1,0},{2,3},{3,2},{4,5},{5,4},{6,7},{7,6},{8,9},{9,8},{10,11... | collective-permute-start | bytes 2359304 | tf_op jit(solution)/shard_map/ppermute | solution.py:959
  169.2 21.3 %collective-permute-start.24 = (bf16[2,64,768]{2,1,0:T(8,128)(2,1)}, bf16[2,64,768]{2,1,0:T(8,128)(2,1)S(1)}, u32[]{:S(2)}, u32[]{:S(2)}) collective-permute-start(bf16[2,64,768]{2,1,0:T(8,128)(2,1)} %get-tuple-element.271), channel_id=1, source_target_pairs={{0,8},{1,9},{2,10},{3,11},{4,12},{5,13},{6,14},{7,15},{8,0},{9,1},... | collective-permute-start | bytes 589832 | tf_op jit(solution)/shard_map/ppermute | solution.py:959
  170.4 20.1 %collective-permute-start.25 = (bf16[4,64,384]{2,1,0:T(8,128)(2,1)}, bf16[4,64,384]{2,1,0:T(8,128)(2,1)S(1)}, u32[]{:S(2)}, u32[]{:S(2)}) collective-permute-start(bf16[4,64,384]{2,1,0:T(8,128)(2,1)} %get-tuple-element.272), channel_id=1, source_target_pairs={{0,2},{1,3},{2,0},{3,1},{4,6},{5,7},{6,4},{7,5},{8,10},{9,11},{10,... | collective-permute-start | bytes 589832 | tf_op jit(solution)/shard_map/ppermute | solution.py:959
  171.2 19.3 %collective-permute-start.26 = (bf16[4,64,384]{2,1,0:T(8,128)(2,1)}, bf16[4,64,384]{2,1,0:T(8,128)(2,1)S(1)}, u32[]{:S(2)}, u32[]{:S(2)}) collective-permute-start(bf16[4,64,384]{2,1,0:T(8,128)(2,1)} %get-tuple-element.273), channel_id=1, source_target_pairs={{0,4},{1,5},{2,6},{3,7},{4,0},{5,1},{6,2},{7,3},{8,12},{9,13},{10,... | collective-permute-start | bytes 589832 | tf_op jit(solution)/shard_map/ppermute | solution.py:959
  172.7 17.8 %collective-permute-start.27 = (bf16[4,64,384]{2,1,0:T(8,128)(2,1)}, bf16[4,64,384]{2,1,0:T(8,128)(2,1)S(1)}, u32[]{:S(2)}, u32[]{:S(2)}) collective-permute-start(bf16[4,64,384]{2,1,0:T(8,128)(2,1)} %get-tuple-element.274), channel_id=1, source_target_pairs={{0,6},{1,7},{2,4},{3,5},{4,2},{5,3},{6,0},{7,1},{8,14},{9,15},{10,... | collective-permute-start | bytes 589832 | tf_op jit(solution)/shard_map/ppermute | solution.py:959
  190.6 3.6 %collective-permute-start.29 = (bf16[16,64,256]{2,1,0:T(8,128)(2,1)S(1)}, bf16[16,64,256]{2,1,0:T(8,128)(2,1)S(1)}, u32[]{:S(2)}, u32[]{:S(2)}) collective-permute-start(bf16[16,64,256]{2,1,0:T(8,128)(2,1)S(1)} %get-tuple-element.283), channel_id=1, source_target_pairs={{0,1},{1,0},{2,3},{3,2},{4,5},{5,4},{6,7},{7,6},{8,9},{9,8},{10,11... | collective-permute-start | bytes 1572872 | tf_op jit(solution)/shard_map/ppermute | solution.py:959
  193.3 7.4 %collective-permute-start.28 = (bf16[2,64,384]{2,1,0:T(8,128)(2,1)}, bf16[2,64,384]{2,1,0:T(8,128)(2,1)S(1)}, u32[]{:S(2)}, u32[]{:S(2)}) collective-permute-start(bf16[2,64,384]{2,1,0:T(8,128)(2,1)} %get-tuple-element.281), channel_id=1, source_target_pairs={{0,8},{1,9},{2,10},{3,11},{4,12},{5,13},{6,14},{7,15},{8,0},{9,1},... | collective-permute-start | bytes 294920 | tf_op jit(solution)/shard_map/ppermute | solution.py:959
  197.2 10.5 %collective-permute-start.31 = (bf16[4,64,256]{2,1,0:T(8,128)(2,1)}, bf16[4,64,256]{2,1,0:T(8,128)(2,1)S(1)}, u32[]{:S(2)}, u32[]{:S(2)}) collective-permute-start(bf16[4,64,256]{2,1,0:T(8,128)(2,1)} %get-tuple-element.284), channel_id=1, source_target_pairs={{0,2},{1,3},{2,0},{3,1},{4,6},{5,7},{6,4},{7,5},{8,10},{9,11},{10,... | collective-permute-start | bytes 393224 | tf_op jit(solution)/shard_map/ppermute | solution.py:959
  198.5 9.2 %collective-permute-start.32 = (bf16[4,64,256]{2,1,0:T(8,128)(2,1)}, bf16[4,64,256]{2,1,0:T(8,128)(2,1)S(1)}, u32[]{:S(2)}, u32[]{:S(2)}) collective-permute-start(bf16[4,64,256]{2,1,0:T(8,128)(2,1)} %get-tuple-element.285), channel_id=1, source_target_pairs={{0,4},{1,5},{2,6},{3,7},{4,0},{5,1},{6,2},{7,3},{8,12},{9,13},{10,... | collective-permute-start | bytes 393224 | tf_op jit(solution)/shard_map/ppermute | solution.py:959
  200.0 7.7 %collective-permute-start.33 = (bf16[4,64,256]{2,1,0:T(8,128)(2,1)}, bf16[4,64,256]{2,1,0:T(8,128)(2,1)S(1)}, u32[]{:S(2)}, u32[]{:S(2)}) collective-permute-start(bf16[4,64,256]{2,1,0:T(8,128)(2,1)} %get-tuple-element.286), channel_id=1, source_target_pairs={{0,6},{1,7},{2,4},{3,5},{4,2},{5,3},{6,0},{7,1},{8,14},{9,15},{10,... | collective-permute-start | bytes 393224 | tf_op jit(solution)/shard_map/ppermute | solution.py:959
  203.4 16.8 %collective-permute-start.30 = (bf16[1,64,1152]{2,1,0:T(8,128)(2,1)}, bf16[1,64,1152]{2,1,0:T(8,128)(2,1)S(1)}, u32[]{:S(2)}, u32[]{:S(2)}) collective-permute-start(bf16[1,64,1152]{2,1,0:T(8,128)(2,1)} %get-tuple-element.289), channel_id=1, source_target_pairs={{0,16},{1,17},{2,18},{3,19},{4,20},{5,21},{6,22},{7,23},{8,24},{9,... | collective-permute-start | bytes 442376 | tf_op jit(solution)/shard_map/ppermute | solution.py:959
  210.3 4.6 %collective-permute-start.34 = (bf16[2,64,256]{2,1,0:T(8,128)(2,1)}, bf16[2,64,256]{2,1,0:T(8,128)(2,1)S(1)}, u32[]{:S(2)}, u32[]{:S(2)}) collective-permute-start(bf16[2,64,256]{2,1,0:T(8,128)(2,1)} %get-tuple-element.300), channel_id=1, source_target_pairs={{0,8},{1,9},{2,10},{3,11},{4,12},{5,13},{6,14},{7,15},{8,0},{9,1},... | collective-permute-start | bytes 196616 | tf_op jit(solution)/shard_map/ppermute | solution.py:959
  217.1 9.1 %collective-permute-start.35 = (bf16[1,64,256]{2,1,0:T(8,128)(2,1)}, bf16[1,64,256]{2,1,0:T(8,128)(2,1)S(1)}, u32[]{:S(2)}, u32[]{:S(2)}) collective-permute-start(bf16[1,64,256]{2,1,0:T(8,128)(2,1)} %get-tuple-element.302), channel_id=1, source_target_pairs={{0,16},{1,17},{2,18},{3,19},{4,20},{5,21},{6,22},{7,23},{8,24},{9,... | collective-permute-start | bytes 98312 | tf_op jit(solution)/shard_map/ppermute | solution.py:959
  229.9 1.4 collective-permute-start.36
  232.1 4.9 %collective-permute-start.39 = (f32[48,128]{1,0:T(8,128)S(1)}, f32[48,128]{1,0:T(8,128)S(1)}, u32[]{:S(2)}, u32[]{:S(2)}) collective-permute-start(f32[48,128]{1,0:T(8,128)S(1)} %pad_maximum_fusion.2), channel_id=1, source_target_pairs={{0,6},{1,7},{2,4},{3,5},{4,2},{5,3},{6,0},{7,1},{8,14},{9,15},{10,... | collective-permute-start | bytes 73736 | tf_op jit(solution)/shard_map/ppermute | solution.py:959
  234.0 3.8 %collective-permute-start.38 = (f32[48,128]{1,0:T(8,128)S(1)}, f32[48,128]{1,0:T(8,128)S(1)}, u32[]{:S(2)}, u32[]{:S(2)}) collective-permute-start(f32[48,128]{1,0:T(8,128)S(1)} %pad_maximum_fusion.2), channel_id=1, source_target_pairs={{0,2},{1,3},{2,0},{3,1},{4,6},{5,7},{6,4},{7,5},{8,10},{9,11},{10,... | collective-permute-start | bytes 73736 | tf_op jit(solution)/shard_map/ppermute | solution.py:959
  234.8 3.8 %collective-permute-start.37 = (f32[48,128]{1,0:T(8,128)S(1)}, f32[48,128]{1,0:T(8,128)S(1)}, u32[]{:S(2)}, u32[]{:S(2)}) collective-permute-start(f32[48,128]{1,0:T(8,128)S(1)} %pad_maximum_fusion.2), channel_id=1, source_target_pairs={{0,4},{1,5},{2,6},{3,7},{4,0},{5,1},{6,2},{7,3},{8,12},{9,13},{10,... | collective-permute-start | bytes 73736 | tf_op jit(solution)/shard_map/ppermute | solution.py:959
  239.3 5.8 %collective-permute-start.42 = (f32[48,128]{1,0:T(8,128)S(1)}, f32[48,128]{1,0:T(8,128)S(1)}, u32[]{:S(2)}, u32[]{:S(2)}) collective-permute-start(f32[48,128]{1,0:T(8,128)S(1)} %pad_maximum_fusion.1), channel_id=1, source_target_pairs={{0,24},{1,25},{2,26},{3,27},{4,28},{5,29},{6,30},{7,31},{8,16},{9,... | collective-permute-start | bytes 73736 | tf_op jit(solution)/shard_map/ppermute | solution.py:959
  240.1 5.3 %collective-permute-start.41 = (f32[48,128]{1,0:T(8,128)S(1)}, f32[48,128]{1,0:T(8,128)S(1)}, u32[]{:S(2)}, u32[]{:S(2)}) collective-permute-start(f32[48,128]{1,0:T(8,128)S(1)} %pad_maximum_fusion.1), channel_id=1, source_target_pairs={{0,16},{1,17},{2,18},{3,19},{4,20},{5,21},{6,22},{7,23},{8,24},{9,... | collective-permute-start | bytes 73736 | tf_op jit(solution)/shard_map/ppermute | solution.py:959
  242.1 3.8 %collective-permute-start.40 = (f32[48,128]{1,0:T(8,128)S(1)}, f32[48,128]{1,0:T(8,128)S(1)}, u32[]{:S(2)}, u32[]{:S(2)}) collective-permute-start(f32[48,128]{1,0:T(8,128)S(1)} %pad_maximum_fusion.1), channel_id=1, source_target_pairs={{0,8},{1,9},{2,10},{3,11},{4,12},{5,13},{6,14},{7,15},{8,0},{9,1},... | collective-permute-start | bytes 73736 | tf_op jit(solution)/shard_map/ppermute | solution.py:959
  (65 other events, 176.9 us)

commit v2 on v0

--- a/solution.py
+++ b/solution.py
@@ -22,6 +22,7 @@
 ROWS = GROUP * CTX
 HALF = D // 2
 VMEM_BYTES = 24 * 1024 * 1024
+MIDDLE_BYTES = 46 * 1024 * 1024
 
 decay_two = 0.9
 step_rate = 0.3
@@ -132,7 +133,7 @@
                 at += width
 
 
-def write_blocks(send_ref, keep_ref, sum_ref, core, widths, mesh_plan):
+def write_blocks(send_ref, keep_ref, sum_ref, core, widths, mesh_plan, start=0):
     outer_count, inner_count, steps = mesh_plan
     rows = keep_ref.shape[1]
     for high in range(inner_count // 2):
@@ -144,7 +145,8 @@
                 for width in widths:
                     block.append(taken[:, column + outer * width : column + (outer + 1) * width])
                     column += width * outer_count
-                target[block_place(outer * inner_count + 2 * high, steps)] = jnp.concatenate(
+                place = block_place(outer * inner_count + 2 * high, steps)
+                target[place, :, start : start + sum(widths)] = jnp.concatenate(
                     block, axis=1
                 ).astype(target.dtype)
 
@@ -308,6 +310,10 @@
     return pl.BlockSpec(shape, lambda step: (0,) * len(shape))
 
 
+def in_hbm(item):
+    return pltpu.with_memory_space_constraint(item, pltpu.HBM)
+
+
 def smem_spec():
     return pl.BlockSpec(memory_space=pltpu.SMEM)
 
@@ -346,26 +352,25 @@
 
 def run_forward(layer, widths, mesh_plan, source, own, other, gains, valid, core):
     tokens = valid.shape[0] * CTX
-    queries = SEG if layer == LAYERS - 1 else CTX
     f32, b16 = jnp.float32, jnp.bfloat16
-    shape = jax.ShapeDtypeStruct
-    short = tokens // CTX * queries
+    chances = HEADS // 2 * CTX
     outs = [
-        (shape((tokens, D), f32), row_spec(D)),
-        (shape((short, D), f32), row_spec(D, GROUP * queries)),
-        (shape((tokens, 3 * D), b16), row_spec(3 * D)),
-        (shape((short, D), b16), row_spec(D, GROUP * queries)),
-        (shape((tokens // CTX, 2, CTX, HEADS // 2 * queries), b16), chance_spec(queries)),
-        (shape((D, 4 * D), b16), whole_spec((D, 4 * D))),
+        (pltpu.HBM((tokens, D), f32), row_spec(D)),
+        (pltpu.HBM((tokens, D), f32), row_spec(D)),
+        (pltpu.HBM((tokens, 3 * D), b16), row_spec(3 * D)),
+        (pltpu.HBM((tokens, D), b16), row_spec(D)),
+        (pltpu.HBM((tokens // CTX, 2, CTX, chances), b16), chance_spec(CTX)),
+        (pltpu.HBM((D, 4 * D), b16), whole_spec((D, 4 * D))),
     ]
-    scratch = [pltpu.VMEM((2, CTX, HEADS // 2 * queries), f32)]
+    scratch = [pltpu.VMEM((2, CTX, chances), f32)]
     if layer == 0:
         scratch = [pltpu.VMEM((D, VOCAB), b16)] + scratch + [pltpu.VMEM((ROWS, VOCAB), b16)]
         source_spec = latent_spec()
     else:
         source_spec = row_spec(D)
-        outs.append((shape((D, 2 * FF), b16), whole_spec((D, 2 * FF))))
-        outs = outs + [(shape((tokens, FF), b16), row_spec(FF))] * 2
+        outs.append((pltpu.HBM((D, 2 * FF), b16), whole_spec((D, 2 * FF))))
+        outs = outs + [(pltpu.HBM((tokens, FF), b16), row_spec(FF))] * 2
+        source = in_hbm(source)
     return pl.pallas_call(
         functools.partial(forward_kernel, layer, widths, mesh_plan),
         grid=(tokens // ROWS,),
@@ -390,23 +395,74 @@
     )(source, own, other, gains, valid, core)
 
 
-def top_kernel(widths, gather_plan, mesh_plan, start, middle_ref, own_ref, other_ref, drawn_ref, gains_ref, horizon_ref, core_ref, *refs):
-    dmiddle_ref, send_ref, keep_ref, gain_ref, loss_ref, count_ref = refs[:6]
-    weight_ref, head_ref, turned_ref, final_ref, dlogits_ref = refs[6:11]
-    normed_ref, inner_ref, slope_ref, dinner_ref, dout_ref, last_ref, sum_ref = refs[11:18]
-    targets_ref, counted_ref = refs[18:]
-    tokens = middle_ref.shape[0]
+def middle_kernel(widths, mesh_plan, *refs):
+    source_ref, own_ref, other_ref, drawn_ref, gains_ref, valid_ref, horizon_ref, core_ref = refs[:8]
+    out_ref, send_ref, keep_ref, gain_ref, loss_ref, count_ref = refs[8:14]
+    bias_ref, weight_one_ref, att_ref, weight_two_ref, head_ref, turned_ref = refs[14:20]
+    entry_ref, qkv_ref, mix_ref, chance_ref, middle_two_ref, inner_one_ref, slope_one_ref = refs[20:27]
+    inner_ref, slope_ref, last_ref, dmiddle_ref, sum_ref, targets_ref, counted_ref = refs[27:34]
+    normed_long, dattend_ref, dqkv_long, mixes_ref, normed_two_long, dinner_long, dout_long = refs[34:]
+    tokens = middle_two_ref.shape[0]
+    final_ref = normed_long.at[0:tokens]
+    dlogits_ref = dqkv_long.at[0:VOCAB]
+    normed_ref = normed_two_long.at[0:tokens]
+    dinner_ref = dinner_long.at[0:tokens]
+    dout_ref = dout_long.at[0:tokens]
+    groups = source_ref.shape[0] // ROWS
+    masks = head_masks()
+    gain_att = gains_ref[LAYERS - 1 : LAYERS, :]
+    gain_before = gains_ref[2 * LAYERS - 2 : 2 * LAYERS - 1, :]
+    gain_ffn = gains_ref[2 * LAYERS - 1 : 2 * LAYERS, :]
     gain_final = gains_ref[2 * LAYERS : 2 * LAYERS + 1, :]
-    gain_ffn = gains_ref[2 * LAYERS - 1 : 2 * LAYERS, :]
+    fill_bias(bias_ref)
     place_weights(
-        [(weight_ref, 0), (weight_ref, FF), (head_ref, 0)],
+        [
+            (weight_one_ref, 0),
+            (weight_one_ref, FF),
+            (att_ref, 0),
+            (att_ref, 3 * D),
+            (weight_two_ref, 0),
+            (weight_two_ref, FF),
+            (head_ref, 0),
+        ],
         own_ref,
         other_ref,
         core_ref[0],
         widths,
-        gather_plan,
-        start,
-    )
+        mesh_plan,
+    )
+
+    def rows_of(group, unit=CTX):
+        return pl.ds(pl.multiple_of(group * (GROUP * unit), GROUP * unit), GROUP * unit)
+
+    def forward(group, carry):
+        rows, short = rows_of(group), rows_of(group, SEG)
+        hidden = feed_forward(
+            source_ref[rows, :],
+            gain_before,
+            weight_one_ref,
+            inner_one_ref.at[rows],
+            slope_one_ref.at[rows],
+        )
+        entry_ref[rows, :] = hidden
+        attend_forward(
+            group,
+            hidden,
+            gain_att,
+            att_ref,
+            valid_ref,
+            bias_ref,
+            masks,
+            (
+                middle_two_ref.at[short],
+                qkv_ref.at[rows],
+                mix_ref.at[short],
+                chance_ref.at[pl.ds(group * GROUP, GROUP)],
+            ),
+        )
+        return carry
+
+    lax.fori_loop(0, groups, forward, 0)
     turned_ref[...] = head_ref[...].T
     samples = tokens // SEG
     targets_ref[...] = jnp.concatenate([drawn_ref[at] for at in range(samples)], axis=1)
@@ -417,18 +473,18 @@
     count_ref[...] = jnp.sum(counted_ref[...], axis=1, keepdims=True)
     for block in range(tokens // ROWS):
         rows = slice(block * ROWS, (block + 1) * ROWS)
-        middle = middle_ref[rows, :]
+        middle = middle_two_ref[rows, :]
         normed = (middle * inverse_rms(middle) * gain_ffn).astype(jnp.bfloat16)
         normed_ref[rows, :] = normed
         for part in range(FF // D):
             columns = slice(part * D, (part + 1) * D)
-            inner = dot_nn(normed, weight_ref[:, columns])
+            inner = dot_nn(normed, weight_two_ref[:, columns])
             for piece in range(GROUP):
                 there = slice(block * ROWS + piece * CTX, block * ROWS + (piece + 1) * CTX)
                 active, slope = gelu_parts(inner[piece * CTX : (piece + 1) * CTX])
                 inner_ref[there, columns] = active.astype(jnp.bfloat16)
-                slope_ref[there, columns] = slope
-        last = middle + dot_nt(inner_ref[rows, :], weight_ref[:, FF : 2 * FF])
+                slope_ref[there, columns] = slope.astype(jnp.bfloat16)
+        last = middle + dot_nt(inner_ref[rows, :], weight_two_ref[:, FF : 2 * FF])
         last_ref[rows, :] = last
         final_ref[rows, :] = (last * inverse_rms(last) * gain_final).astype(jnp.bfloat16)
     span = D
@@ -455,7 +511,7 @@
                     jnp.bfloat16
                 )
     loss_ref[...] = jnp.sum(loss, axis=1, keepdims=True)
-    sum_ref[:, 2 * FF :] = dot_nt(final_ref[...].T, dlogits_ref[...])
+    sum_ref[:, 2 * FF : 2 * FF + VOCAB] = dot_nt(final_ref[...].T, dlogits_ref[...])
     dfinal = dot_nn(head_ref[...], dlogits_ref[...]).T
     last = last_ref[...]
     dlast, gain_part = rms_back(last, inverse_rms(last), gain_final, dfinal)
@@ -469,17 +525,68 @@
         dout_ref[rows, :] = dout
         for part in range(FF // D):
             columns = slice(part * D, (part + 1) * D)
-            dact = dot_nn(dout, weight_ref[:, FF + part * D : FF + (part + 1) * D])
-            dinner_ref[rows, columns] = (dact * slope_ref[rows, columns]).astype(jnp.bfloat16)
-        dnormed = dot_nt(dinner_ref[rows, :], weight_ref[:, 0:FF])
-        middle = middle_ref[rows, :]
+            dact = dot_nn(dout, weight_two_ref[:, FF + part * D : FF + (part + 1) * D])
+            dinner_ref[rows, columns] = (dact * slope_ref[rows, columns].astype(jnp.float32)).astype(jnp.bfloat16)
+        dnormed = dot_nt(dinner_ref[rows, :], weight_two_ref[:, 0:FF])
+        middle = middle_two_ref[rows, :]
         through, gain_part = rms_back(middle, inverse_rms(middle), gain_ffn, dnormed)
         gain_sum = gain_sum + gain_part
         dmiddle_ref[rows, :] = upstream + through
     gain_ref[0:1, :] = gain_sum
     sum_ref[:, 0:FF] = dot_nn(normed_ref[...].T, dinner_ref[...])
     sum_ref[:, FF : 2 * FF] = dot_nn(dout_ref[...].T, inner_ref[...])
-    write_blocks(send_ref, keep_ref, sum_ref, core_ref[0], widths, mesh_plan)
+    write_blocks(send_ref, keep_ref, sum_ref, core_ref[0], widths[4:], mesh_plan)
+    gain_ref[2:4, :] = jnp.zeros((2, D), jnp.float32)
+
+    def backward(group, carry):
+        rows, short = rows_of(group), rows_of(group, SEG)
+
+        def here(start, length, unit=CTX):
+            return pl.ds(pl.multiple_of(group * (GROUP * unit) + start, 16), length)
+
+        dentry, gain_part = attend_back(
+            group,
+            here,
+            (
+                entry_ref[rows, :],
+                qkv_ref.at[rows],
+                mix_ref.at[short],
+                chance_ref.at[pl.ds(group * GROUP, GROUP)],
+            ),
+            dmiddle_ref[short, :],
+            gain_att,
+            att_ref,
+            masks,
+            (normed_long, dattend_ref, dqkv_long, mixes_ref),
+        )
+        gain_ref[2:3, :] += gain_part
+        dbefore, gain_part = feed_back(
+            here,
+            dentry,
+            source_ref[rows, :],
+            gain_before,
+            weight_one_ref,
+            slope_one_ref.at[rows],
+            (normed_two_long, dinner_long, dout_long),
+        )
+        out_ref[rows, :] = dbefore
+        gain_ref[3:4, :] += gain_part
+        return carry
+
+    lax.fori_loop(0, groups, backward, 0)
+    column = 0
+    for left, right in [
+        (normed_two_long, dinner_long),
+        (dout_long, inner_one_ref),
+        (normed_long, dqkv_long),
+        (mixes_ref, dattend_ref),
+    ]:
+        wide = right.shape[1]
+        sum_ref[:, column : column + wide] = dot_nn(left[...].T, right[...])
+        column += wide
+    write_blocks(
+        send_ref, keep_ref, sum_ref, core_ref[0], widths[:4], mesh_plan, sum(widths[4:])
+    )
 
 
 def block_outs(own, widths):
@@ -488,42 +595,58 @@
     return [shape(blocks, jnp.bfloat16), shape(blocks, jnp.float32)]
 
 
-def run_top(widths, gather_plan, mesh_plan, start, middle, own, other, targets, gains, horizon, core):
-    tokens = middle.shape[0]
+def run_middle(widths, mesh_plan, source, own, other, targets, gains, valid, horizon, core):
+    tokens = source.shape[0]
+    short = tokens // CTX * SEG
+    samples = tokens // CTX
+    chances = HEADS // 2 * SEG
     f32, b16 = jnp.float32, jnp.bfloat16
     shape = jax.ShapeDtypeStruct
     vmem = pl.BlockSpec(memory_space=pltpu.VMEM)
     return pl.pallas_call(
-        functools.partial(top_kernel, widths, gather_plan, mesh_plan, start),
-        in_specs=[vmem] * 5 + [smem_spec()] * 2,
+        functools.partial(middle_kernel, widths, mesh_plan),
+        in_specs=[vmem] * 5 + [smem_spec()] * 3,
         out_specs=[vmem] * 6,
         out_shape=[shape((tokens, D), f32)]
         + block_outs(own, widths)
-        + [shape((2, D), f32), shape((1, 1), f32), shape((1, 1), f32)],
+        + [shape((4, D), f32), shape((1, 1), f32), shape((1, 1), f32)],
         scratch_shapes=[
+            pltpu.VMEM((2, CTX, chances), f32),
+            pltpu.VMEM((D, 2 * FF), b16),
+            pltpu.VMEM((D, 4 * D), b16),
             pltpu.VMEM((D, 2 * FF), b16),
             pltpu.VMEM((D, VOCAB), b16),
             pltpu.VMEM((VOCAB, D), b16),
+            pltpu.VMEM((tokens, D), f32),
+            pltpu.VMEM((tokens, 3 * D), b16),
+            pltpu.VMEM((short, D), b16),
+            pltpu.VMEM((samples, 2, CTX, chances), b16),
+            pltpu.VMEM((short, D), f32),
+            pltpu.VMEM((tokens, FF), b16),
+            pltpu.VMEM((tokens, FF), b16),
+            pltpu.VMEM((short, FF), b16),
+            pltpu.VMEM((short, FF), b16),
+            pltpu.VMEM((short, D), f32),
+            pltpu.VMEM((short, D), f32),
+            pltpu.VMEM((D, 2 * FF + max(4 * D, VOCAB)), f32),
+            pltpu.VMEM((CATS, short), jnp.int32),
+            pltpu.VMEM((1, short), f32),
             pltpu.VMEM((tokens, D), b16),
-            pltpu.VMEM((VOCAB, tokens), b16),
+            pltpu.VMEM((short, D), b16),
+            pltpu.VMEM((tokens, 3 * D), b16),
+            pltpu.VMEM((short, D), b16),
             pltpu.VMEM((tokens, D), b16),
             pltpu.VMEM((tokens, FF), b16),
-            pltpu.VMEM((tokens, FF), f32),
-            pltpu.VMEM((tokens, FF), b16),
             pltpu.VMEM((tokens, D), b16),
-            pltpu.VMEM((tokens, D), f32),
-            pltpu.VMEM((D, 2 * FF + VOCAB), f32),
-            pltpu.VMEM((CATS, tokens), jnp.int32),
-            pltpu.VMEM((1, tokens), f32),
         ],
-        compiler_params=pltpu.CompilerParams(vmem_limit_bytes=VMEM_BYTES),
+        compiler_params=pltpu.CompilerParams(vmem_limit_bytes=MIDDLE_BYTES + (0 if own.shape[1] >= 64 else VMEM_BYTES // 2)),
         cost_estimate=pl.CostEstimate(
-            flops=6 * tokens * D * 3 * FF,
-            bytes_accessed=tokens * D * 8 + D * 3 * FF * 10,
-            transcendentals=tokens * (FF + VOCAB),
+            flops=6 * tokens * D * 8 * FF,
+            bytes_accessed=tokens * D * 8 + D * 6 * FF * 10,
+            transcendentals=2 * tokens * (FF + VOCAB),
         ),
-        name="loss_part",
-    )(middle, own, other, targets, gains, horizon, core)
+        name="middle_part",
+    )(source, own, other, targets, gains, valid, horizon, core)
 
 
 def backward_kernel(layer, widths, mesh_plan, *refs):
@@ -594,7 +717,9 @@
 
 
 def run_backward(layer, widths, mesh_plan, blocks_like, saved, dmiddle, gains, core, before):
-    entry, _, qkv, mix, chance, weights = saved[:6]
+    entry, _, qkv, mix, chance, weights = [in_hbm(item) for item in saved[:6]]
+    if layer > 0:
+        before = [in_hbm(item) for item in before]
     tokens = entry.shape[0]
     queries = chance.shape[3] // (HEADS // 2)
     short = tokens // CTX * queries
@@ -646,7 +771,7 @@
         out_specs=[spec for _, spec in outs],
         out_shape=[item for item, _ in outs],
         scratch_shapes=scratch,
-        compiler_params=pltpu.CompilerParams(vmem_limit_bytes=VMEM_BYTES),
+        compiler_params=pltpu.CompilerParams(vmem_limit_bytes=VMEM_BYTES * 3 // 2),
         cost_estimate=pl.CostEstimate(
             flops=6 * tokens * D * wide,
             bytes_accessed=tokens * D * 24 + D * wide * 6,
@@ -771,7 +896,7 @@
 
 def early_kernel(widths, *refs):
     raw_ref, masters, row_refs = refs[0], refs[1:7], refs[7:13]
-    gains_at, loss_ref, count_ref, packet_ref = refs[13:16], refs[16], refs[17], refs[18]
+    gains_at, loss_ref, count_ref, packet_ref = refs[13:15], refs[15], refs[16], refs[17]
     plan, _ = matrix_plan(widths)
     chosen = [item for item in matrix_list() if item not in LATE]
     inner, entries, outer = square_sums(raw_ref[...], chosen, plan, 0)
@@ -782,9 +907,10 @@
         row_sums.append(whole_sum(old_row(row_refs, which, layer)))
     packet_ref[...] = jnp.zeros_like(packet_ref)
     packet_ref[0:INNER_ROWS, 0 : inner.shape[1]] = inner[0:INNER_ROWS, :]
-    top, two, one = [ref[...] for ref in gains_at]
+    last, one = [ref[...] for ref in gains_at]
     gain = jnp.concatenate(
-        [jnp.zeros((1, D), jnp.float32), one[0:1], two[0:1], one[1:2], two[1:2], top], axis=0
+        [jnp.zeros((1, D), jnp.float32), one[0:1], last[2:3], one[1:2], last[3:4], last[0:2]],
+        axis=0,
     )
     scalars = [loss_ref[...], count_ref[...]] + weights + entries + row_sums
     scalars.append(jnp.zeros((1, LANES - len(scalars)), jnp.float32))
@@ -994,23 +1120,22 @@
 
     def join(self):
         self.at += 1
-        summed = self.kept
-        for other in self.others:
-            summed = summed + other.astype(jnp.float32)
-        if self.at == len(self.steps):
-            self.kept = summed
-            return
-        step = self.steps[self.at]
+        step = self.steps[self.at] if self.at < len(self.steps) else ()
         count = 1 << len(step)
         own = 0
         for bit in step:
             own = 2 * own + ((device_index() >> bit) & 1)
-        parts = summed.reshape((count, summed.shape[0] // count) + summed.shape[1:])
-        if count == 2:
-            self.sent = (jnp.where(own == 1, parts[0], parts[1]).astype(jnp.bfloat16),)
-            self.kept = jnp.where(own == 1, parts[1], parts[0])
-            return
-        pick = lambda digit: lax.dynamic_index_in_dim(parts, own ^ digit, 0, keepdims=False)
+        shape = (count, self.kept.shape[0] // count) + self.kept.shape[1:]
+        terms = [item.reshape(shape) for item in (self.kept,) + self.others]
+
+        def pick(digit):
+            total = None
+            for term in terms:
+                part = lax.dynamic_index_in_dim(term, own ^ digit, 0, keepdims=False)
+                part = part.astype(jnp.float32)
+                total = part if total is None else total + part
+            return total
+
         self.sent = tuple(pick(digit).astype(jnp.bfloat16) for digit in range(1, count))
         self.kept = pick(0)
 
@@ -1074,10 +1199,8 @@
     sizes = (lax.axis_size("dp"), lax.axis_size("fsdp"))
     highest = (sizes[0] * sizes[1]).bit_length() - 1
     gather_steps = [(bit,) for bit in reversed(range(3, highest))] + [(2, 1), (0,)]
-    third_steps = [(4, 3)] + [(bit,) for bit in range(5, highest)] + [(2, 1), (0,)]
     scatter_steps = gather_steps[::-1]
     mesh_plan = (sizes[0], sizes[1], gather_steps)
-    third_plan = (sizes[0], sizes[1], third_steps)
     core = (lax.axis_index("fsdp") & 1).astype(jnp.int32).reshape(1)
 
     out_turned = jnp.swapaxes(out_weight, 1, 2)
@@ -1091,27 +1214,21 @@
         ffn_widths + att_widths,
         ffn_widths + att_widths + ffn_widths + widths[5:6],
     ]
-    first, second, third = [
-        Gather(piece, steps)
-        for piece, steps in zip(
-            run_pack(masters, chunk_widths), [gather_steps, gather_steps, third_steps]
-        )
-    ]
+    chunks = [Gather(piece, gather_steps) for piece in run_pack(masters, chunk_widths)]
+    first, second, third = chunks
     latent_rows = latents.transpose(0, 2, 1)
     target_rows = targets.transpose(0, 2, 1)
     shared = (gains, memory_valid, core)
     back_shared = (gains, core)
 
     count = len(gather_steps)
-    while first.at < count - 1:
-        first.send()
-        second.send()
-        first.join()
-        second.join()
-    while third.at < len(third_steps) - 2:
-        third.send()
-        third.join()
-    third.send()
+    for at in range(count - 1):
+        for chunk in chunks:
+            chunk.send()
+        for chunk in chunks[: 2 if at == count - 2 else 3]:
+            chunk.join()
+            if at == count - 3 and chunk is first:
+                first.held, third.held = tie(first.held, third.held)
     first.send()
     (other,) = first.others
     held, other, second.held = tie(first.held, other, second.held)
@@ -1125,38 +1242,27 @@
         run_forward(1, chunk_widths[1], mesh_plan, middle, second.held, other, *shared)
     )
     middle, (other,) = tie(kept[1][1], third.others)
-    kept.append(run_forward(2, chunk_widths[2], third_plan, middle, third.held, other, *shared))
-
-    dmiddle, sent, held, gain_top, loss, counted = run_top(
-        ffn_widths + widths[5:6],
-        third_plan,
+    dmiddle, sent, held, gain_middle, loss, counted = run_middle(
+        chunk_widths[2],
         mesh_plan,
-        sum(ffn_widths + att_widths),
-        kept[2][1],
+        middle,
         third.held,
         other,
         target_rows,
         gains,
+        memory_valid,
         horizon,
         core,
     )
-    top = Scatter(sent, held, scatter_steps)
-    top.send()
+    pair = Scatter(sent, held, scatter_steps)
+    pair.send()
+    pair.join()
     like = first.held
-    before = [(kept[at][1], kept[at + 1][6], kept[at + 1][8], kept[at + 1][7]) for at in range(2)]
-    dmiddle, sent, held, gain_two = run_backward(
-        2, chunk_widths[1], mesh_plan, like, kept[2], dmiddle, *back_shared, before[1]
-    )
-    dmiddle, sent, held, top.others = tie(dmiddle, sent, held, top.others)
-    two = Scatter(sent, held, scatter_steps)
-    two.send()
-    top.join()
-    two.join()
-    pair = merged([top, two])
+    before = (kept[0][1], kept[1][6], kept[1][8], kept[1][7])
     dmiddle, pair.sent = tie(dmiddle, pair.sent)
     pair.send()
     dmiddle, sent, held, gain_one = run_backward(
-        1, chunk_widths[1], mesh_plan, like, kept[1], dmiddle, *back_shared, before[0]
+        1, chunk_widths[1], mesh_plan, like, kept[1], dmiddle, *back_shared, before
     )
     dmiddle, sent, held, pair.others = tie(dmiddle, sent, held, pair.others)
     one = Scatter(sent, held, scatter_steps)
@@ -1191,7 +1297,7 @@
     outer = [flat(item) for item in (qkv_cols, out_cols, up_cols, down_rows, embed_rows, head_cols)]
     row_stats = [inner[at] if ROW_IS_INNER[at] else outer[at] for at in range(6)]
     packet = run_early(
-        widths, raw_early, masters, row_stats, [gain_top, gain_two, gain_one], loss, counted
+        widths, raw_early, masters, row_stats, [gain_middle, gain_one], loss, counted
     )
     while zero.at < count:
         zero.join()

time: 215 us -> 213 us (level)
  local copies, waits for them, and re-layouts: 24.9 us -> 7.07 us
  waiting for transfers between devices: 31.2 us -> 41.8 us
  Pallas kernels: 86.5 us -> 94.6 us
  starting transfers between devices: 55.4 us -> 50.3 us
  other arithmetic: 14.6 us -> 17.5 us
    pallas_call x1, Pallas kernels: 8.48 us -> 31.9 us  [run_middle(): pl.pallas_call(functools.partial(middle_kernel, widths, mesh_plan), in_sp...]
    unnamed x104 -> x36, local copies, waits for them, and re-layouts: 23.2 us -> 7.07 us
    ppermute x44 -> x42, waiting for transfers between devices: 31.2 us -> 41.8 us  [swap(): lax.ppermute(value, ('dp', 'fsdp'), [(place, place ^ mask) for place in r...]
    pallas_call x3 -> x2, Pallas kernels: 35.6 us -> 27.3 us  [run_backward(): pl.pallas_call(functools.partial(backward_kernel, layer, widths, mesh_pla...]
    pallas_call x3 -> x2, Pallas kernels: 31.8 us -> 24.9 us  [run_forward(): pl.pallas_call(functools.partial(forward_kernel, layer, widths, mesh_plan...]
    ppermute x44 -> x42, starting transfers between devices: 55.4 us -> 50.3 us  [swap(): lax.ppermute(value, ('dp', 'fsdp'), [(place, place ^ mask) for place in r...]
    convert_element_type x6 -> x4, other arithmetic: 0.13 us -> 2.56 us  [join(): pick(digit).astype(jnp.bfloat16)]
    add x10 -> x5, other arithmetic: 4.82 us -> 6.09 us  [pick(): total = part if total is None else total + part]
  transfers between devices with their start and end apart: 44 -> 42, of which waited for: 18 -> 22; matrix products, arithmetic and copies ran while one was open for 4% -> 4% of each run, Pallas kernels for 28% -> 26%
where the time goes in v2:
time: 213 us
  Pallas kernels  94.6 us (44%)
  starting transfers between devices  50.3 us (24%)
  waiting for transfers between devices  41.8 us (20%)
  other arithmetic  17.5 us (8%)
  local copies, waits for them, and re-layouts  7.07 us (3%)
    ppermute x42, starting transfers between devices, swap(): lax.ppermute(value, ('dp', 'fsdp'), [(place, place ^ mask) for place in r...  50.3 us
    ppermute x42, waiting for transfers between devices, swap(): lax.ppermute(value, ('dp', 'fsdp'), [(place, place ^ mask) for place in r...  41.8 us
    pallas_call x1, Pallas kernels, run_middle(): pl.pallas_call(functools.partial(middle_kernel, widths, mesh_plan), in_sp...  31.9 us
    pallas_call x2, Pallas kernels, run_backward(): pl.pallas_call(functools.partial(backward_kernel, layer, widths, mesh_pla...  27.3 us
    pallas_call x2, Pallas kernels, run_forward(): pl.pallas_call(functools.partial(forward_kernel, layer, widths, mesh_plan...  24.9 us
    unnamed x36, local copies, waits for them, and re-layouts  7.07 us
    add x5, other arithmetic, pick(): total = part if total is None else total + part  6.09 us
  transfers between devices with their start and end apart: 42, of which 22 were waited for; matrix products, arithmetic and copies ran while one was open for 4% of the time, Pallas kernels for 26%

profile of v2, /device:TPU:0, one launch (start us, length us, event | category | flops | bytes accessed | tf_op | source)
XLA Modules:
  0.0 212.6 jit_solution(7491846598032001394)
XLA Ops:
  0.7 1.8 pack.1
  2.5 4.0 %collective-permute-start = (bf16[1,64,256]{2,1,0:T(8,128)(2,1)}, bf16[1,64,256]{2,1,0:T(8,128)(2,1)S(1)}, u32[]{:S(2)}, u32[]{:S(2)}) collective-permute-start(bf16[1,64,256]{2,1,0:T(8,128)(2,1)} %bitcast.129), channel_id=1, source_target_pairs={{0,16},{1,17},{2,18},{3,19},{4,20},{5,21},{6,22},{7,23},{8,24},{9,... | collective-permute-start | bytes 98312 | tf_op jit(solution)/shard_map/ppermute | solution.py:1071
  6.6 2.9 %collective-permute-start.2 = (bf16[1,64,768]{2,1,0:T(8,128)(2,1)}, bf16[1,64,768]{2,1,0:T(8,128)(2,1)S(1)}, u32[]{:S(2)}, u32[]{:S(2)}) collective-permute-start(bf16[1,64,768]{2,1,0:T(8,128)(2,1)} %bitcast.127), channel_id=1, source_target_pairs={{0,16},{1,17},{2,18},{3,19},{4,20},{5,21},{6,22},{7,23},{8,24},{9,... | collective-permute-start | bytes 294920 | tf_op jit(solution)/shard_map/ppermute | solution.py:1071
  10.3 1.6 collective-permute-start.1
  11.9 3.4 %collective-permute-done.7 = bf16[1,64,384]{2,1,0:T(8,128)(2,1)S(1)} collective-permute-done((bf16[1,64,384]{2,1,0:T(8,128)(2,1)}, bf16[1,64,384]{2,1,0:T(8,128)(2,1)S(1)}, u32[]{:S(2)}, u32[]{:S(2)}) %collective-permute-start.7) | collective-permute-done | bytes 49184 | tf_op jit(solution)/shard_map/ppermute | solution.py:1071
  18.2 2.5 %collective-permute-start.3 = (bf16[4,64,256]{2,1,0:T(8,128)(2,1)S(1)}, bf16[4,64,256]{2,1,0:T(8,128)(2,1)S(1)}, u32[]{:S(2)}, u32[]{:S(2)}) collective-permute-start(bf16[4,64,256]{2,1,0:T(8,128)(2,1)S(1)} %pad_maximum_fusion.7), channel_id=1, source_target_pairs={{0,6},{1,7},{2,4},{3,5},{4,2},{5,3},{6,0},{7,1},{8,14},{9,15},{10,... | collective-permute-start | bytes 393224 | tf_op jit(solution)/shard_map/ppermute | solution.py:1071
  21.8 1.6 collective-permute-start.10
  23.4 1.5 collective-permute-start.11
  25.6 2.5 %collective-permute-start.9 = (bf16[4,64,384]{2,1,0:T(8,128)(2,1)S(1)}, bf16[4,64,384]{2,1,0:T(8,128)(2,1)S(1)}, u32[]{:S(2)}, u32[]{:S(2)}) collective-permute-start(bf16[4,64,384]{2,1,0:T(8,128)(2,1)S(1)} %pad_maximum_fusion.5), channel_id=1, source_target_pairs={{0,6},{1,7},{2,4},{3,5},{4,2},{5,3},{6,0},{7,1},{8,14},{9,15},{10,... | collective-permute-start | bytes 589832 | tf_op jit(solution)/shard_map/ppermute | solution.py:1071
  28.9 1.2 collective-permute-start.13
  30.1 1.9 collective-permute-done.10
  32.0 2.2 %collective-permute-done.11 = bf16[4,64,384]{2,1,0:T(8,128)(2,1)S(1)} collective-permute-done((bf16[4,64,384]{2,1,0:T(8,128)(2,1)S(1)}, bf16[4,64,384]{2,1,0:T(8,128)(2,1)S(1)}, u32[]{:S(2)}, u32[]{:S(2)}) %collective-permute-start.11) | collective-permute-done | bytes 196640 | tf_op jit(solution)/shard_map/ppermute | solution.py:1071
  34.6 1.6 collective-permute-done.13
  38.1 1.4 collective-permute-start.15
  40.5 10.5 %forward_part.2 = (f32[1536,256]{1,0:T(8,128)}, f32[1536,256]{1,0:T(8,128)}, bf16[1536,768]{1,0:T(8,128)(2,1)}, bf16[1536,256]{1,0:T(8,128)(2,1)}, bf16[16,2,96,...) custom-call(s32[16,32,96]{2,1,0:T(8,128)S(1)} %bitcast.103, bf16[16,64,256]{2,1,0:T(8,128)(2,1)S(1)} %pad_maximum_fusion.2.own_ref, ...), custom_call_target="tpu_custom_call" | custom-call | flops 2415919104 | bytes 9437184 | tf_op jit(solution)/shard_map/forward_part/pallas_call | solution.py:374
  51.0 6.6 %collective-permute-done.16 = bf16[4,64,768]{2,1,0:T(8,128)(2,1)} collective-permute-done((bf16[4,64,768]{2,1,0:T(8,128)(2,1)}, bf16[4,64,768]{2,1,0:T(8,128)(2,1)}, u32[]{:S(2)}, u32[]{:S(2)}) %collective-permute-start.16) | collective-permute-done | bytes 393248 | tf_op jit(solution)/shard_map/ppermute | solution.py:1071
  57.6 1.4 broadcast_select_fusion.7
  59.3 14.4 %forward_part.3 = (f32[1536,256]{1,0:T(8,128)}, f32[1536,256]{1,0:T(8,128)}, bf16[1536,768]{1,0:T(8,128)(2,1)}, bf16[1536,256]{1,0:T(8,128)(2,1)}, bf16[16,2,96,...) custom-call(f32[1536,256]{1,0:T(8,128)} %get-tuple-element.143.sourc, ...), custom_call_target="tpu_custom_call" | custom-call | flops 2415919104 | bytes 9437184 | tf_op jit(solution)/shard_map/forward_part/pallas_call | solution.py:374
  73.7 1.4 copy-done.8
  75.1 31.9 %middle_part.1 = (f32[1536,256]{1,0:T(8,128)S(1)}, bf16[16,64,768]{2,1,0:T(8,128)(2,1)S(1)}, f32[16,64,768]{2,1,0:T(8,128)}, f32[4,256]{1,0:T(4,128)S(1)}, f32[1,1]{1,0:T(1,128)}, /*index=5*/f32[1,1]{1,0:T(1,128)}) custom-call(f32[1536,256]{1,0:T(8,128)S(1)} %copy-done.8, bf16[16,64,768]{2,1,0:T(8,128)(2,1)S(1)} %pad_maximum_fusion.refs_1_, ...), custom_call_target="tpu_custom_call" | custom-call | flops 19327352832 | bytes 18874368 | tf_op jit(solution)/shard_map/middle_part/pallas_call | solution.py:606
  107.6 1.2 copy-done.11
  109.3 3.0 %collective-permute-done.18 = bf16[16,64,768]{2,1,0:T(8,128)(2,1)S(1)} collective-permute-done((bf16[16,64,768]{2,1,0:T(8,128)(2,1)S(1)}, bf16[16,64,768]{2,1,0:T(8,128)(2,1)S(1)}, u32[]{:S(2)}, u32[]{:S(2)}) %collective-permute-start.18) | collective-permute-done | bytes 1572896 | tf_op jit(solution)/shard_map/ppermute | solution.py:1071
  112.3 2.4 %convert_add_fusion = (f32[1,4,64,768]{3,2,1,0:T(8,128)S(1)}, bf16[4,64,768]{2,1,0:T(8,128)(2,1)S(1)}, bf16[4,64,768]{2,1,0:T(8,128)(2,1)S(1)}, bf16[4,64,768]{2,1,0:T(8,128)(2,1)S(1)}) fusion(f32[4,4,64,768]{3,2,1,0:T(8,128)} %bitcast.105, s32[]{:T(128)S(6)} %select_n.336, bf16[4,4,64,768]{3,2,1,0:T(8,128)(2,1)S(1)} %bitcast.107, s32[]{:T(128)S(6)} %select_n.340, ...), kind=kLoop, calls=%fused_computation.5 | loop fusion | flops 2162688 | bytes 6684688 | tf_op jit(solution)/shard_map/add | solution.py:1136
  114.8 1.4 collective-permute-start.19
  118.4 15.7 %backward_part.2 = (f32[1536,256]{1,0:T(8,128)S(1)}, bf16[16,64,384]{2,1,0:T(8,128)(2,1)S(1)}, f32[16,64,384]{2,1,0:T(8,128)S(1)}, f32[2,256]{1,0:T(2,128)S(1)}) custom-call(f32[1536,256]{1,0:T(8,128)} %get-tuple-element.151.refs_0_, bf16[1536,768]{1,0:T(8,128)(2,1)} %get-tuple-element.152.refs_1_, bf16[1536,256]{1,0:T(8,128)(2,1)} %get-tuple-element.153.refs_2_, ...), custom_call_target="tpu_custom_call" | custom-call | flops 7247757312 | bytes 14155776 | tf_op jit(solution)/shard_map/backward_part/pallas_call | solution.py:767
  136.6 2.3 %convert_add_fusion.2 = (f32[1,2,64,768]{3,2,1,0:T(8,128)}, bf16[2,64,768]{2,1,0:T(8,128)(2,1)S(1)}) fusion(f32[2,2,64,768]{3,2,1,0:T(8,128)S(1)} %bitcast.106, s32[]{:T(128)S(6)} %select_n.337, bf16[2,2,64,768]{3,2,1,0:T(8,128)(2,1)} %bitcast.117, bf16[2,2,64,768]{3,2,1,0:T(8,128)(2,1)} %bitcast.16, bf16[2,2,64,768]{3,2,1,0:T(8,128)(2,1)} %bitcast.15, ...), kind=kLoop, calls=%fused_computation.16 | loop fusion | flops 1277952 | bytes 2555912 | tf_op jit(solution)/shard_map/add | solution.py:1136
  139.0 1.5 fusion.7
  140.6 1.3 collective-permute-start.23
  141.8 1.7 collective-permute-start.24
  145.3 11.6 %backward_part.3 = (bf16[16,64,256]{2,1,0:T(8,128)(2,1)S(1)}, f32[16,64,256]{2,1,0:T(8,128)S(1)}, f32[2,256]{1,0:T(2,128)S(1)}) custom-call(f32[1536,256]{1,0:T(8,128)} %get-tuple-element.170.refs_0_, bf16[1536,768]{1,0:T(8,128)(2,1)} %get-tuple-element.171.refs_1_, bf16[1536,256]{1,0:T(8,128)(2,1)} %get-tuple-element.172.refs_2_, ...), custom_call_target="tpu_custom_call" | custom-call | flops 4831838208 | bytes 12582912 | tf_op jit(solution)/shard_map/backward_part/pallas_call | solution.py:767
  161.5 1.4 collective-permute-start.30
  162.8 1.2 collective-permute-start.31
  165.1 2.1 collective-permute-done.30
  167.1 2.1 collective-permute-done.31
  169.2 1.9 collective-permute-done.32
  171.2 1.3 collective-permute-start.33
  172.5 2.7 %collective-permute-start.29 = (bf16[1,64,1152]{2,1,0:T(8,128)(2,1)S(1)}, bf16[1,64,1152]{2,1,0:T(8,128)(2,1)S(1)}, u32[]{:S(2)}, u32[]{:S(2)}) collective-permute-start(bf16[1,64,1152]{2,1,0:T(8,128)(2,1)S(1)} %pad_maximum_fusion.6), channel_id=1, source_target_pairs={{0,16},{1,17},{2,18},{3,19},{4,20},{5,21},{6,22},{7,23},{8,24},{9,... | collective-permute-start | bytes 442376 | tf_op jit(solution)/shard_map/ppermute | solution.py:1071
  176.1 2.4 %collective-permute-start.34 = (bf16[1,64,256]{2,1,0:T(8,128)(2,1)S(1)}, bf16[1,64,256]{2,1,0:T(8,128)(2,1)S(1)}, u32[]{:S(2)}, u32[]{:S(2)}) collective-permute-start(bf16[1,64,256]{2,1,0:T(8,128)(2,1)S(1)} %fusion.15), channel_id=1, source_target_pairs={{0,16},{1,17},{2,18},{3,19},{4,20},{5,21},{6,22},{7,23},{8,24},{9,... | collective-permute-start | bytes 98312 | tf_op jit(solution)/shard_map/ppermute | solution.py:1071
  178.5 3.9 %collective-permute-done.29 = bf16[1,64,1152]{2,1,0:T(8,128)(2,1)S(1)} collective-permute-done((bf16[1,64,1152]{2,1,0:T(8,128)(2,1)S(1)}, bf16[1,64,1152]{2,1,0:T(8,128)(2,1)S(1)}, u32[]{:S(2)}, u32[]{:S(2)}) %collective-permute-start.29) | collective-permute-done | bytes 147488 | tf_op jit(solution)/shard_map/ppermute | solution.py:1071
  183.2 3.6 %early_statistics.1.early_ref = f32[48,128]{1,0:T(8,128)} custom-call(f32[64,1152]{1,0:T(8,128)} %fusion.3.refs_0_.refs_1_, f32[3,64,96]{2,1,0:T(8,128)} %refs_3_.3, f32[3,32,64]{2,1,0:T(8,128)} %bitcast.115, f32[3,64,128]{2,1,0:T(8,128)} %refs_5_.5, f32[3,64,128]{2,1,0:T(8,128)} %bitcast.111, f32[64,128]{1,0:T(8,128)} %bitcast.119, f32[64,128]{1,0:T(8,128)} %refs_8_.3, ...), custom_call_target="tpu_custom_call" | custom-call | tf_op jit(solution)/shard_map/early_statistics/pallas_call | solution.py:941
  187.5 1.7 late_statistics.1
  189.1 1.4 collective-permute-done.35
  191.3 1.3 collective-permute-start.36
  192.5 1.4 collective-permute-start.37
  196.4 2.3 %collective-permute-done.38 = f32[48,128]{1,0:T(8,128)S(1)} collective-permute-done((f32[48,128]{1,0:T(8,128)S(1)}, f32[48,128]{1,0:T(8,128)S(1)}, u32[]{:S(2)}, u32[]{:S(2)}) %collective-permute-start.38) | collective-permute-done | bytes 24608 | tf_op jit(solution)/shard_map/ppermute | solution.py:1071
  199.4 3.2 %collective-permute-start.40 = (f32[48,128]{1,0:T(8,128)S(1)}, f32[48,128]{1,0:T(8,128)S(1)}, u32[]{:S(2)}, u32[]{:S(2)}) collective-permute-start(f32[48,128]{1,0:T(8,128)S(1)} %pad_maximum_fusion.11), channel_id=1, source_target_pairs={{0,16},{1,17},{2,18},{3,19},{4,20},{5,21},{6,22},{7,23},{8,24},{9,... | collective-permute-start | bytes 73736 | tf_op jit(solution)/shard_map/ppermute | solution.py:1071
  204.5 3.8 %collective-permute-done.41 = f32[48,128]{1,0:T(8,128)S(1)} collective-permute-done((f32[48,128]{1,0:T(8,128)S(1)}, f32[48,128]{1,0:T(8,128)S(1)}, u32[]{:S(2)}, u32[]{:S(2)}) %collective-permute-start.41) | collective-permute-done | bytes 24608 | tf_op jit(solution)/shard_map/ppermute | solution.py:1071
  208.9 3.5 %update.1 = (f32[1,1]{1,0:T(1,128)}, f32[1,1]{1,0:T(1,128)}, f32[1,1]{1,0:T(1,128)}, f32[64,128]{1,0:T(8,128)}, f32[64,128]{1,0:T(8,128)}, /*index=5*/f32[1,128]...) custom-call(f32[48,128]{1,0:T(8,128)} %pad_maximum_fusion.10.refs_0_, ...), custom_call_target="tpu_custom_call" | custom-call | tf_op jit(solution)/shard_map/update/pallas_call | solution.py:1060
  (117 shorter events, 31.7 us)
Async XLA Ops:
  2.5 7.0 %collective-permute-start = (bf16[1,64,256]{2,1,0:T(8,128)(2,1)}, bf16[1,64,256]{2,1,0:T(8,128)(2,1)S(1)}, u32[]{:S(2)}, u32[]{:S(2)}) collective-permute-start(bf16[1,64,256]{2,1,0:T(8,128)(2,1)} %bitcast.129), channel_id=1, source_target_pairs={{0,16},{1,17},{2,18},{3,19},{4,20},{5,21},{6,22},{7,23},{8,24},{9,... | collective-permute-start | bytes 98312 | tf_op jit(solution)/shard_map/ppermute | solution.py:1071
  6.6 8.7 %collective-permute-start.7 = (bf16[1,64,384]{2,1,0:T(8,128)(2,1)}, bf16[1,64,384]{2,1,0:T(8,128)(2,1)S(1)}, u32[]{:S(2)}, u32[]{:S(2)}) collective-permute-start(bf16[1,64,384]{2,1,0:T(8,128)(2,1)} %bitcast.128), channel_id=1, source_target_pairs={{0,16},{1,17},{2,18},{3,19},{4,20},{5,21},{6,22},{7,23},{8,24},{9,... | collective-permute-start | bytes 147464 | tf_op jit(solution)/shard_map/ppermute | solution.py:1071
  6.6 10.7 %collective-permute-start.2 = (bf16[1,64,768]{2,1,0:T(8,128)(2,1)}, bf16[1,64,768]{2,1,0:T(8,128)(2,1)S(1)}, u32[]{:S(2)}, u32[]{:S(2)}) collective-permute-start(bf16[1,64,768]{2,1,0:T(8,128)(2,1)} %bitcast.127), channel_id=1, source_target_pairs={{0,16},{1,17},{2,18},{3,19},{4,20},{5,21},{6,22},{7,23},{8,24},{9,... | collective-permute-start | bytes 294920 | tf_op jit(solution)/shard_map/ppermute | solution.py:1071
  10.3 7.0 %collective-permute-start.1 = (bf16[2,64,256]{2,1,0:T(8,128)(2,1)S(1)}, bf16[2,64,256]{2,1,0:T(8,128)(2,1)S(1)}, u32[]{:S(2)}, u32[]{:S(2)}) collective-permute-start(bf16[2,64,256]{2,1,0:T(8,128)(2,1)S(1)} %pad_maximum_fusion.9), channel_id=1, source_target_pairs={{0,8},{1,9},{2,10},{3,11},{4,12},{5,13},{6,14},{7,15},{8,0},{9,1},... | collective-permute-start | bytes 196616 | tf_op jit(solution)/shard_map/ppermute | solution.py:1071
  16.1 5.6 %collective-permute-start.8 = (bf16[2,64,384]{2,1,0:T(8,128)(2,1)S(1)}, bf16[2,64,384]{2,1,0:T(8,128)(2,1)S(1)}, u32[]{:S(2)}, u32[]{:S(2)}) collective-permute-start(bf16[2,64,384]{2,1,0:T(8,128)(2,1)S(1)} %pad_maximum_fusion.8), channel_id=1, source_target_pairs={{0,8},{1,9},{2,10},{3,11},{4,12},{5,13},{6,14},{7,15},{8,0},{9,1},... | collective-permute-start | bytes 294920 | tf_op jit(solution)/shard_map/ppermute | solution.py:1071
  18.2 7.4 %collective-permute-start.3 = (bf16[4,64,256]{2,1,0:T(8,128)(2,1)S(1)}, bf16[4,64,256]{2,1,0:T(8,128)(2,1)S(1)}, u32[]{:S(2)}, u32[]{:S(2)}) collective-permute-start(bf16[4,64,256]{2,1,0:T(8,128)(2,1)S(1)} %pad_maximum_fusion.7), channel_id=1, source_target_pairs={{0,6},{1,7},{2,4},{3,5},{4,2},{5,3},{6,0},{7,1},{8,14},{9,15},{10,... | collective-permute-start | bytes 393224 | tf_op jit(solution)/shard_map/ppermute | solution.py:1071
  20.7 7.8 %collective-permute-start.4 = (bf16[4,64,256]{2,1,0:T(8,128)(2,1)S(1)}, bf16[4,64,256]{2,1,0:T(8,128)(2,1)S(1)}, u32[]{:S(2)}, u32[]{:S(2)}) collective-permute-start(bf16[4,64,256]{2,1,0:T(8,128)(2,1)S(1)} %pad_maximum_fusion.7), channel_id=1, source_target_pairs={{0,4},{1,5},{2,6},{3,7},{4,0},{5,1},{6,2},{7,3},{8,12},{9,13},{10,... | collective-permute-start | bytes 393224 | tf_op jit(solution)/shard_map/ppermute | solution.py:1071
  21.3 7.4 %collective-permute-start.5 = (bf16[4,64,256]{2,1,0:T(8,128)(2,1)S(1)}, bf16[4,64,256]{2,1,0:T(8,128)(2,1)S(1)}, u32[]{:S(2)}, u32[]{:S(2)}) collective-permute-start(bf16[4,64,256]{2,1,0:T(8,128)(2,1)S(1)} %pad_maximum_fusion.7), channel_id=1, source_target_pairs={{0,2},{1,3},{2,0},{3,1},{4,6},{5,7},{6,4},{7,5},{8,10},{9,11},{10,... | collective-permute-start | bytes 393224 | tf_op jit(solution)/shard_map/ppermute | solution.py:1071
  21.8 10.2 %collective-permute-start.10 = (bf16[4,64,384]{2,1,0:T(8,128)(2,1)S(1)}, bf16[4,64,384]{2,1,0:T(8,128)(2,1)S(1)}, u32[]{:S(2)}, u32[]{:S(2)}) collective-permute-start(bf16[4,64,384]{2,1,0:T(8,128)(2,1)S(1)} %pad_maximum_fusion.5), channel_id=1, source_target_pairs={{0,4},{1,5},{2,6},{3,7},{4,0},{5,1},{6,2},{7,3},{8,12},{9,13},{10,... | collective-permute-start | bytes 589832 | tf_op jit(solution)/shard_map/ppermute | solution.py:1071
  23.4 10.8 %collective-permute-start.11 = (bf16[4,64,384]{2,1,0:T(8,128)(2,1)S(1)}, bf16[4,64,384]{2,1,0:T(8,128)(2,1)S(1)}, u32[]{:S(2)}, u32[]{:S(2)}) collective-permute-start(bf16[4,64,384]{2,1,0:T(8,128)(2,1)S(1)} %pad_maximum_fusion.5), channel_id=1, source_target_pairs={{0,2},{1,3},{2,0},{3,1},{4,6},{5,7},{6,4},{7,5},{8,10},{9,11},{10,... | collective-permute-start | bytes 589832 | tf_op jit(solution)/shard_map/ppermute | solution.py:1071
  25.6 8.6 %collective-permute-start.9 = (bf16[4,64,384]{2,1,0:T(8,128)(2,1)S(1)}, bf16[4,64,384]{2,1,0:T(8,128)(2,1)S(1)}, u32[]{:S(2)}, u32[]{:S(2)}) collective-permute-start(bf16[4,64,384]{2,1,0:T(8,128)(2,1)S(1)} %pad_maximum_fusion.5), channel_id=1, source_target_pairs={{0,6},{1,7},{2,4},{3,5},{4,2},{5,3},{6,0},{7,1},{8,14},{9,15},{10,... | collective-permute-start | bytes 589832 | tf_op jit(solution)/shard_map/ppermute | solution.py:1071
  28.8 5.7 %collective-permute-start.6 = (bf16[16,64,256]{2,1,0:T(8,128)(2,1)S(1)}, bf16[16,64,256]{2,1,0:T(8,128)(2,1)S(1)}, u32[]{:S(2)}, u32[]{:S(2)}) collective-permute-start(bf16[16,64,256]{2,1,0:T(8,128)(2,1)S(1)} %pad_maximum_fusion.2.own_ref), channel_id=1, source_target_pairs={{0,1},{1,0},{2,3},{3,2},{4,5},{5,4},{6,7},{7,6},{8,9},{9,8},{10,11... | collective-permute-start | bytes 1572872 | tf_op jit(solution)/shard_map/ppermute | solution.py:1071
  28.9 7.3 %collective-permute-start.13 = (bf16[2,64,768]{2,1,0:T(8,128)(2,1)S(1)}, bf16[2,64,768]{2,1,0:T(8,128)(2,1)S(1)}, u32[]{:S(2)}, u32[]{:S(2)}) collective-permute-start(bf16[2,64,768]{2,1,0:T(8,128)(2,1)S(1)} %pad_maximum_fusion.4), channel_id=1, source_target_pairs={{0,8},{1,9},{2,10},{3,11},{4,12},{5,13},{6,14},{7,15},{8,0},{9,1},... | collective-permute-start | bytes 589832 | tf_op jit(solution)/shard_map/ppermute | solution.py:1071
  34.3 6.2 %copy-start = (f32[7,256]{1,0:T(8,128)S(1)}, f32[7,256]{1,0:T(8,128)}, u32[]{:S(2)}) copy-start(f32[7,256]{1,0:T(8,128)} %refs_21_.1) | copy-start | bytes 21508
  34.3 6.2 %copy-start.5 = (s32[16,96,32]{1,2,0:T(8,128)S(1)}, s32[16,96,32]{1,2,0:T(8,128)}, u32[]{:S(2)}) copy-start(s32[16,96,32]{1,2,0:T(8,128)} %param.24) | copy-start | bytes 589828
  34.3 6.2 %copy-start.6 = (s32[16]{0:T(128)S(1)}, s32[16]{0:T(128)}, u32[]{:S(2)}) copy-start(s32[16]{0:T(128)} %refs_5_.4) | copy-start | bytes 196
  34.5 23.1 %collective-permute-start.12 = (bf16[16,64,384]{2,1,0:T(8,128)(2,1)S(1)}, bf16[16,64,384]{2,1,0:T(8,128)(2,1)S(1)}, u32[]{:S(2)}, u32[]{:S(2)}) collective-permute-start(bf16[16,64,384]{2,1,0:T(8,128)(2,1)S(1)} %pad_maximum_fusion.1.own_ref), channel_id=1, source_target_pairs={{0,1},{1,0},{2,3},{3,2},{4,5},{5,4},{6,7},{7,6},{8,9},{9,8},{10,11... | collective-permute-start | bytes 2359304 | tf_op jit(solution)/shard_map/ppermute | solution.py:1071
  37.0 14.0 %collective-permute-start.14 = (bf16[4,64,768]{2,1,0:T(8,128)(2,1)}, bf16[4,64,768]{2,1,0:T(8,128)(2,1)}, u32[]{:S(2)}, u32[]{:S(2)}) collective-permute-start(bf16[4,64,768]{2,1,0:T(8,128)(2,1)} %pad_maximum_fusion.3), channel_id=1, source_target_pairs={{0,2},{1,3},{2,0},{3,1},{4,6},{5,7},{6,4},{7,5},{8,10},{9,11},{10,... | collective-permute-start | bytes 1179656 | tf_op jit(solution)/shard_map/ppermute | solution.py:1071
  38.1 12.9 %collective-permute-start.15 = (bf16[4,64,768]{2,1,0:T(8,128)(2,1)}, bf16[4,64,768]{2,1,0:T(8,128)(2,1)}, u32[]{:S(2)}, u32[]{:S(2)}) collective-permute-start(bf16[4,64,768]{2,1,0:T(8,128)(2,1)} %pad_maximum_fusion.3), channel_id=1, source_target_pairs={{0,4},{1,5},{2,6},{3,7},{4,0},{5,1},{6,2},{7,3},{8,12},{9,13},{10,... | collective-permute-start | bytes 1179656 | tf_op jit(solution)/shard_map/ppermute | solution.py:1071
  39.5 18.1 %collective-permute-start.16 = (bf16[4,64,768]{2,1,0:T(8,128)(2,1)}, bf16[4,64,768]{2,1,0:T(8,128)(2,1)}, u32[]{:S(2)}, u32[]{:S(2)}) collective-permute-start(bf16[4,64,768]{2,1,0:T(8,128)(2,1)} %pad_maximum_fusion.3), channel_id=1, source_target_pairs={{0,6},{1,7},{2,4},{3,5},{4,2},{5,3},{6,0},{7,1},{8,14},{9,15},{10,... | collective-permute-start | bytes 1179656 | tf_op jit(solution)/shard_map/ppermute | solution.py:1071
  59.2 14.5 %copy-start.4 = (s32[16,48,32]{1,2,0:T(8,128)S(1)}, s32[16,48,32]{1,2,0:T(8,128)}, u32[]{:S(2)}) copy-start(s32[16,48,32]{1,2,0:T(8,128)} %param.25) | copy-start | bytes 294916
  59.2 14.5 %copy-start.7 = (s32[16]{0:T(128)S(1)}, s32[16]{0:T(128)}, u32[]{:S(2)}) copy-start(s32[16]{0:T(128)} %refs_6_.4) | copy-start | bytes 196
  59.2 14.5 %collective-permute-start.17 = (bf16[16,64,768]{2,1,0:T(8,128)(2,1)S(1)}, bf16[16,64,768]{2,1,0:T(8,128)(2,1)S(1)}, u32[]{:S(2)}, u32[]{:S(2)}) collective-permute-start(bf16[16,64,768]{2,1,0:T(8,128)(2,1)S(1)} %pad_maximum_fusion.refs_1_), channel_id=1, source_target_pairs={{0,1},{1,0},{2,3},{3,2},{4,5},{5,4},{6,7},{7,6},{8,9},{9,8},{10,11... | collective-permute-start | bytes 4718600 | tf_op jit(solution)/shard_map/ppermute | solution.py:1071
  108.8 3.5 %collective-permute-start.18 = (bf16[16,64,768]{2,1,0:T(8,128)(2,1)S(1)}, bf16[16,64,768]{2,1,0:T(8,128)(2,1)S(1)}, u32[]{:S(2)}, u32[]{:S(2)}) collective-permute-start(bf16[16,64,768]{2,1,0:T(8,128)(2,1)S(1)} %get-tuple-element.150), channel_id=1, source_target_pairs={{0,1},{1,0},{2,3},{3,2},{4,5},{5,4},{6,7},{7,6},{8,9},{9,8},{10,11... | collective-permute-start | bytes 4718600 | tf_op jit(solution)/shard_map/ppermute | solution.py:1071
  114.8 21.0 %collective-permute-start.19 = (bf16[4,64,768]{2,1,0:T(8,128)(2,1)S(1)}, bf16[4,64,768]{2,1,0:T(8,128)(2,1)}, u32[]{:S(2)}, u32[]{:S(2)}) collective-permute-start(bf16[4,64,768]{2,1,0:T(8,128)(2,1)S(1)} %get-tuple-element.164), channel_id=1, source_target_pairs={{0,2},{1,3},{2,0},{3,1},{4,6},{5,7},{6,4},{7,5},{8,10},{9,11},{10,... | collective-permute-start | bytes 1179656 | tf_op jit(solution)/shard_map/ppermute | solution.py:1071
  116.2 19.6 %collective-permute-start.20 = (bf16[4,64,768]{2,1,0:T(8,128)(2,1)S(1)}, bf16[4,64,768]{2,1,0:T(8,128)(2,1)}, u32[]{:S(2)}, u32[]{:S(2)}) collective-permute-start(bf16[4,64,768]{2,1,0:T(8,128)(2,1)S(1)} %get-tuple-element.165), channel_id=1, source_target_pairs={{0,4},{1,5},{2,6},{3,7},{4,0},{5,1},{6,2},{7,3},{8,12},{9,13},{10,... | collective-permute-start | bytes 1179656 | tf_op jit(solution)/shard_map/ppermute | solution.py:1071
  117.4 18.5 %collective-permute-start.21 = (bf16[4,64,768]{2,1,0:T(8,128)(2,1)S(1)}, bf16[4,64,768]{2,1,0:T(8,128)(2,1)S(1)}, u32[]{:S(2)}, u32[]{:S(2)}) collective-permute-start(bf16[4,64,768]{2,1,0:T(8,128)(2,1)S(1)} %get-tuple-element.166), channel_id=1, source_target_pairs={{0,6},{1,7},{2,4},{3,5},{4,2},{5,3},{6,0},{7,1},{8,14},{9,15},{10,... | collective-permute-start | bytes 1179656 | tf_op jit(solution)/shard_map/ppermute | solution.py:1071
  136.6 2.4 %collective-permute-start.22 = (bf16[16,64,384]{2,1,0:T(8,128)(2,1)S(1)}, bf16[16,64,384]{2,1,0:T(8,128)(2,1)}, u32[]{:S(2)}, u32[]{:S(2)}) collective-permute-start(bf16[16,64,384]{2,1,0:T(8,128)(2,1)S(1)} %get-tuple-element.176), channel_id=1, source_target_pairs={{0,1},{1,0},{2,3},{3,2},{4,5},{5,4},{6,7},{7,6},{8,9},{9,8},{10,11... | collective-permute-start | bytes 2359304 | tf_op jit(solution)/shard_map/ppermute | solution.py:1071
  139.0 6.3 %copy-start.10 = (f32[1536,256]{1,0:T(8,128)S(1)}, f32[1536,256]{1,0:T(8,128)}, u32[]{:S(2)}) copy-start(f32[1536,256]{1,0:T(8,128)} %copy-done.9) | copy-start | bytes 4718596
  140.6 16.9 %collective-permute-start.23 = (bf16[2,64,768]{2,1,0:T(8,128)(2,1)S(1)}, bf16[2,64,768]{2,1,0:T(8,128)(2,1)S(1)}, u32[]{:S(2)}, u32[]{:S(2)}) collective-permute-start(bf16[2,64,768]{2,1,0:T(8,128)(2,1)S(1)} %get-tuple-element.181), channel_id=1, source_target_pairs={{0,8},{1,9},{2,10},{3,11},{4,12},{5,13},{6,14},{7,15},{8,0},{9,1},... | collective-permute-start | bytes 589832 | tf_op jit(solution)/shard_map/ppermute | solution.py:1071
  141.8 15.7 %collective-permute-start.24 = (bf16[4,64,384]{2,1,0:T(8,128)(2,1)S(1)}, bf16[4,64,384]{2,1,0:T(8,128)(2,1)S(1)}, u32[]{:S(2)}, u32[]{:S(2)}) collective-permute-start(bf16[4,64,384]{2,1,0:T(8,128)(2,1)S(1)} %get-tuple-element.182), channel_id=1, source_target_pairs={{0,2},{1,3},{2,0},{3,1},{4,6},{5,7},{6,4},{7,5},{8,10},{9,11},{10,... | collective-permute-start | bytes 589832 | tf_op jit(solution)/shard_map/ppermute | solution.py:1071
  143.5 14.0 %collective-permute-start.25 = (bf16[4,64,384]{2,1,0:T(8,128)(2,1)S(1)}, bf16[4,64,384]{2,1,0:T(8,128)(2,1)S(1)}, u32[]{:S(2)}, u32[]{:S(2)}) collective-permute-start(bf16[4,64,384]{2,1,0:T(8,128)(2,1)S(1)} %get-tuple-element.183), channel_id=1, source_target_pairs={{0,4},{1,5},{2,6},{3,7},{4,0},{5,1},{6,2},{7,3},{8,12},{9,13},{10,... | collective-permute-start | bytes 589832 | tf_op jit(solution)/shard_map/ppermute | solution.py:1071
  144.4 13.1 %collective-permute-start.26 = (bf16[4,64,384]{2,1,0:T(8,128)(2,1)S(1)}, bf16[4,64,384]{2,1,0:T(8,128)(2,1)S(1)}, u32[]{:S(2)}, u32[]{:S(2)}) collective-permute-start(bf16[4,64,384]{2,1,0:T(8,128)(2,1)S(1)} %get-tuple-element.184), channel_id=1, source_target_pairs={{0,6},{1,7},{2,4},{3,5},{4,2},{5,3},{6,0},{7,1},{8,14},{9,15},{10,... | collective-permute-start | bytes 589832 | tf_op jit(solution)/shard_map/ppermute | solution.py:1071
  158.3 3.0 %collective-permute-start.28 = (bf16[16,64,256]{2,1,0:T(8,128)(2,1)S(1)}, bf16[16,64,256]{2,1,0:T(8,128)(2,1)S(1)}, u32[]{:S(2)}, u32[]{:S(2)}) collective-permute-start(bf16[16,64,256]{2,1,0:T(8,128)(2,1)S(1)} %get-tuple-element.190), channel_id=1, source_target_pairs={{0,1},{1,0},{2,3},{3,2},{4,5},{5,4},{6,7},{7,6},{8,9},{9,8},{10,11... | collective-permute-start | bytes 1572872 | tf_op jit(solution)/shard_map/ppermute | solution.py:1071
  159.4 5.6 %collective-permute-start.27 = (bf16[2,64,384]{2,1,0:T(8,128)(2,1)S(1)}, bf16[2,64,384]{2,1,0:T(8,128)(2,1)S(1)}, u32[]{:S(2)}, u32[]{:S(2)}) collective-permute-start(bf16[2,64,384]{2,1,0:T(8,128)(2,1)S(1)} %get-tuple-element.248), channel_id=1, source_target_pairs={{0,8},{1,9},{2,10},{3,11},{4,12},{5,13},{6,14},{7,15},{8,0},{9,1},... | collective-permute-start | bytes 294920 | tf_op jit(solution)/shard_map/ppermute | solution.py:1071
  161.5 5.7 %collective-permute-start.30 = (bf16[4,64,256]{2,1,0:T(8,128)(2,1)S(1)}, bf16[4,64,256]{2,1,0:T(8,128)(2,1)S(1)}, u32[]{:S(2)}, u32[]{:S(2)}) collective-permute-start(bf16[4,64,256]{2,1,0:T(8,128)(2,1)S(1)} %get-tuple-element.243), channel_id=1, source_target_pairs={{0,2},{1,3},{2,0},{3,1},{4,6},{5,7},{6,4},{7,5},{8,10},{9,11},{10,... | collective-permute-start | bytes 393224 | tf_op jit(solution)/shard_map/ppermute | solution.py:1071
  162.8 6.4 %collective-permute-start.31 = (bf16[4,64,256]{2,1,0:T(8,128)(2,1)S(1)}, bf16[4,64,256]{2,1,0:T(8,128)(2,1)S(1)}, u32[]{:S(2)}, u32[]{:S(2)}) collective-permute-start(bf16[4,64,256]{2,1,0:T(8,128)(2,1)S(1)} %get-tuple-element.242), channel_id=1, source_target_pairs={{0,4},{1,5},{2,6},{3,7},{4,0},{5,1},{6,2},{7,3},{8,12},{9,13},{10,... | collective-permute-start | bytes 393224 | tf_op jit(solution)/shard_map/ppermute | solution.py:1071
  164.1 7.1 %collective-permute-start.32 = (bf16[4,64,256]{2,1,0:T(8,128)(2,1)S(1)}, bf16[4,64,256]{2,1,0:T(8,128)(2,1)S(1)}, u32[]{:S(2)}, u32[]{:S(2)}) collective-permute-start(bf16[4,64,256]{2,1,0:T(8,128)(2,1)S(1)} %get-tuple-element.241), channel_id=1, source_target_pairs={{0,6},{1,7},{2,4},{3,5},{4,2},{5,3},{6,0},{7,1},{8,14},{9,15},{10,... | collective-permute-start | bytes 393224 | tf_op jit(solution)/shard_map/ppermute | solution.py:1071
  171.2 4.9 %collective-permute-start.33 = (bf16[2,64,256]{2,1,0:T(8,128)(2,1)S(1)}, bf16[2,64,256]{2,1,0:T(8,128)(2,1)S(1)}, u32[]{:S(2)}, u32[]{:S(2)}) collective-permute-start(bf16[2,64,256]{2,1,0:T(8,128)(2,1)S(1)} %get-tuple-element.254), channel_id=1, source_target_pairs={{0,8},{1,9},{2,10},{3,11},{4,12},{5,13},{6,14},{7,15},{8,0},{9,1},... | collective-permute-start | bytes 196616 | tf_op jit(solution)/shard_map/ppermute | solution.py:1071
  172.5 10.0 %collective-permute-start.29 = (bf16[1,64,1152]{2,1,0:T(8,128)(2,1)S(1)}, bf16[1,64,1152]{2,1,0:T(8,128)(2,1)S(1)}, u32[]{:S(2)}, u32[]{:S(2)}) collective-permute-start(bf16[1,64,1152]{2,1,0:T(8,128)(2,1)S(1)} %pad_maximum_fusion.6), channel_id=1, source_target_pairs={{0,16},{1,17},{2,18},{3,19},{4,20},{5,21},{6,22},{7,23},{8,24},{9,... | collective-permute-start | bytes 442376 | tf_op jit(solution)/shard_map/ppermute | solution.py:1071
  176.1 10.7 %collective-permute-start.34 = (bf16[1,64,256]{2,1,0:T(8,128)(2,1)S(1)}, bf16[1,64,256]{2,1,0:T(8,128)(2,1)S(1)}, u32[]{:S(2)}, u32[]{:S(2)}) collective-permute-start(bf16[1,64,256]{2,1,0:T(8,128)(2,1)S(1)} %fusion.15), channel_id=1, source_target_pairs={{0,16},{1,17},{2,18},{3,19},{4,20},{5,21},{6,22},{7,23},{8,24},{9,... | collective-permute-start | bytes 98312 | tf_op jit(solution)/shard_map/ppermute | solution.py:1071
  189.1 1.4 collective-permute-start.35
  191.3 3.9 %collective-permute-start.36 = (f32[48,128]{1,0:T(8,128)S(1)}, f32[48,128]{1,0:T(8,128)S(1)}, u32[]{:S(2)}, u32[]{:S(2)}) collective-permute-start(f32[48,128]{1,0:T(8,128)S(1)} %pad_maximum_fusion.12), channel_id=1, source_target_pairs={{0,4},{1,5},{2,6},{3,7},{4,0},{5,1},{6,2},{7,3},{8,12},{9,13},{10,... | collective-permute-start | bytes 73736 | tf_op jit(solution)/shard_map/ppermute | solution.py:1071
  192.5 3.8 %collective-permute-start.37 = (f32[48,128]{1,0:T(8,128)S(1)}, f32[48,128]{1,0:T(8,128)S(1)}, u32[]{:S(2)}, u32[]{:S(2)}) collective-permute-start(f32[48,128]{1,0:T(8,128)S(1)} %pad_maximum_fusion.12), channel_id=1, source_target_pairs={{0,2},{1,3},{2,0},{3,1},{4,6},{5,7},{6,4},{7,5},{8,10},{9,11},{10,... | collective-permute-start | bytes 73736 | tf_op jit(solution)/shard_map/ppermute | solution.py:1071
  193.9 4.7 %collective-permute-start.38 = (f32[48,128]{1,0:T(8,128)S(1)}, f32[48,128]{1,0:T(8,128)S(1)}, u32[]{:S(2)}, u32[]{:S(2)}) collective-permute-start(f32[48,128]{1,0:T(8,128)S(1)} %pad_maximum_fusion.12), channel_id=1, source_target_pairs={{0,6},{1,7},{2,4},{3,5},{4,2},{5,3},{6,0},{7,1},{8,14},{9,15},{10,... | collective-permute-start | bytes 73736 | tf_op jit(solution)/shard_map/ppermute | solution.py:1071
  199.4 4.4 %collective-permute-start.39 = (f32[48,128]{1,0:T(8,128)S(1)}, f32[48,128]{1,0:T(8,128)S(1)}, u32[]{:S(2)}, u32[]{:S(2)}) collective-permute-start(f32[48,128]{1,0:T(8,128)S(1)} %pad_maximum_fusion.11), channel_id=1, source_target_pairs={{0,8},{1,9},{2,10},{3,11},{4,12},{5,13},{6,14},{7,15},{8,0},{9,1},... | collective-permute-start | bytes 73736 | tf_op jit(solution)/shard_map/ppermute | solution.py:1071
  199.4 5.0 %collective-permute-start.40 = (f32[48,128]{1,0:T(8,128)S(1)}, f32[48,128]{1,0:T(8,128)S(1)}, u32[]{:S(2)}, u32[]{:S(2)}) collective-permute-start(f32[48,128]{1,0:T(8,128)S(1)} %pad_maximum_fusion.11), channel_id=1, source_target_pairs={{0,16},{1,17},{2,18},{3,19},{4,20},{5,21},{6,22},{7,23},{8,24},{9,... | collective-permute-start | bytes 73736 | tf_op jit(solution)/shard_map/ppermute | solution.py:1071
  202.7 5.6 %collective-permute-start.41 = (f32[48,128]{1,0:T(8,128)S(1)}, f32[48,128]{1,0:T(8,128)S(1)}, u32[]{:S(2)}, u32[]{:S(2)}) collective-permute-start(f32[48,128]{1,0:T(8,128)S(1)} %pad_maximum_fusion.11), channel_id=1, source_target_pairs={{0,24},{1,25},{2,26},{3,27},{4,28},{5,29},{6,30},{7,31},{8,16},{9,... | collective-permute-start | bytes 73736 | tf_op jit(solution)/shard_map/ppermute | solution.py:1071
  (12 other events, 17.4 us)

commit v3 on v2

--- a/solution.py
+++ b/solution.py
@@ -19,6 +19,7 @@
 CTX = 96
 VOCAB = 1024
 GROUP = 4
+WIDE_GROUP = 8
 ROWS = GROUP * CTX
 HALF = D // 2
 VMEM_BYTES = 24 * 1024 * 1024
@@ -178,9 +179,10 @@
 def attend_forward(step, hidden, gain_row, weight_ref, valid_ref, bias_ref, masks, refs):
     middle_ref, qkv_ref, mix_ref, chance_ref = refs
     queries = chance_ref.shape[3] // (HEADS // 2)
+    group = hidden.shape[0] // CTX
     normed = (hidden * inverse_rms(hidden) * gain_row).astype(jnp.bfloat16)
     qkv_ref[...] = dot_nn(normed, weight_ref[:, 0 : 3 * D]).astype(jnp.bfloat16)
-    units = [(sample, side) for sample in range(GROUP) for side in range(2)]
+    units = [(sample, side) for sample in range(group) for side in range(2)]
     scores = []
     for sample, side in units:
         rows = slice(sample * CTX, (sample + 1) * CTX)
@@ -188,7 +190,7 @@
         spread = expand_heads(qkv_ref[tail, half_of(0, side)], masks)
         scores.append(dot_nt(qkv_ref[rows, half_of(1, side)], spread))
     for (sample, side), score in zip(units, scores):
-        score = score + bias_ref[valid_ref[step * GROUP + sample]]
+        score = score + bias_ref[valid_ref[step * group + sample]]
         peak = jnp.max(score, axis=0, keepdims=True)
         exponent = jnp.exp2((score - peak) * (score_scale * log2_e))
         total = jnp.sum(exponent, axis=0, keepdims=True)
@@ -216,7 +218,7 @@
     for part in range(FF // D):
         columns = slice(part * D, (part + 1) * D)
         inner = dot_nn(normed, weight_ref[:, columns])
-        for sample in range(GROUP):
+        for sample in range(middle.shape[0] // CTX):
             rows = slice(sample * CTX, (sample + 1) * CTX)
             active, slope = gelu_parts(inner[rows])
             inner_ref[rows, columns] = active.astype(jnp.bfloat16)
@@ -227,16 +229,16 @@
 def feed_back(here, upstream, middle, gain_row, weight_ref, slope_ref, refs):
     normed_ref, dinner_ref, dout_ref = refs
     dout = upstream.astype(jnp.bfloat16)
-    dout_ref[here(0, ROWS), :] = dout
+    dout_ref[here(0, middle.shape[0]), :] = dout
     inverse = inverse_rms(middle)
-    normed_ref[here(0, ROWS), :] = (middle * inverse * gain_row).astype(jnp.bfloat16)
+    normed_ref[here(0, middle.shape[0]), :] = (middle * inverse * gain_row).astype(jnp.bfloat16)
     for part in range(FF // D):
         columns = slice(part * D, (part + 1) * D)
         dact = dot_nn(dout, weight_ref[:, FF + part * D : FF + (part + 1) * D])
-        dinner_ref[here(0, ROWS), columns] = (
+        dinner_ref[here(0, middle.shape[0]), columns] = (
             dact * slope_ref[:, columns].astype(jnp.float32)
         ).astype(jnp.bfloat16)
-    dnormed = dot_nt(dinner_ref[here(0, ROWS), :], weight_ref[:, 0:FF])
+    dnormed = dot_nt(dinner_ref[here(0, middle.shape[0]), :], weight_ref[:, 0:FF])
     through, gain_part = rms_back(middle, inverse, gain_row, dnormed)
     return upstream + through, gain_part
 
@@ -244,13 +246,14 @@
 def attend_back(step, here, saved, dmiddle, gain_row, weight_ref, masks, refs):
     hidden, qkv_ref, mix_ref, chance_ref = saved
     normed_ref, dmiddle_ref, dqkv_ref, mixes_ref = refs
+    group = hidden.shape[0] // CTX
     queries = chance_ref.shape[3] // (HEADS // 2)
-    short = here(0, GROUP * queries, queries)
+    short = here(0, group * queries, queries)
     dattend = dmiddle.astype(jnp.bfloat16)
     dmiddle_ref[short, :] = dattend
     mixes_ref[short, :] = mix_ref[...]
     dmix = dot_nt(dattend, weight_ref[:, 3 * D : 4 * D]).astype(jnp.bfloat16)
-    units = [(sample, side) for sample in range(GROUP) for side in range(2)]
+    units = [(sample, side) for sample in range(group) for side in range(2)]
     slopes, dchances, dscores = [], [], []
     for sample, side in units:
         rows = slice(sample * CTX, (sample + 1) * CTX)
@@ -282,13 +285,13 @@
         dqkv_ref[there, half_of(1, side)] = dkeys.astype(jnp.bfloat16)
         dqkv_ref[there, half_of(2, side)] = dvalues.astype(jnp.bfloat16)
     inverse = inverse_rms(hidden)
-    normed_ref[here(0, ROWS), :] = (hidden * inverse * gain_row).astype(jnp.bfloat16)
-    dnormed = dot_nt(dqkv_ref[here(0, ROWS), :], weight_ref[:, 0 : 3 * D])
+    normed_ref[here(0, hidden.shape[0]), :] = (hidden * inverse * gain_row).astype(jnp.bfloat16)
+    dnormed = dot_nt(dqkv_ref[here(0, hidden.shape[0]), :], weight_ref[:, 0 : 3 * D])
     through, gain_part = rms_back(hidden, inverse, gain_row, dnormed)
     if queries < CTX:
         nothing = jnp.zeros((CTX - queries, D), jnp.float32)
         pieces = []
-        for sample in range(GROUP):
+        for sample in range(group):
             pieces = pieces + [nothing, dmiddle[sample * queries : (sample + 1) * queries]]
         dmiddle = jnp.concatenate(pieces, axis=0)
     return dmiddle + through, gain_part
@@ -408,7 +411,7 @@
     normed_ref = normed_two_long.at[0:tokens]
     dinner_ref = dinner_long.at[0:tokens]
     dout_ref = dout_long.at[0:tokens]
-    groups = source_ref.shape[0] // ROWS
+    groups = source_ref.shape[0] // (WIDE_GROUP * CTX)
     masks = head_masks()
     gain_att = gains_ref[LAYERS - 1 : LAYERS, :]
     gain_before = gains_ref[2 * LAYERS - 2 : 2 * LAYERS - 1, :]
@@ -433,7 +436,7 @@
     )
 
     def rows_of(group, unit=CTX):
-        return pl.ds(pl.multiple_of(group * (GROUP * unit), GROUP * unit), GROUP * unit)
+        return pl.ds(pl.multiple_of(group * (WIDE_GROUP * unit), WIDE_GROUP * unit), WIDE_GROUP * unit)
 
     def forward(group, carry):
         rows, short = rows_of(group), rows_of(group, SEG)
@@ -457,7 +460,7 @@
                 middle_two_ref.at[short],
                 qkv_ref.at[rows],
                 mix_ref.at[short],
-                chance_ref.at[pl.ds(group * GROUP, GROUP)],
+                chance_ref.at[pl.ds(group * WIDE_GROUP, WIDE_GROUP)],
             ),
         )
         return carry
@@ -542,7 +545,7 @@
         rows, short = rows_of(group), rows_of(group, SEG)
 
         def here(start, length, unit=CTX):
-            return pl.ds(pl.multiple_of(group * (GROUP * unit) + start, 16), length)
+            return pl.ds(pl.multiple_of(group * (WIDE_GROUP * unit) + start, 16), length)
 
         dentry, gain_part = attend_back(
             group,
@@ -551,7 +554,7 @@
                 entry_ref[rows, :],
                 qkv_ref.at[rows],
                 mix_ref.at[short],
-                chance_ref.at[pl.ds(group * GROUP, GROUP)],
+                chance_ref.at[pl.ds(group * WIDE_GROUP, WIDE_GROUP)],
             ),
             dmiddle_ref[short, :],
             gain_att,
@@ -592,7 +595,7 @@
 def block_outs(own, widths):
     shape = jax.ShapeDtypeStruct
     blocks = own.shape[:2] + (sum(widths),)
-    return [shape(blocks, jnp.bfloat16), shape(blocks, jnp.float32)]
+    return [shape(blocks, jnp.bfloat16)] * 2
 
 
 def run_middle(widths, mesh_plan, source, own, other, targets, gains, valid, horizon, core):
@@ -894,17 +897,41 @@
     return -(-(late_row(widths) + -(-late // LANES)) // 8) * 8
 
 
-def early_kernel(widths, *refs):
-    raw_ref, masters, row_refs = refs[0], refs[1:7], refs[7:13]
-    gains_at, loss_ref, count_ref, packet_ref = refs[13:15], refs[15], refs[16], refs[17]
-    plan, _ = matrix_plan(widths)
-    chosen = [item for item in matrix_list() if item not in LATE]
-    inner, entries, outer = square_sums(raw_ref[...], chosen, plan, 0)
+def first_kernel(*refs):
+    masters, row_refs, row_ref = refs[0:6], refs[6:12], refs[12]
     weights, row_sums = [], []
     for which, layer in matrix_list():
         master = masters[which][layer] if which < 4 else masters[which][...]
         weights.append(whole_sum(master * master))
         row_sums.append(whole_sum(old_row(row_refs, which, layer)))
+    nothing = lambda count: [jnp.zeros((1, count), jnp.float32)]
+    pieces = nothing(2) + weights + nothing(MATRICES) + row_sums
+    row_ref[...] = jnp.concatenate(pieces + nothing(LANES - 2 - 3 * MATRICES), axis=1)
+
+
+def run_first(masters, rows):
+    vmem = pl.BlockSpec(memory_space=pltpu.VMEM)
+    return pl.pallas_call(
+        first_kernel,
+        in_specs=[vmem] * 12,
+        out_specs=vmem,
+        out_shape=jax.ShapeDtypeStruct((1, LANES), jnp.float32),
+        name="first_statistics",
+    )(*masters, *rows)
+
+
+def early_kernel(widths, *refs):
+    raw_ref, row_ref, gains_at, loss_ref, count_ref, packet_ref = (
+        refs[0],
+        refs[1],
+        refs[2:4],
+        refs[4],
+        refs[5],
+        refs[6],
+    )
+    plan, _ = matrix_plan(widths)
+    chosen = [item for item in matrix_list() if item not in LATE]
+    inner, entries, outer = square_sums(raw_ref[...], chosen, plan, 0)
     packet_ref[...] = jnp.zeros_like(packet_ref)
     packet_ref[0:INNER_ROWS, 0 : inner.shape[1]] = inner[0:INNER_ROWS, :]
     last, one = [ref[...] for ref in gains_at]
@@ -912,11 +939,12 @@
         [jnp.zeros((1, D), jnp.float32), one[0:1], last[2:3], one[1:2], last[3:4], last[0:2]],
         axis=0,
     )
-    scalars = [loss_ref[...], count_ref[...]] + weights + entries + row_sums
-    scalars.append(jnp.zeros((1, LANES - len(scalars)), jnp.float32))
+    nothing = lambda count: [jnp.zeros((1, count), jnp.float32)]
+    scalars = [loss_ref[...], count_ref[...]] + nothing(MATRICES) + entries
+    scalars = scalars + nothing(LANES - 2 - 2 * MATRICES)
     at = INNER_ROWS
     packet_ref[at : at + 7, :] = gain[:, 0:LANES]
-    packet_ref[at + 7 : at + 8, :] = jnp.concatenate(scalars, axis=1)
+    packet_ref[at + 7 : at + 8, :] = row_ref[...] + jnp.concatenate(scalars, axis=1)
     packet_ref[at + 8 : at + 15, :] = gain[:, LANES:]
     store_row(packet_ref, EDGE, outer)
 
@@ -935,9 +963,9 @@
     store_row(packet_ref, late_row(widths), outer)
 
 
-def run_early(widths, raw, masters, rows, gain_parts, loss, count):
+def run_early(widths, raw, row, gain_parts, loss, count):
     vmem = pl.BlockSpec(memory_space=pltpu.VMEM)
-    operands = [raw] + masters + rows + gain_parts + [loss, count]
+    operands = [raw, row] + gain_parts + [loss, count]
     return pl.pallas_call(
         functools.partial(early_kernel, widths),
         in_specs=[vmem] * len(operands),
@@ -1222,9 +1250,16 @@
     back_shared = (gains, core)
 
     count = len(gather_steps)
+    flat = lambda item: item if item.ndim == 2 else item.reshape(1, -1)
+    inner = [flat(item) for item in (qkv_rows, out_rows, up_rows, down_cols, embed_cols, head_rows)]
+    outer = [flat(item) for item in (qkv_cols, out_cols, up_cols, down_rows, embed_rows, head_cols)]
+    row_stats = [inner[at] if ROW_IS_INNER[at] else outer[at] for at in range(6)]
+    first_row = run_first(masters, row_stats)
     for at in range(count - 1):
         for chunk in chunks:
             chunk.send()
+        if at == 0:
+            first.others, first_row = tie(first.others, first_row)
         for chunk in chunks[: 2 if at == count - 2 else 3]:
             chunk.join()
             if at == count - 3 and chunk is first:
@@ -1234,14 +1269,14 @@
     held, other, second.held = tie(first.held, other, second.held)
     second.send()
     kept = [run_forward(0, chunk_widths[0], mesh_plan, latent_rows, held, other, *shared)]
-    middle, (other,), third.others = tie(kept[0][1], second.others, third.others)
-    third.join()
-    middle, third.held = tie(middle, third.held)
-    third.send()
+    middle, (other,) = tie(kept[0][1], second.others)
     kept.append(
         run_forward(1, chunk_widths[1], mesh_plan, middle, second.held, other, *shared)
     )
-    middle, (other,) = tie(kept[1][1], third.others)
+    middle, third.others = tie(kept[1][1], third.others)
+    third.join()
+    third.send()
+    (other,) = third.others
     dmiddle, sent, held, gain_middle, loss, counted = run_middle(
         chunk_widths[2],
         mesh_plan,
@@ -1292,12 +1327,8 @@
         early.join()
     raw_early = early.kept[0]
 
-    flat = lambda item: item if item.ndim == 2 else item.reshape(1, -1)
-    inner = [flat(item) for item in (qkv_rows, out_rows, up_rows, down_cols, embed_cols, head_rows)]
-    outer = [flat(item) for item in (qkv_cols, out_cols, up_cols, down_rows, embed_rows, head_cols)]
-    row_stats = [inner[at] if ROW_IS_INNER[at] else outer[at] for at in range(6)]
     packet = run_early(
-        widths, raw_early, masters, row_stats, [gain_middle, gain_one], loss, counted
+        widths, raw_early, first_row, [gain_middle, gain_one], loss, counted
     )
     while zero.at < count:
         zero.join()

time: 213 us -> 203 us (0.953)
  other arithmetic: 17.5 us -> 14.1 us
  starting transfers between devices: 50.3 us -> 47.7 us
  local copies, waits for them, and re-layouts: 7.07 us -> 4.93 us
    pallas_call x1, Pallas kernels: 31.9 us -> 28.2 us  [run_middle(): pl.pallas_call(functools.partial(middle_kernel, widths, mesh_plan), in_sp...]
    ppermute x42, starting transfers between devices: 50.3 us -> 47.7 us  [swap(): lax.ppermute(value, ('dp', 'fsdp'), [(place, place ^ mask) for place in r...]
    unnamed x36 -> x34, local copies, waits for them, and re-layouts: 7.07 us -> 4.93 us
    select_n x9, other arithmetic: 4.11 us -> 1.98 us  [join(): jnp.where(upper, pieces[place ^ 1 << at], pieces[place])]
    ppermute x42, waiting for transfers between devices: 41.8 us -> 39.7 us  [swap(): lax.ppermute(value, ('dp', 'fsdp'), [(place, place ^ mask) for place in r...]
  transfers between devices with their start and end apart: 42 -> 42, of which waited for: 22 -> 21; matrix products, arithmetic and copies ran while one was open for 4% -> 3% of each run, Pallas kernels for 26% -> 29%
where the time goes in v3:
time: 203 us; the launch traced here: 200 us
  Pallas kernels  92.7 us (46%)
  starting transfers between devices  47.7 us (23%)
  waiting for transfers between devices  39.7 us (20%)
  other arithmetic  14.1 us (7%)
  local copies, waits for them, and re-layouts  4.93 us (2%)
    ppermute x42, starting transfers between devices, swap(): lax.ppermute(value, ('dp', 'fsdp'), [(place, place ^ mask) for place in r...  47.7 us
    ppermute x42, waiting for transfers between devices, swap(): lax.ppermute(value, ('dp', 'fsdp'), [(place, place ^ mask) for place in r...  39.7 us
    pallas_call x1, Pallas kernels, run_middle(): pl.pallas_call(functools.partial(middle_kernel, widths, mesh_plan), in_sp...  28.2 us
    pallas_call x2, Pallas kernels, run_backward(): pl.pallas_call(functools.partial(backward_kernel, layer, widths, mesh_pla...  27.3 us
    pallas_call x2, Pallas kernels, run_forward(): pl.pallas_call(functools.partial(forward_kernel, layer, widths, mesh_plan...  25.2 us
    add x5, other arithmetic, pick(): total = part if total is None else total + part  6.63 us
    unnamed x34, local copies, waits for them, and re-layouts  4.93 us
  transfers between devices with their start and end apart: 42, of which 21 were waited for; matrix products, arithmetic and copies ran while one was open for 3% of the time, Pallas kernels for 29%

profile of v3, /device:TPU:0, one launch (start us, length us, event | category | flops | bytes accessed | tf_op | source)
XLA Modules:
  0.0 200.4 jit_solution(14344057025805412418)
XLA Ops:
  0.7 1.8 pack.1
  2.5 4.0 %collective-permute-start = (bf16[1,64,256]{2,1,0:T(8,128)(2,1)}, bf16[1,64,256]{2,1,0:T(8,128)(2,1)S(1)}, u32[]{:S(2)}, u32[]{:S(2)}) collective-permute-start(bf16[1,64,256]{2,1,0:T(8,128)(2,1)} %bitcast.127), channel_id=1, source_target_pairs={{0,16},{1,17},{2,18},{3,19},{4,20},{5,21},{6,22},{7,23},{8,24},{9,... | collective-permute-start | bytes 98312 | tf_op jit(solution)/shard_map/ppermute | solution.py:1099
  6.6 2.9 %collective-permute-start.2 = (bf16[1,64,768]{2,1,0:T(8,128)(2,1)}, bf16[1,64,768]{2,1,0:T(8,128)(2,1)S(1)}, u32[]{:S(2)}, u32[]{:S(2)}) collective-permute-start(bf16[1,64,768]{2,1,0:T(8,128)(2,1)} %bitcast.125), channel_id=1, source_target_pairs={{0,16},{1,17},{2,18},{3,19},{4,20},{5,21},{6,22},{7,23},{8,24},{9,... | collective-permute-start | bytes 294920 | tf_op jit(solution)/shard_map/ppermute | solution.py:1099
  9.5 1.8 first_statistics.1.refs_1_
  12.1 1.6 collective-permute-start.1
  13.7 1.6 collective-permute-done.7
  16.2 1.7 collective-permute-done.1
  18.0 2.5 %collective-permute-start.3 = (bf16[4,64,256]{2,1,0:T(8,128)(2,1)S(1)}, bf16[4,64,256]{2,1,0:T(8,128)(2,1)S(1)}, u32[]{:S(2)}, u32[]{:S(2)}) collective-permute-start(bf16[4,64,256]{2,1,0:T(8,128)(2,1)S(1)} %pad_maximum_fusion.7), channel_id=1, source_target_pairs={{0,6},{1,7},{2,4},{3,5},{4,2},{5,3},{6,0},{7,1},{8,14},{9,15},{10,... | collective-permute-start | bytes 393224 | tf_op jit(solution)/shard_map/ppermute | solution.py:1099
  21.6 1.6 collective-permute-start.10
  23.2 1.5 collective-permute-start.11
  25.4 2.4 %collective-permute-start.9 = (bf16[4,64,384]{2,1,0:T(8,128)(2,1)S(1)}, bf16[4,64,384]{2,1,0:T(8,128)(2,1)S(1)}, u32[]{:S(2)}, u32[]{:S(2)}) collective-permute-start(bf16[4,64,384]{2,1,0:T(8,128)(2,1)S(1)} %pad_maximum_fusion.5), channel_id=1, source_target_pairs={{0,6},{1,7},{2,4},{3,5},{4,2},{5,3},{6,0},{7,1},{8,14},{9,15},{10,... | collective-permute-start | bytes 589832 | tf_op jit(solution)/shard_map/ppermute | solution.py:1099
  29.1 3.4 %collective-permute-done.10 = bf16[4,64,384]{2,1,0:T(8,128)(2,1)S(1)} collective-permute-done((bf16[4,64,384]{2,1,0:T(8,128)(2,1)S(1)}, bf16[4,64,384]{2,1,0:T(8,128)(2,1)S(1)}, u32[]{:S(2)}, u32[]{:S(2)}) %collective-permute-start.10) | collective-permute-done | bytes 196640 | tf_op jit(solution)/shard_map/ppermute | solution.py:1099
  32.5 2.3 %collective-permute-done.11 = bf16[4,64,384]{2,1,0:T(8,128)(2,1)S(1)} collective-permute-done((bf16[4,64,384]{2,1,0:T(8,128)(2,1)S(1)}, bf16[4,64,384]{2,1,0:T(8,128)(2,1)S(1)}, u32[]{:S(2)}, u32[]{:S(2)}) %collective-permute-start.11) | collective-permute-done | bytes 196640 | tf_op jit(solution)/shard_map/ppermute | solution.py:1099
  36.7 1.5 collective-permute-start.15
  38.2 1.2 collective-permute-start.16
  39.5 11.0 %forward_part.2 = (f32[1536,256]{1,0:T(8,128)}, f32[1536,256]{1,0:T(8,128)}, bf16[1536,768]{1,0:T(8,128)(2,1)}, bf16[1536,256]{1,0:T(8,128)(2,1)}, bf16[16,2,96,...) custom-call(s32[16,32,96]{2,1,0:T(8,128)S(1)} %bitcast.104, bf16[16,64,256]{2,1,0:T(8,128)(2,1)S(1)} %pad_maximum_fusion.2.own_ref, ...), custom_call_target="tpu_custom_call" | custom-call | flops 2415919104 | bytes 9437184 | tf_op jit(solution)/shard_map/forward_part/pallas_call | solution.py:377
  50.4 14.3 %forward_part.3 = (f32[1536,256]{1,0:T(8,128)}, f32[1536,256]{1,0:T(8,128)}, bf16[1536,768]{1,0:T(8,128)(2,1)}, bf16[1536,256]{1,0:T(8,128)(2,1)}, bf16[16,2,96,...) custom-call(f32[1536,256]{1,0:T(8,128)} %get-tuple-element.138.sourc, ...), custom_call_target="tpu_custom_call" | custom-call | flops 2415919104 | bytes 9437184 | tf_op jit(solution)/shard_map/forward_part/pallas_call | solution.py:377
  65.2 3.4 %collective-permute-done.17.refs_2_ = bf16[16,64,768]{2,1,0:T(8,128)(2,1)S(1)} collective-permute-done((bf16[16,64,768]{2,1,0:T(8,128)(2,1)S(1)}, bf16[16,64,768]{2,1,0:T(8,128)(2,1)S(1)}, u32[]{:S(2)}, u32[]{:S(2)}) %collective-permute-start.17) | collective-permute-done | bytes 1572896 | tf_op jit(solution)/shard_map/ppermute | solution.py:1099
  69.7 28.2 %middle_part.1 = (f32[1536,256]{1,0:T(8,128)S(1)}, bf16[16,64,768]{2,1,0:T(8,128)(2,1)S(1)}, bf16[16,64,768]{2,1,0:T(8,128)(2,1)S(1)}, f32[4,256]{1,0:T(4,128)S(1)}, f32[1,1]{1,0:T(1,128)}, /*index=5*/f32[1,1]{1,0:T(1,128)}) custom-call(f32[1536,256]{1,0:T(8,128)S(1)} %copy-done.8, bf16[16,64,768]{2,1,0:T(8,128)(2,1)S(1)} %pad_maximum_fusion.refs_1_, ...), custom_call_target="tpu_custom_call" | custom-call | flops 19327352832 | bytes 18874368 | tf_op jit(solution)/shard_map/middle_part/pallas_call | solution.py:609
  99.8 3.4 %collective-permute-done.18 = bf16[16,64,768]{2,1,0:T(8,128)(2,1)} collective-permute-done((bf16[16,64,768]{2,1,0:T(8,128)(2,1)S(1)}, bf16[16,64,768]{2,1,0:T(8,128)(2,1)}, u32[]{:S(2)}, u32[]{:S(2)}) %collective-permute-start.18) | collective-permute-done | bytes 1572896 | tf_op jit(solution)/shard_map/ppermute | solution.py:1099
  103.2 2.8 %convert_add_fusion = (f32[1,4,64,768]{3,2,1,0:T(8,128)}, bf16[4,64,768]{2,1,0:T(8,128)(2,1)S(1)}, bf16[4,64,768]{2,1,0:T(8,128)(2,1)S(1)}, bf16[4,64,768]{2,1,0:T(8,128)(2,1)S(1)}) fusion(bf16[4,4,64,768]{3,2,1,0:T(8,128)(2,1)} %bitcast.12, s32[]{:T(128)S(6)} %select_n.333, bf16[4,4,64,768]{3,2,1,0:T(8,128)(2,1)S(1)} %bitcast.100, s32[]{:T(128)S(6)} %select_n.337, ...), kind=kLoop, calls=%fused_computation.5 | loop fusion | flops 2949120 | bytes 5111824 | tf_op jit(solution)/shard_map/add | solution.py:1164
  106.8 1.5 collective-permute-start.20
  108.3 1.2 collective-permute-start.21
  109.5 15.6 %backward_part.2 = (f32[1536,256]{1,0:T(8,128)S(1)}, bf16[16,64,384]{2,1,0:T(8,128)(2,1)S(1)}, bf16[16,64,384]{2,1,0:T(8,128)(2,1)S(1)}, f32[2,256]{1,0:T(2,128)S(1)}) custom-call(f32[1536,256]{1,0:T(8,128)} %get-tuple-element.148.refs_0_, bf16[1536,768]{1,0:T(8,128)(2,1)} %get-tuple-element.149.refs_1_, bf16[1536,256]{1,0:T(8,128)(2,1)} %get-tuple-element.150.refs_2_, ...), custom_call_target="tpu_custom_call" | custom-call | flops 7247757312 | bytes 14155776 | tf_op jit(solution)/shard_map/backward_part/pallas_call | solution.py:770
  126.9 2.4 %convert_add_fusion.2 = (f32[1,2,64,768]{3,2,1,0:T(8,128)}, bf16[2,64,768]{2,1,0:T(8,128)(2,1)S(1)}) fusion(f32[2,2,64,768]{3,2,1,0:T(8,128)} %bitcast.106, s32[]{:T(128)S(6)} %select_n.334, bf16[2,2,64,768]{3,2,1,0:T(8,128)(2,1)} %bitcast.19, bf16[2,2,64,768]{3,2,1,0:T(8,128)(2,1)} %bitcast.18, bf16[2,2,64,768]{3,2,1,0:T(8,128)(2,1)} %bitcast.17, ...), kind=kLoop, calls=%fused_computation.16 | loop fusion | flops 1277952 | bytes 2555912 | tf_op jit(solution)/shard_map/add | solution.py:1164
  129.3 1.4 fusion.7
  132.5 1.6 collective-permute-start.25
  134.8 11.7 %backward_part.3 = (bf16[16,64,256]{2,1,0:T(8,128)(2,1)S(1)}, bf16[16,64,256]{2,1,0:T(8,128)(2,1)S(1)}, f32[2,256]{1,0:T(2,128)S(1)}) custom-call(f32[1536,256]{1,0:T(8,128)} %get-tuple-element.167.refs_0_, bf16[1536,768]{1,0:T(8,128)(2,1)} %get-tuple-element.168.refs_1_, bf16[1536,256]{1,0:T(8,128)(2,1)} %get-tuple-element.169.refs_2_, ...), custom_call_target="tpu_custom_call" | custom-call | flops 4831838208 | bytes 12582912 | tf_op jit(solution)/shard_map/backward_part/pallas_call | solution.py:770
  149.2 1.6 collective-permute-start.27
  151.8 1.5 collective-permute-start.31
  153.3 1.2 collective-permute-start.32
  154.6 2.1 %collective-permute-done.30 = bf16[4,64,256]{2,1,0:T(8,128)(2,1)S(1)} collective-permute-done((bf16[4,64,256]{2,1,0:T(8,128)(2,1)S(1)}, bf16[4,64,256]{2,1,0:T(8,128)(2,1)S(1)}, u32[]{:S(2)}, u32[]{:S(2)}) %collective-permute-start.30) | collective-permute-done | bytes 131104 | tf_op jit(solution)/shard_map/ppermute | solution.py:1099
  156.7 1.4 collective-permute-done.31
  158.1 2.6 %collective-permute-done.32 = bf16[4,64,256]{2,1,0:T(8,128)(2,1)S(1)} collective-permute-done((bf16[4,64,256]{2,1,0:T(8,128)(2,1)S(1)}, bf16[4,64,256]{2,1,0:T(8,128)(2,1)S(1)}, u32[]{:S(2)}, u32[]{:S(2)}) %collective-permute-start.32) | collective-permute-done | bytes 131104 | tf_op jit(solution)/shard_map/ppermute | solution.py:1099
  161.4 2.5 %collective-permute-start.29 = (bf16[1,64,1152]{2,1,0:T(8,128)(2,1)S(1)}, bf16[1,64,1152]{2,1,0:T(8,128)(2,1)S(1)}, u32[]{:S(2)}, u32[]{:S(2)}) collective-permute-start(bf16[1,64,1152]{2,1,0:T(8,128)(2,1)S(1)} %pad_maximum_fusion.6), channel_id=1, source_target_pairs={{0,16},{1,17},{2,18},{3,19},{4,20},{5,21},{6,22},{7,23},{8,24},{9,... | collective-permute-start | bytes 442376 | tf_op jit(solution)/shard_map/ppermute | solution.py:1099
  163.8 1.6 collective-permute-done.33
  165.4 1.8 collective-permute-start.34
  167.2 3.9 %collective-permute-done.29 = bf16[1,64,1152]{2,1,0:T(8,128)(2,1)S(1)} collective-permute-done((bf16[1,64,1152]{2,1,0:T(8,128)(2,1)S(1)}, bf16[1,64,1152]{2,1,0:T(8,128)(2,1)S(1)}, u32[]{:S(2)}, u32[]{:S(2)}) %collective-permute-start.29) | collective-permute-done | bytes 147488 | tf_op jit(solution)/shard_map/ppermute | solution.py:1099
  171.9 3.2 %early_statistics.1.early_ref = f32[48,128]{1,0:T(8,128)} custom-call(f32[64,1152]{1,0:T(8,128)} %fusion.3.refs_0_.refs_1_, f32[1,128]{1,0:T(1,128)} %first_statistics.1.refs_1_, f32[4,256]{1,0:T(4,128)} %copy-done.1, f32[2,256]{1,0:T(2,128)} %copy-done.2, f32[1,1]{1,0:T(1,128)} %get-tuple-element.192.refs_4_, f32[1,1]{1,0:T(1,128)} %get-tuple-element.193.refs_5_), custom_call_target="tpu_custom_call" | custom-call | tf_op jit(solution)/shard_map/early_statistics/pallas_call | solution.py:969
  175.7 1.7 late_statistics.1
  177.4 1.4 collective-permute-done.35
  179.5 1.3 collective-permute-start.36
  180.8 1.4 collective-permute-start.37
  184.6 2.3 %collective-permute-done.38 = f32[48,128]{1,0:T(8,128)S(1)} collective-permute-done((f32[48,128]{1,0:T(8,128)S(1)}, f32[48,128]{1,0:T(8,128)S(1)}, u32[]{:S(2)}, u32[]{:S(2)}) %collective-permute-start.38) | collective-permute-done | bytes 24608 | tf_op jit(solution)/shard_map/ppermute | solution.py:1099
  187.7 2.7 %collective-permute-start.40 = (f32[48,128]{1,0:T(8,128)S(1)}, f32[48,128]{1,0:T(8,128)S(1)}, u32[]{:S(2)}, u32[]{:S(2)}) collective-permute-start(f32[48,128]{1,0:T(8,128)S(1)} %pad_maximum_fusion.11), channel_id=1, source_target_pairs={{0,16},{1,17},{2,18},{3,19},{4,20},{5,21},{6,22},{7,23},{8,24},{9,... | collective-permute-start | bytes 73736 | tf_op jit(solution)/shard_map/ppermute | solution.py:1099
  190.5 1.6 collective-permute-start.41
  192.5 3.6 %collective-permute-done.41 = f32[48,128]{1,0:T(8,128)S(1)} collective-permute-done((f32[48,128]{1,0:T(8,128)S(1)}, f32[48,128]{1,0:T(8,128)S(1)}, u32[]{:S(2)}, u32[]{:S(2)}) %collective-permute-start.41) | collective-permute-done | bytes 24608 | tf_op jit(solution)/shard_map/ppermute | solution.py:1099
  196.7 3.5 %update.1 = (f32[1,1]{1,0:T(1,128)}, f32[1,1]{1,0:T(1,128)}, f32[1,1]{1,0:T(1,128)}, f32[64,128]{1,0:T(8,128)}, f32[64,128]{1,0:T(8,128)}, /*index=5*/f32[1,128]...) custom-call(f32[48,128]{1,0:T(8,128)} %pad_maximum_fusion.10.refs_0_, ...), custom_call_target="tpu_custom_call" | custom-call | tf_op jit(solution)/shard_map/update/pallas_call | solution.py:1088
  (116 shorter events, 25.8 us)
Async XLA Ops:
  2.5 15.4 %copy-start.15 = (bf16[64,768]{1,0:T(8,128)(2,1)S(1)}, bf16[64,768]{1,0:T(8,128)(2,1)}, u32[]{:S(2)}) copy-start(bf16[64,768]{1,0:T(8,128)(2,1)} %get-tuple-element.131) | copy-start | bytes 294916
  2.5 8.8 %collective-permute-start = (bf16[1,64,256]{2,1,0:T(8,128)(2,1)}, bf16[1,64,256]{2,1,0:T(8,128)(2,1)S(1)}, u32[]{:S(2)}, u32[]{:S(2)}) collective-permute-start(bf16[1,64,256]{2,1,0:T(8,128)(2,1)} %bitcast.127), channel_id=1, source_target_pairs={{0,16},{1,17},{2,18},{3,19},{4,20},{5,21},{6,22},{7,23},{8,24},{9,... | collective-permute-start | bytes 98312 | tf_op jit(solution)/shard_map/ppermute | solution.py:1099
  6.6 8.7 %collective-permute-start.7 = (bf16[1,64,384]{2,1,0:T(8,128)(2,1)}, bf16[1,64,384]{2,1,0:T(8,128)(2,1)S(1)}, u32[]{:S(2)}, u32[]{:S(2)}) collective-permute-start(bf16[1,64,384]{2,1,0:T(8,128)(2,1)} %bitcast.126), channel_id=1, source_target_pairs={{0,16},{1,17},{2,18},{3,19},{4,20},{5,21},{6,22},{7,23},{8,24},{9,... | collective-permute-start | bytes 147464 | tf_op jit(solution)/shard_map/ppermute | solution.py:1099
  6.6 11.3 %collective-permute-start.2 = (bf16[1,64,768]{2,1,0:T(8,128)(2,1)}, bf16[1,64,768]{2,1,0:T(8,128)(2,1)S(1)}, u32[]{:S(2)}, u32[]{:S(2)}) collective-permute-start(bf16[1,64,768]{2,1,0:T(8,128)(2,1)} %bitcast.125), channel_id=1, source_target_pairs={{0,16},{1,17},{2,18},{3,19},{4,20},{5,21},{6,22},{7,23},{8,24},{9,... | collective-permute-start | bytes 294920 | tf_op jit(solution)/shard_map/ppermute | solution.py:1099
  12.1 5.8 %collective-permute-start.1 = (bf16[2,64,256]{2,1,0:T(8,128)(2,1)S(1)}, bf16[2,64,256]{2,1,0:T(8,128)(2,1)S(1)}, u32[]{:S(2)}, u32[]{:S(2)}) collective-permute-start(bf16[2,64,256]{2,1,0:T(8,128)(2,1)S(1)} %pad_maximum_fusion.9), channel_id=1, source_target_pairs={{0,8},{1,9},{2,10},{3,11},{4,12},{5,13},{6,14},{7,15},{8,0},{9,1},... | collective-permute-start | bytes 196616 | tf_op jit(solution)/shard_map/ppermute | solution.py:1099
  16.1 5.4 %collective-permute-start.8 = (bf16[2,64,384]{2,1,0:T(8,128)(2,1)S(1)}, bf16[2,64,384]{2,1,0:T(8,128)(2,1)S(1)}, u32[]{:S(2)}, u32[]{:S(2)}) collective-permute-start(bf16[2,64,384]{2,1,0:T(8,128)(2,1)S(1)} %pad_maximum_fusion.8), channel_id=1, source_target_pairs={{0,8},{1,9},{2,10},{3,11},{4,12},{5,13},{6,14},{7,15},{8,0},{9,1},... | collective-permute-start | bytes 294920 | tf_op jit(solution)/shard_map/ppermute | solution.py:1099
  18.0 7.4 %collective-permute-start.3 = (bf16[4,64,256]{2,1,0:T(8,128)(2,1)S(1)}, bf16[4,64,256]{2,1,0:T(8,128)(2,1)S(1)}, u32[]{:S(2)}, u32[]{:S(2)}) collective-permute-start(bf16[4,64,256]{2,1,0:T(8,128)(2,1)S(1)} %pad_maximum_fusion.7), channel_id=1, source_target_pairs={{0,6},{1,7},{2,4},{3,5},{4,2},{5,3},{6,0},{7,1},{8,14},{9,15},{10,... | collective-permute-start | bytes 393224 | tf_op jit(solution)/shard_map/ppermute | solution.py:1099
  20.5 7.8 %collective-permute-start.4 = (bf16[4,64,256]{2,1,0:T(8,128)(2,1)S(1)}, bf16[4,64,256]{2,1,0:T(8,128)(2,1)S(1)}, u32[]{:S(2)}, u32[]{:S(2)}) collective-permute-start(bf16[4,64,256]{2,1,0:T(8,128)(2,1)S(1)} %pad_maximum_fusion.7), channel_id=1, source_target_pairs={{0,4},{1,5},{2,6},{3,7},{4,0},{5,1},{6,2},{7,3},{8,12},{9,13},{10,... | collective-permute-start | bytes 393224 | tf_op jit(solution)/shard_map/ppermute | solution.py:1099
  21.1 7.2 %collective-permute-start.5 = (bf16[4,64,256]{2,1,0:T(8,128)(2,1)S(1)}, bf16[4,64,256]{2,1,0:T(8,128)(2,1)S(1)}, u32[]{:S(2)}, u32[]{:S(2)}) collective-permute-start(bf16[4,64,256]{2,1,0:T(8,128)(2,1)S(1)} %pad_maximum_fusion.7), channel_id=1, source_target_pairs={{0,2},{1,3},{2,0},{3,1},{4,6},{5,7},{6,4},{7,5},{8,10},{9,11},{10,... | collective-permute-start | bytes 393224 | tf_op jit(solution)/shard_map/ppermute | solution.py:1099
  21.6 10.9 %collective-permute-start.10 = (bf16[4,64,384]{2,1,0:T(8,128)(2,1)S(1)}, bf16[4,64,384]{2,1,0:T(8,128)(2,1)S(1)}, u32[]{:S(2)}, u32[]{:S(2)}) collective-permute-start(bf16[4,64,384]{2,1,0:T(8,128)(2,1)S(1)} %pad_maximum_fusion.5), channel_id=1, source_target_pairs={{0,4},{1,5},{2,6},{3,7},{4,0},{5,1},{6,2},{7,3},{8,12},{9,13},{10,... | collective-permute-start | bytes 589832 | tf_op jit(solution)/shard_map/ppermute | solution.py:1099
  23.2 11.5 %collective-permute-start.11 = (bf16[4,64,384]{2,1,0:T(8,128)(2,1)S(1)}, bf16[4,64,384]{2,1,0:T(8,128)(2,1)S(1)}, u32[]{:S(2)}, u32[]{:S(2)}) collective-permute-start(bf16[4,64,384]{2,1,0:T(8,128)(2,1)S(1)} %pad_maximum_fusion.5), channel_id=1, source_target_pairs={{0,2},{1,3},{2,0},{3,1},{4,6},{5,7},{6,4},{7,5},{8,10},{9,11},{10,... | collective-permute-start | bytes 589832 | tf_op jit(solution)/shard_map/ppermute | solution.py:1099
  25.4 9.3 %collective-permute-start.9 = (bf16[4,64,384]{2,1,0:T(8,128)(2,1)S(1)}, bf16[4,64,384]{2,1,0:T(8,128)(2,1)S(1)}, u32[]{:S(2)}, u32[]{:S(2)}) collective-permute-start(bf16[4,64,384]{2,1,0:T(8,128)(2,1)S(1)} %pad_maximum_fusion.5), channel_id=1, source_target_pairs={{0,6},{1,7},{2,4},{3,5},{4,2},{5,3},{6,0},{7,1},{8,14},{9,15},{10,... | collective-permute-start | bytes 589832 | tf_op jit(solution)/shard_map/ppermute | solution.py:1099
  28.4 6.6 %collective-permute-start.6 = (bf16[16,64,256]{2,1,0:T(8,128)(2,1)S(1)}, bf16[16,64,256]{2,1,0:T(8,128)(2,1)S(1)}, u32[]{:S(2)}, u32[]{:S(2)}) collective-permute-start(bf16[16,64,256]{2,1,0:T(8,128)(2,1)S(1)} %pad_maximum_fusion.2.own_ref), channel_id=1, source_target_pairs={{0,1},{1,0},{2,3},{3,2},{4,5},{5,4},{6,7},{7,6},{8,9},{9,8},{10,11... | collective-permute-start | bytes 1572872 | tf_op jit(solution)/shard_map/ppermute | solution.py:1099
  28.5 7.3 %collective-permute-start.13 = (bf16[2,64,768]{2,1,0:T(8,128)(2,1)S(1)}, bf16[2,64,768]{2,1,0:T(8,128)(2,1)S(1)}, u32[]{:S(2)}, u32[]{:S(2)}) collective-permute-start(bf16[2,64,768]{2,1,0:T(8,128)(2,1)S(1)} %pad_maximum_fusion.4), channel_id=1, source_target_pairs={{0,8},{1,9},{2,10},{3,11},{4,12},{5,13},{6,14},{7,15},{8,0},{9,1},... | collective-permute-start | bytes 589832 | tf_op jit(solution)/shard_map/ppermute | solution.py:1099
  34.9 4.6 %copy-start = (f32[7,256]{1,0:T(8,128)S(1)}, f32[7,256]{1,0:T(8,128)}, u32[]{:S(2)}) copy-start(f32[7,256]{1,0:T(8,128)} %refs_21_.1) | copy-start | bytes 21508
  35.1 15.3 %collective-permute-start.12 = (bf16[16,64,384]{2,1,0:T(8,128)(2,1)S(1)}, bf16[16,64,384]{2,1,0:T(8,128)(2,1)S(1)}, u32[]{:S(2)}, u32[]{:S(2)}) collective-permute-start(bf16[16,64,384]{2,1,0:T(8,128)(2,1)S(1)} %pad_maximum_fusion.1.own_ref), channel_id=1, source_target_pairs={{0,1},{1,0},{2,3},{3,2},{4,5},{5,4},{6,7},{7,6},{8,9},{9,8},{10,11... | collective-permute-start | bytes 2359304 | tf_op jit(solution)/shard_map/ppermute | solution.py:1099
  35.9 28.8 %collective-permute-start.14 = (bf16[4,64,768]{2,1,0:T(8,128)(2,1)S(1)}, bf16[4,64,768]{2,1,0:T(8,128)(2,1)S(1)}, u32[]{:S(2)}, u32[]{:S(2)}) collective-permute-start(bf16[4,64,768]{2,1,0:T(8,128)(2,1)S(1)} %pad_maximum_fusion.3), channel_id=1, source_target_pairs={{0,2},{1,3},{2,0},{3,1},{4,6},{5,7},{6,4},{7,5},{8,10},{9,11},{10,... | collective-permute-start | bytes 1179656 | tf_op jit(solution)/shard_map/ppermute | solution.py:1099
  36.7 28.0 %collective-permute-start.15 = (bf16[4,64,768]{2,1,0:T(8,128)(2,1)S(1)}, bf16[4,64,768]{2,1,0:T(8,128)(2,1)S(1)}, u32[]{:S(2)}, u32[]{:S(2)}) collective-permute-start(bf16[4,64,768]{2,1,0:T(8,128)(2,1)S(1)} %pad_maximum_fusion.3), channel_id=1, source_target_pairs={{0,4},{1,5},{2,6},{3,7},{4,0},{5,1},{6,2},{7,3},{8,12},{9,13},{10,... | collective-permute-start | bytes 1179656 | tf_op jit(solution)/shard_map/ppermute | solution.py:1099
  38.2 26.5 %collective-permute-start.16 = (bf16[4,64,768]{2,1,0:T(8,128)(2,1)S(1)}, bf16[4,64,768]{2,1,0:T(8,128)(2,1)S(1)}, u32[]{:S(2)}, u32[]{:S(2)}) collective-permute-start(bf16[4,64,768]{2,1,0:T(8,128)(2,1)S(1)} %pad_maximum_fusion.3), channel_id=1, source_target_pairs={{0,6},{1,7},{2,4},{3,5},{4,2},{5,3},{6,0},{7,1},{8,14},{9,15},{10,... | collective-permute-start | bytes 1179656 | tf_op jit(solution)/shard_map/ppermute | solution.py:1099
  64.8 4.9 %copy-start.4 = (s32[16,48,32]{1,2,0:T(8,128)S(1)}, s32[16,48,32]{1,2,0:T(8,128)}, u32[]{:S(2)}) copy-start(s32[16,48,32]{1,2,0:T(8,128)} %param.25) | copy-start | bytes 294916
  64.9 4.9 %copy-start.7 = (s32[16]{0:T(128)S(1)}, s32[16]{0:T(128)}, u32[]{:S(2)}) copy-start(s32[16]{0:T(128)} %refs_6_.5) | copy-start | bytes 196
  64.9 4.8 %copy-start.8 = (f32[1536,256]{1,0:T(8,128)S(1)}, f32[1536,256]{1,0:T(8,128)}, u32[]{:S(2)}) copy-start(f32[1536,256]{1,0:T(8,128)} %get-tuple-element.142.refs_0_) | copy-start | bytes 4718596
  65.1 3.5 %collective-permute-start.17 = (bf16[16,64,768]{2,1,0:T(8,128)(2,1)S(1)}, bf16[16,64,768]{2,1,0:T(8,128)(2,1)S(1)}, u32[]{:S(2)}, u32[]{:S(2)}) collective-permute-start(bf16[16,64,768]{2,1,0:T(8,128)(2,1)S(1)} %pad_maximum_fusion.refs_1_), channel_id=1, source_target_pairs={{0,1},{1,0},{2,3},{3,2},{4,5},{5,4},{6,7},{7,6},{8,9},{9,8},{10,11... | collective-permute-start | bytes 4718600 | tf_op jit(solution)/shard_map/ppermute | solution.py:1099
  99.7 3.5 %collective-permute-start.18 = (bf16[16,64,768]{2,1,0:T(8,128)(2,1)S(1)}, bf16[16,64,768]{2,1,0:T(8,128)(2,1)}, u32[]{:S(2)}, u32[]{:S(2)}) collective-permute-start(bf16[16,64,768]{2,1,0:T(8,128)(2,1)S(1)} %get-tuple-element.147), channel_id=1, source_target_pairs={{0,1},{1,0},{2,3},{3,2},{4,5},{5,4},{6,7},{7,6},{8,9},{9,8},{10,11... | collective-permute-start | bytes 4718600 | tf_op jit(solution)/shard_map/ppermute | solution.py:1099
  103.2 6.3 %copy-start.10 = (f32[1536,256]{1,0:T(8,128)S(1)}, f32[1536,256]{1,0:T(8,128)}, u32[]{:S(2)}) copy-start(f32[1536,256]{1,0:T(8,128)} %copy-done.9) | copy-start | bytes 4718596
  106.0 19.7 %collective-permute-start.19 = (bf16[4,64,768]{2,1,0:T(8,128)(2,1)S(1)}, bf16[4,64,768]{2,1,0:T(8,128)(2,1)}, u32[]{:S(2)}, u32[]{:S(2)}) collective-permute-start(bf16[4,64,768]{2,1,0:T(8,128)(2,1)S(1)} %get-tuple-element.161), channel_id=1, source_target_pairs={{0,2},{1,3},{2,0},{3,1},{4,6},{5,7},{6,4},{7,5},{8,10},{9,11},{10,... | collective-permute-start | bytes 1179656 | tf_op jit(solution)/shard_map/ppermute | solution.py:1099
  106.8 18.9 %collective-permute-start.20 = (bf16[4,64,768]{2,1,0:T(8,128)(2,1)S(1)}, bf16[4,64,768]{2,1,0:T(8,128)(2,1)}, u32[]{:S(2)}, u32[]{:S(2)}) collective-permute-start(bf16[4,64,768]{2,1,0:T(8,128)(2,1)S(1)} %get-tuple-element.162), channel_id=1, source_target_pairs={{0,4},{1,5},{2,6},{3,7},{4,0},{5,1},{6,2},{7,3},{8,12},{9,13},{10,... | collective-permute-start | bytes 1179656 | tf_op jit(solution)/shard_map/ppermute | solution.py:1099
  108.3 18.6 %collective-permute-start.21 = (bf16[4,64,768]{2,1,0:T(8,128)(2,1)S(1)}, bf16[4,64,768]{2,1,0:T(8,128)(2,1)}, u32[]{:S(2)}, u32[]{:S(2)}) collective-permute-start(bf16[4,64,768]{2,1,0:T(8,128)(2,1)S(1)} %get-tuple-element.163), channel_id=1, source_target_pairs={{0,6},{1,7},{2,4},{3,5},{4,2},{5,3},{6,0},{7,1},{8,14},{9,15},{10,... | collective-permute-start | bytes 1179656 | tf_op jit(solution)/shard_map/ppermute | solution.py:1099
  126.9 2.4 %collective-permute-start.22 = (bf16[16,64,384]{2,1,0:T(8,128)(2,1)S(1)}, bf16[16,64,384]{2,1,0:T(8,128)(2,1)}, u32[]{:S(2)}, u32[]{:S(2)}) collective-permute-start(bf16[16,64,384]{2,1,0:T(8,128)(2,1)S(1)} %get-tuple-element.173), channel_id=1, source_target_pairs={{0,1},{1,0},{2,3},{3,2},{4,5},{5,4},{6,7},{7,6},{8,9},{9,8},{10,11... | collective-permute-start | bytes 2359304 | tf_op jit(solution)/shard_map/ppermute | solution.py:1099
  130.7 16.4 %collective-permute-start.23 = (bf16[2,64,768]{2,1,0:T(8,128)(2,1)S(1)}, bf16[2,64,768]{2,1,0:T(8,128)(2,1)S(1)}, u32[]{:S(2)}, u32[]{:S(2)}) collective-permute-start(bf16[2,64,768]{2,1,0:T(8,128)(2,1)S(1)} %get-tuple-element.178), channel_id=1, source_target_pairs={{0,8},{1,9},{2,10},{3,11},{4,12},{5,13},{6,14},{7,15},{8,0},{9,1},... | collective-permute-start | bytes 589832 | tf_op jit(solution)/shard_map/ppermute | solution.py:1099
  131.3 15.8 %collective-permute-start.24 = (bf16[4,64,384]{2,1,0:T(8,128)(2,1)S(1)}, bf16[4,64,384]{2,1,0:T(8,128)(2,1)S(1)}, u32[]{:S(2)}, u32[]{:S(2)}) collective-permute-start(bf16[4,64,384]{2,1,0:T(8,128)(2,1)S(1)} %get-tuple-element.179), channel_id=1, source_target_pairs={{0,2},{1,3},{2,0},{3,1},{4,6},{5,7},{6,4},{7,5},{8,10},{9,11},{10,... | collective-permute-start | bytes 589832 | tf_op jit(solution)/shard_map/ppermute | solution.py:1099
  132.5 14.7 %collective-permute-start.25 = (bf16[4,64,384]{2,1,0:T(8,128)(2,1)S(1)}, bf16[4,64,384]{2,1,0:T(8,128)(2,1)S(1)}, u32[]{:S(2)}, u32[]{:S(2)}) collective-permute-start(bf16[4,64,384]{2,1,0:T(8,128)(2,1)S(1)} %get-tuple-element.180), channel_id=1, source_target_pairs={{0,4},{1,5},{2,6},{3,7},{4,0},{5,1},{6,2},{7,3},{8,12},{9,13},{10,... | collective-permute-start | bytes 589832 | tf_op jit(solution)/shard_map/ppermute | solution.py:1099
  134.1 13.1 %collective-permute-start.26 = (bf16[4,64,384]{2,1,0:T(8,128)(2,1)S(1)}, bf16[4,64,384]{2,1,0:T(8,128)(2,1)S(1)}, u32[]{:S(2)}, u32[]{:S(2)}) collective-permute-start(bf16[4,64,384]{2,1,0:T(8,128)(2,1)S(1)} %get-tuple-element.181), channel_id=1, source_target_pairs={{0,6},{1,7},{2,4},{3,5},{4,2},{5,3},{6,0},{7,1},{8,14},{9,15},{10,... | collective-permute-start | bytes 589832 | tf_op jit(solution)/shard_map/ppermute | solution.py:1099
  148.0 2.9 %collective-permute-start.28 = (bf16[16,64,256]{2,1,0:T(8,128)(2,1)S(1)}, bf16[16,64,256]{2,1,0:T(8,128)(2,1)S(1)}, u32[]{:S(2)}, u32[]{:S(2)}) collective-permute-start(bf16[16,64,256]{2,1,0:T(8,128)(2,1)S(1)} %get-tuple-element.187), channel_id=1, source_target_pairs={{0,1},{1,0},{2,3},{3,2},{4,5},{5,4},{6,7},{7,6},{8,9},{9,8},{10,11... | collective-permute-start | bytes 1572872 | tf_op jit(solution)/shard_map/ppermute | solution.py:1099
  149.2 5.3 %collective-permute-start.27 = (bf16[2,64,384]{2,1,0:T(8,128)(2,1)S(1)}, bf16[2,64,384]{2,1,0:T(8,128)(2,1)S(1)}, u32[]{:S(2)}, u32[]{:S(2)}) collective-permute-start(bf16[2,64,384]{2,1,0:T(8,128)(2,1)S(1)} %get-tuple-element.246), channel_id=1, source_target_pairs={{0,8},{1,9},{2,10},{3,11},{4,12},{5,13},{6,14},{7,15},{8,0},{9,1},... | collective-permute-start | bytes 294920 | tf_op jit(solution)/shard_map/ppermute | solution.py:1099
  151.0 5.7 %collective-permute-start.30 = (bf16[4,64,256]{2,1,0:T(8,128)(2,1)S(1)}, bf16[4,64,256]{2,1,0:T(8,128)(2,1)S(1)}, u32[]{:S(2)}, u32[]{:S(2)}) collective-permute-start(bf16[4,64,256]{2,1,0:T(8,128)(2,1)S(1)} %get-tuple-element.245), channel_id=1, source_target_pairs={{0,2},{1,3},{2,0},{3,1},{4,6},{5,7},{6,4},{7,5},{8,10},{9,11},{10,... | collective-permute-start | bytes 393224 | tf_op jit(solution)/shard_map/ppermute | solution.py:1099
  151.8 6.2 %collective-permute-start.31 = (bf16[4,64,256]{2,1,0:T(8,128)(2,1)S(1)}, bf16[4,64,256]{2,1,0:T(8,128)(2,1)S(1)}, u32[]{:S(2)}, u32[]{:S(2)}) collective-permute-start(bf16[4,64,256]{2,1,0:T(8,128)(2,1)S(1)} %get-tuple-element.244), channel_id=1, source_target_pairs={{0,4},{1,5},{2,6},{3,7},{4,0},{5,1},{6,2},{7,3},{8,12},{9,13},{10,... | collective-permute-start | bytes 393224 | tf_op jit(solution)/shard_map/ppermute | solution.py:1099
  153.3 7.4 %collective-permute-start.32 = (bf16[4,64,256]{2,1,0:T(8,128)(2,1)S(1)}, bf16[4,64,256]{2,1,0:T(8,128)(2,1)S(1)}, u32[]{:S(2)}, u32[]{:S(2)}) collective-permute-start(bf16[4,64,256]{2,1,0:T(8,128)(2,1)S(1)} %get-tuple-element.243), channel_id=1, source_target_pairs={{0,6},{1,7},{2,4},{3,5},{4,2},{5,3},{6,0},{7,1},{8,14},{9,15},{10,... | collective-permute-start | bytes 393224 | tf_op jit(solution)/shard_map/ppermute | solution.py:1099
  160.8 4.6 %collective-permute-start.33 = (bf16[2,64,256]{2,1,0:T(8,128)(2,1)S(1)}, bf16[2,64,256]{2,1,0:T(8,128)(2,1)S(1)}, u32[]{:S(2)}, u32[]{:S(2)}) collective-permute-start(bf16[2,64,256]{2,1,0:T(8,128)(2,1)S(1)} %get-tuple-element.252), channel_id=1, source_target_pairs={{0,8},{1,9},{2,10},{3,11},{4,12},{5,13},{6,14},{7,15},{8,0},{9,1},... | collective-permute-start | bytes 196616 | tf_op jit(solution)/shard_map/ppermute | solution.py:1099
  161.4 9.8 %collective-permute-start.29 = (bf16[1,64,1152]{2,1,0:T(8,128)(2,1)S(1)}, bf16[1,64,1152]{2,1,0:T(8,128)(2,1)S(1)}, u32[]{:S(2)}, u32[]{:S(2)}) collective-permute-start(bf16[1,64,1152]{2,1,0:T(8,128)(2,1)S(1)} %pad_maximum_fusion.6), channel_id=1, source_target_pairs={{0,16},{1,17},{2,18},{3,19},{4,20},{5,21},{6,22},{7,23},{8,24},{9,... | collective-permute-start | bytes 442376 | tf_op jit(solution)/shard_map/ppermute | solution.py:1099
  165.4 9.7 %collective-permute-start.34 = (bf16[1,64,256]{2,1,0:T(8,128)(2,1)S(1)}, bf16[1,64,256]{2,1,0:T(8,128)(2,1)S(1)}, u32[]{:S(2)}, u32[]{:S(2)}) collective-permute-start(bf16[1,64,256]{2,1,0:T(8,128)(2,1)S(1)} %fusion.15), channel_id=1, source_target_pairs={{0,16},{1,17},{2,18},{3,19},{4,20},{5,21},{6,22},{7,23},{8,24},{9,... | collective-permute-start | bytes 98312 | tf_op jit(solution)/shard_map/ppermute | solution.py:1099
  177.4 1.4 collective-permute-start.35
  179.5 3.9 %collective-permute-start.36 = (f32[48,128]{1,0:T(8,128)S(1)}, f32[48,128]{1,0:T(8,128)S(1)}, u32[]{:S(2)}, u32[]{:S(2)}) collective-permute-start(f32[48,128]{1,0:T(8,128)S(1)} %pad_maximum_fusion.12), channel_id=1, source_target_pairs={{0,4},{1,5},{2,6},{3,7},{4,0},{5,1},{6,2},{7,3},{8,12},{9,13},{10,... | collective-permute-start | bytes 73736 | tf_op jit(solution)/shard_map/ppermute | solution.py:1099
  180.8 3.8 %collective-permute-start.37 = (f32[48,128]{1,0:T(8,128)S(1)}, f32[48,128]{1,0:T(8,128)S(1)}, u32[]{:S(2)}, u32[]{:S(2)}) collective-permute-start(f32[48,128]{1,0:T(8,128)S(1)} %pad_maximum_fusion.12), channel_id=1, source_target_pairs={{0,2},{1,3},{2,0},{3,1},{4,6},{5,7},{6,4},{7,5},{8,10},{9,11},{10,... | collective-permute-start | bytes 73736 | tf_op jit(solution)/shard_map/ppermute | solution.py:1099
  182.2 4.7 %collective-permute-start.38 = (f32[48,128]{1,0:T(8,128)S(1)}, f32[48,128]{1,0:T(8,128)S(1)}, u32[]{:S(2)}, u32[]{:S(2)}) collective-permute-start(f32[48,128]{1,0:T(8,128)S(1)} %pad_maximum_fusion.12), channel_id=1, source_target_pairs={{0,6},{1,7},{2,4},{3,5},{4,2},{5,3},{6,0},{7,1},{8,14},{9,15},{10,... | collective-permute-start | bytes 73736 | tf_op jit(solution)/shard_map/ppermute | solution.py:1099
  187.7 4.4 %collective-permute-start.39 = (f32[48,128]{1,0:T(8,128)S(1)}, f32[48,128]{1,0:T(8,128)S(1)}, u32[]{:S(2)}, u32[]{:S(2)}) collective-permute-start(f32[48,128]{1,0:T(8,128)S(1)} %pad_maximum_fusion.11), channel_id=1, source_target_pairs={{0,8},{1,9},{2,10},{3,11},{4,12},{5,13},{6,14},{7,15},{8,0},{9,1},... | collective-permute-start | bytes 73736 | tf_op jit(solution)/shard_map/ppermute | solution.py:1099
  187.7 4.8 %collective-permute-start.40 = (f32[48,128]{1,0:T(8,128)S(1)}, f32[48,128]{1,0:T(8,128)S(1)}, u32[]{:S(2)}, u32[]{:S(2)}) collective-permute-start(f32[48,128]{1,0:T(8,128)S(1)} %pad_maximum_fusion.11), channel_id=1, source_target_pairs={{0,16},{1,17},{2,18},{3,19},{4,20},{5,21},{6,22},{7,23},{8,24},{9,... | collective-permute-start | bytes 73736 | tf_op jit(solution)/shard_map/ppermute | solution.py:1099
  190.5 5.6 %collective-permute-start.41 = (f32[48,128]{1,0:T(8,128)S(1)}, f32[48,128]{1,0:T(8,128)S(1)}, u32[]{:S(2)}, u32[]{:S(2)}) collective-permute-start(f32[48,128]{1,0:T(8,128)S(1)} %pad_maximum_fusion.11), channel_id=1, source_target_pairs={{0,24},{1,25},{2,26},{3,27},{4,28},{5,29},{6,30},{7,31},{8,16},{9,... | collective-permute-start | bytes 73736 | tf_op jit(solution)/shard_map/ppermute | solution.py:1099
  (11 other events, 19.1 us)
